TPU v7x, 256 devices: a whole 4x4x8 slice. The times are simulated.
256 devices in a mesh: ctx: 8 (over x_hi, y), dp: 32 (over z, x_lo, core).
Axes of the slice: x: 4 (x_hi: 2, x_lo: 2; x = x_hi * 2 + x_lo), y: 4, z: 8, core: 2. Of those that a mesh axis runs over, the one named last changes fastest.
Arguments:
- query_gate: bfloat16 [32, 1024, 4096], P('dp', 'ctx'), may hold values from -0.3125 to 0.3125
- key_gate: bfloat16 [32, 1024, 4096], P('dp', 'ctx'), may hold values from -6 to 6
- value_in: bfloat16 [32, 1024, 4096], P('dp', 'ctx'), may hold values from -6 to 6
- conv_out: bfloat16 [32, 1024, 4096], P('dp', 'ctx'), may hold values from -6 to 6
- out_grad: bfloat16 [32, 1024, 4096], P('dp', 'ctx'), may hold values from -6 to 6
- filters: float32 [2048, 1024], P('dp', 'ctx'), may hold values from -8 to 8
Outputs:
- query_grad: bfloat16 [32, 1024, 4096], P('dp', 'ctx')
- key_grad: bfloat16 [32, 1024, 4096], P('dp', 'ctx')
- value_grad: bfloat16 [32, 1024, 4096], P('dp', 'ctx')
- filter_grad: float32 [2048, 1024], P('dp', 'ctx')
All inputs are finite; a program needn't handle non-finite values.
Results may differ from a plain program's by a relative error of at most 0.013.
Values may be sent and summed in bfloat16 or wider, within the bound.
No kernel may reach another device: no remote copies, remote signals or barrier semaphores. Data moves between devices by JAX's collectives and lax.ppermute only.
A program may use at most 320 MiB of HBM per device.

v0:
```python
import jax
import jax.numpy as jnp
from jax import lax
from jax.sharding import PartitionSpec as P

HIGHEST = lax.Precision.HIGHEST


def swapped(block, axis, bit):
    count = lax.axis_size(axis)
    route = []
    for low in range(count):
        high = low | 1 << bit
        if high != low and high < count:
            route += [(low, high), (high, low)]
    return lax.ppermute(block, axis, route)


def passed_along(block, axis, distance):
    devices = range(lax.axis_size(axis))
    route = [(i - distance, i) for i in devices if i - distance in devices]
    return lax.ppermute(block, axis, route)


def matmul_plain(left, right):
    return jnp.dot(left, right, preferred_element_type=jnp.float32)


def contract_first(left, right):
    return lax.dot_general(
        left, right, (((0,), (0,)), ((), ())), precision=HIGHEST, preferred_element_type=jnp.float32
    )


def tables(length):
    freq_bins = length + 1
    period = 2 * length
    freq_index = lax.broadcasted_iota(jnp.int32, (freq_bins, length), 0)
    place_index = lax.broadcasted_iota(jnp.int32, (freq_bins, length), 1)
    angles = 2.0 * jnp.pi / period * (freq_index * place_index % period).astype(jnp.float32)
    column = lax.broadcasted_iota(jnp.int32, (freq_bins, 1), 0)
    weights = (jnp.where((column == 0) | (column == length), 1.0, 2.0) / period).astype(jnp.float32)
    parity = jnp.where(column % 2 == 0, 1.0, -1.0).astype(jnp.float32)
    return (jnp.cos(angles), jnp.sin(angles), weights, parity)


def split_table(table):
    upper = table.astype(jnp.bfloat16)
    lower = (table - upper.astype(jnp.float32)).astype(jnp.bfloat16)
    return (upper, lower)


def strand_core(mixed_cols, grad_cols, lag_filter, move_piece):
    shape_four = mixed_cols.shape
    length = shape_four[0]
    freq_bins = length + 1
    flat_width = shape_four[1] * shape_four[2] * shape_four[3]
    channels = shape_four[3]
    blocks = lag_filter.shape[1] // length
    cosine, sine, weights, parity = tables(length)
    cos_upper, cos_lower = split_table(cosine)
    sin_upper, sin_lower = split_table(sine)
    analysis = jnp.concatenate(
        [
            jnp.concatenate([cos_upper, cos_lower], axis=1),
            jnp.concatenate([sin_upper, sin_lower], axis=1),
        ],
        axis=0,
    )
    cos_weighted = cosine * weights
    sin_weighted = sine * weights
    synthesis = jnp.concatenate([cos_weighted, sin_weighted], axis=0)
    filter_pieces = lag_filter.reshape(channels, blocks, length)
    base_re = jnp.einsum("fb,cnb->nfc", cosine, filter_pieces, precision=HIGHEST)
    base_im = -jnp.einsum("fb,cnb->nfc", sine, filter_pieces, precision=HIGHEST)
    spec_shape = (2, freq_bins) + tuple(shape_four[1:])

    def spectrum(values):
        flat = values.reshape(length, flat_width)
        doubled = jnp.concatenate([flat, flat], axis=0)
        return matmul_plain(analysis, doubled).reshape(spec_shape)

    mixed_spec = spectrum(mixed_cols)
    mixed_real = mixed_spec[0]
    mixed_negim = mixed_spec[1]
    total = None
    lag_terms = []
    current = grad_cols
    for block_index in range(blocks):
        if block_index > 0:
            current = move_piece(current)
        spec = spectrum(current)
        real_part = spec[0]
        neg_imag = spec[1]
        coef_re = base_re[block_index]
        coef_im = base_im[block_index]
        if block_index > 0:
            coef_re = coef_re + parity * base_re[block_index - 1]
            coef_im = coef_im + parity * base_im[block_index - 1]
        coef_re = coef_re[:, None, None, :]
        coef_im = coef_im[:, None, None, :]
        update = jnp.stack(
            [coef_re * real_part - coef_im * neg_imag, coef_re * neg_imag + coef_im * real_part],
            axis=0,
        )
        total = update if total is None else total + update
        lag_re = jnp.sum(real_part * mixed_real + neg_imag * mixed_negim, axis=(1, 2))
        lag_im = jnp.sum(real_part * mixed_negim - neg_imag * mixed_real, axis=(1, 2))
        lag_terms.append((lag_re, lag_im))
    conv_flat = contract_first(synthesis, total.reshape(2 * freq_bins, flat_width))
    conv_grad = conv_flat.reshape(shape_four).astype(jnp.bfloat16)
    lag_rows = []
    for block_index in range(blocks):
        edge_re = lag_terms[block_index][0]
        edge_im = lag_terms[block_index][1]
        if block_index + 1 < blocks:
            edge_re = edge_re + parity * lag_terms[block_index + 1][0]
            edge_im = edge_im + parity * lag_terms[block_index + 1][1]
        lag_rows.append(
            contract_first(edge_re, cos_weighted) - contract_first(edge_im, sin_weighted)
        )
    filter_grad = jnp.stack(lag_rows, axis=1).reshape(channels, blocks * length)
    return (conv_grad, filter_grad)


def mirror_forward(values):
    for bit_index in range(lax.axis_size("ctx").bit_length() - 1):
        values = swapped(values, "ctx", bit_index)
    return values


def mirror_back(values):
    for bit_index in range(lax.axis_size("ctx").bit_length() - 1):
        values = swapped(values, "ctx", bit_index)
    return values


def move_whole(piece):
    return passed_along(piece, "ctx", -1)


def local(query_gate, key_gate, value_in, conv_out, out_grad, filters):
    length = query_gate.shape[1]
    half_width = query_gate.shape[2] // 2
    key_float = key_gate[0].astype(jnp.float32)
    value_float = value_in[0].astype(jnp.float32)
    mixed = (key_float * value_float).astype(jnp.bfloat16)
    grad_mix = (out_grad[0].astype(jnp.float32) * query_gate[0].astype(jnp.float32)).astype(
        jnp.bfloat16
    )
    mixed, grad_mix = lax.optimization_barrier((mixed, grad_mix))
    query_grad = (out_grad.astype(jnp.float32) * conv_out.astype(jnp.float32)).astype(jnp.bfloat16)
    ahead_mixed = mixed[:, :half_width]
    ahead_grad = grad_mix[:, :half_width]
    behind_mixed = mixed[::-1, half_width:][:, ::-1]
    behind_grad = grad_mix[::-1, half_width:][:, ::-1]
    behind_pair = mirror_forward(jnp.stack([behind_mixed, behind_grad], axis=0))
    behind_mixed = behind_pair[0]
    behind_grad = behind_pair[1]
    lag_filter = lax.all_gather(filters, "ctx", axis=1, tiled=True)
    groups = lax.axis_size("dp")
    block_width = half_width // groups
    mixed_cols = jnp.stack(
        [
            ahead_mixed.reshape(length, groups, block_width),
            behind_mixed.reshape(length, groups, block_width),
        ],
        axis=2,
    )
    grad_cols = jnp.stack(
        [
            ahead_grad.reshape(length, groups, block_width),
            behind_grad.reshape(length, groups, block_width),
        ],
        axis=2,
    )
    mixed_cols, grad_cols = (
        lax.all_to_all(mixed_cols, "dp", split_axis=1, concat_axis=1, tiled=True),
        lax.all_to_all(grad_cols, "dp", split_axis=1, concat_axis=1, tiled=True),
    )
    conv_grad, lag_grad = strand_core(mixed_cols, grad_cols, lag_filter, move_whole)
    conv_grad = lax.all_to_all(conv_grad, "dp", split_axis=1, concat_axis=1, tiled=True)
    ahead_conv = conv_grad[:, :, 0].reshape(length, half_width)
    behind_conv = conv_grad[:, :, 1].reshape(length, half_width)
    behind_conv = mirror_back(behind_conv)
    conv_whole = jnp.concatenate([ahead_conv, behind_conv[::-1, ::-1]], axis=1)
    conv_whole = lax.optimization_barrier(conv_whole)
    conv_float = conv_whole.astype(jnp.float32)
    key_grad = (conv_float * value_float).astype(jnp.bfloat16)[None]
    value_grad = (conv_float * key_float).astype(jnp.bfloat16)[None]
    filter_grad = lax.psum_scatter(lag_grad, "ctx", scatter_dimension=1, tiled=True)
    return (query_grad, key_grad, value_grad, filter_grad)


def solution(mesh):
    placed = (
        P("dp", "ctx", None),
        P("dp", "ctx", None),
        P("dp", "ctx", None),
        P("dp", "ctx", None),
        P("dp", "ctx", None),
        P("dp", "ctx"),
    )
    return jax.shard_map(
        local,
        mesh=mesh,
        in_specs=placed,
        out_specs=(
            P("dp", "ctx", None),
            P("dp", "ctx", None),
            P("dp", "ctx", None),
            P("dp", "ctx"),
        ),
        check_vma=False,
    )
```

profile of v0, /device:TPU:192, one launch (start us, length us, event | category | flops | bytes accessed | tf_op | source)
XLA Modules:
  0.0 907.3 jit_solution(14620971849233106879)
XLA Ops:
  25.9 23.3 %collective-permute-done = bf16[2,128,2048]{1,2,0:T(8,128)(2,1)S(1)} collective-permute-done((bf16[2,128,2048]{1,2,0:T(8,128)(2,1)S(1)}, bf16[2,128,2048]{1,2,0:T(8,128)(2,1)S(1)}, u32[]{:S(2)}, u32[]{:S(2)}) %collective-permute-start) | collective-permute-done | bytes 1048608 | tf_op jit(solution)/shard_map/ppermute | solution.py:16
  52.4 22.3 %collective-permute-done.1 = bf16[2,128,2048]{1,2,0:T(8,128)(2,1)S(1)} collective-permute-done((bf16[2,128,2048]{1,2,0:T(8,128)(2,1)S(1)}, bf16[2,128,2048]{1,2,0:T(8,128)(2,1)S(1)}, u32[]{:S(2)}, u32[]{:S(2)}) %collective-permute-start.1) | collective-permute-done | bytes 1048608 | tf_op jit(solution)/shard_map/ppermute | solution.py:16
  77.7 21.6 %collective-permute-done.2 = bf16[2,128,2048]{1,2,0:T(8,128)(2,1)S(1)} collective-permute-done((bf16[2,128,2048]{1,2,0:T(8,128)(2,1)S(1)}, bf16[2,128,2048]{1,2,0:T(8,128)(2,1)S(1)}, u32[]{:S(2)}, u32[]{:S(2)}) %collective-permute-start.2) | collective-permute-done | bytes 1048608 | tf_op jit(solution)/shard_map/ppermute | solution.py:16
  99.6 32.9 %all_to_all.15 = bf16[128,32,2,64]{0,3,2,1:T(8,128)(2,1)S(1)} all-to-all(bf16[128,32,2,64]{0,3,2,1:T(8,128)(2,1)S(1)} %copy.110), channel_id=1, replica_groups=mesh['ctx'=8,'dp'=32] {'dp'}, dimensions={1} | all-to-all | bytes 2097152 | tf_op jit(solution)/shard_map/all_to_all | solution.py:179
  133.8 25.6 %collective-permute-done.3 = bf16[128,32,2,64]{0,3,2,1:T(8,128)(2,1)} collective-permute-done((bf16[128,32,2,64]{0,3,2,1:T(8,128)(2,1)S(1)}, bf16[128,32,2,64]{0,3,2,1:T(8,128)(2,1)}, u32[]{:S(2)}, u32[]{:S(2)}) %collective-permute-start.3) | collective-permute-done | bytes 1048608 | tf_op jit(solution)/shard_map/ppermute | solution.py:22
  160.7 52.4 %all_gather.3 = f32[64,1024]{1,0:T(8,128)S(1)} all-gather(f32[64,128]{1,0:T(8,128)S(1)} %copy-done.33), channel_id=1, replica_groups=mesh['ctx'=8,'dp'=32] {'ctx'}, dimensions={1}, use_global_device_ids=true | all-gather | bytes 294912 | tf_op jit(solution)/shard_map/all_gather | solution.py:160
  215.1 7.5 all-to-all-start.2
  245.5 9.9 %collective-permute-done.5 = bf16[128,32,2,64]{0,3,2,1:T(8,128)(2,1)} collective-permute-done((bf16[128,32,2,64]{0,3,2,1:T(8,128)(2,1)}, bf16[128,32,2,64]{0,3,2,1:T(8,128)(2,1)}, u32[]{:S(2)}, u32[]{:S(2)}) %collective-permute-start.5) | collective-permute-done | bytes 1048608 | tf_op jit(solution)/shard_map/ppermute | solution.py:22
  299.6 7.2 multiply_subtract_fusion.11
  306.8 5.9 squeeze.125
  312.6 5.8 squeeze.127
  323.6 10.4 %multiply_subtract_fusion.3 = (f32[1,129,32,2,64]{4,3,2,1,0:T(2,128)}, f32[1,129,32,2,64]{4,3,2,1,0:T(2,128)}) fusion(f32[1,129,32,2,64]{4,3,2,1,0:T(2,128)} %squeeze.127, f32[1,129,32,2,64]{4,3,2,1,0:T(2,128)} %squeeze.125, f32[129,64]{1,0:T(8,128)S(1)} %copy-done.30, f32[129,64]{1,0:T(8,128)S(1)} %copy-done.29), kind=kLoop, calls=%fused_computation.14 | loop fusion | flops 3170304 | bytes 8520192 | tf_op jit(solution)/shard_map/sub | solution.py:103
  335.5 6.7 multiply_subtract_fusion.4
  342.1 19.4 %collective-permute-done.7 = bf16[128,32,2,64]{0,3,2,1:T(8,128)(2,1)S(1)} collective-permute-done((bf16[128,32,2,64]{0,3,2,1:T(8,128)(2,1)}, bf16[128,32,2,64]{0,3,2,1:T(8,128)(2,1)S(1)}, u32[]{:S(2)}, u32[]{:S(2)}) %collective-permute-start.7) | collective-permute-done | bytes 1048608 | tf_op jit(solution)/shard_map/ppermute | solution.py:22
  363.3 6.0 multiply_subtract_fusion.10
  369.3 5.8 squeeze.119
  375.2 5.8 squeeze.129
  386.1 10.4 %multiply_subtract_fusion.5 = (f32[1,129,32,2,64]{4,3,2,1,0:T(2,128)}, f32[1,129,32,2,64]{4,3,2,1,0:T(2,128)}) fusion(f32[1,129,32,2,64]{4,3,2,1,0:T(2,128)} %squeeze.119, f32[1,129,32,2,64]{4,3,2,1,0:T(2,128)} %squeeze.117, f32[129,64]{1,0:T(8,128)S(1)} %copy-done.26, f32[129,64]{1,0:T(8,128)S(1)} %copy-done.25), kind=kLoop, calls=%fused_computation.18 | loop fusion | flops 3170304 | bytes 8520192 | tf_op jit(solution)/shard_map/sub | solution.py:103
  398.2 6.5 multiply_subtract_fusion.2
  404.8 20.3 %collective-permute-done.8 = bf16[128,32,2,64]{0,3,2,1:T(8,128)(2,1)S(1)} collective-permute-done((bf16[128,32,2,64]{0,3,2,1:T(8,128)(2,1)}, bf16[128,32,2,64]{0,3,2,1:T(8,128)(2,1)S(1)}, u32[]{:S(2)}, u32[]{:S(2)}) %collective-permute-start.8) | collective-permute-done | bytes 1048608 | tf_op jit(solution)/shard_map/ppermute | solution.py:22
  426.8 6.0 multiply_subtract_fusion.9
  432.9 5.9 squeeze.115
  438.7 5.8 squeeze.133
  449.7 10.5 %multiply_subtract_fusion.6 = (f32[1,129,32,2,64]{4,3,2,1,0:T(2,128)}, f32[1,129,32,2,64]{4,3,2,1,0:T(2,128)}) fusion(f32[1,129,32,2,64]{4,3,2,1,0:T(2,128)} %squeeze.115, f32[1,129,32,2,64]{4,3,2,1,0:T(2,128)} %squeeze.113, f32[129,64]{1,0:T(8,128)S(1)} %copy-done.22, f32[129,64]{1,0:T(8,128)S(1)} %copy-done.21), kind=kLoop, calls=%fused_computation.20 | loop fusion | flops 3170304 | bytes 8520192 | tf_op jit(solution)/shard_map/sub | solution.py:103
  462.0 6.4 multiply_subtract_fusion.1
  468.5 26.8 %collective-permute-done.9 = bf16[128,32,2,64]{0,3,2,1:T(8,128)(2,1)S(1)} collective-permute-done((bf16[128,32,2,64]{0,3,2,1:T(8,128)(2,1)}, bf16[128,32,2,64]{0,3,2,1:T(8,128)(2,1)S(1)}, u32[]{:S(2)}, u32[]{:S(2)}) %collective-permute-start.9) | collective-permute-done | bytes 1048608 | tf_op jit(solution)/shard_map/ppermute | solution.py:22
  501.4 5.8 squeeze.111
  507.3 5.8 squeeze.137
  513.1 5.9 squeeze.139
  519.1 10.4 %multiply_subtract_fusion.7 = (f32[1,129,32,2,64]{4,3,2,1,0:T(2,128)}, f32[1,129,32,2,64]{4,3,2,1,0:T(2,128)}) fusion(f32[1,129,32,2,64]{4,3,2,1,0:T(2,128)} %squeeze.111, f32[1,129,32,2,64]{4,3,2,1,0:T(2,128)} %squeeze.110, f32[129,64]{1,0:T(8,128)S(1)} %copy-done.18, f32[129,64]{1,0:T(8,128)S(1)} %copy.106), kind=kLoop, calls=%fused_computation.22 | loop fusion | flops 3170304 | bytes 8520192 | tf_op jit(solution)/shard_map/sub | solution.py:103
  529.5 10.3 %multiply_subtract_fusion = (f32[1,129,32,2,64]{4,3,2,1,0:T(2,128)}, f32[1,129,32,2,64]{4,3,2,1,0:T(2,128)}) fusion(f32[1,129,32,2,64]{4,3,2,1,0:T(2,128)} %squeeze.139, f32[1,129,32,2,64]{4,3,2,1,0:T(2,128)} %squeeze.137, f32[129,64]{1,0:T(8,128)S(1)} %copy-done.17, f32[129,64]{1,0:T(8,128)S(1)} %copy-done.16), kind=kLoop, calls=%fused_computation.8 | loop fusion | flops 3170304 | bytes 8520192 | tf_op jit(solution)/shard_map/sub | solution.py:103
  539.9 33.2 %maximum_add_fusion.1 = f32[2,129,32,2,64]{4,3,2,1,0:T(2,128)} fusion(f32[1,129,32,2,64]{4,3,2,1,0:T(2,128)} %get-tuple-element.51, f32[1,129,32,2,64]{4,3,2,1,0:T(2,128)} %get-tuple-element.50, f32[1,129,32,2,64]{4,3,2,1,0:T(2,128)} %get-tuple-element.49, f32[1,129,32,2,64]{4,3,2,1,0:T(2,128)} %get-tuple-element.48, ...), kind=kLoop, calls=%fused_computation.6 | loop fusion | flops 15851520 | bytes 38043648 | tf_op jit(solution)/shard_map/add | solution.py:106
  573.1 10.7 %reshape.870 = f32[258,4096]{1,0:T(8,128)} reshape(f32[2,129,32,2,64]{4,3,2,1,0:T(2,128)} %maximum_add_fusion.1) | data formatting | bytes 8454144 | tf_op jit(solution)/shard_map/add | solution.py:106
  583.9 6.2 copy.127
  590.0 8.1 convolution_convert_fusion
  598.1 7.0 all-to-all-start.1
  607.6 5.8 add.464
  613.5 5.6 reduce_sum.150
  619.2 5.9 sub.177
  625.1 5.6 reduce_sum.151
  630.8 6.3 add.468
  642.8 5.9 sub.180
  654.9 6.0 add.460
  660.9 5.6 reduce_sum.148
  666.7 5.9 sub.174
  678.3 6.1 add.472
  690.1 6.2 sub.183
  696.3 5.6 reduce_sum.155
  703.6 5.9 add.456
  709.5 5.6 reduce_sum.145
  715.2 6.0 sub.171
  721.3 5.6 reduce_sum.147
  727.0 5.9 add.476
  738.6 6.1 sub.186
  752.0 6.2 add.454
  758.2 5.6 reduce_sum.144
  763.9 5.8 sub.169
  784.2 6.0 add.480
  790.2 5.6 reduce_sum.158
  797.7 10.7 %collective-permute-start.11 = (bf16[128,2048]{0,1:T(8,128)(2,1)}, bf16[128,2048]{0,1:T(8,128)(2,1)}, u32[]{:S(2)}, u32[]{:S(2)}) collective-permute-start(bf16[128,2048]{0,1:T(8,128)(2,1)} %collective-permute-done.10), channel_id=1, source_target_pairs={{0,64},{64,0},{32,96},{96,32},{128,192},{192,128},{160,224},{224,1... | collective-permute-start | bytes 1572872 | tf_op jit(solution)/shard_map/ppermute | solution.py:16
  814.6 5.8 reduce_sum.159
  823.4 13.4 %collective-permute-done.12 = bf16[128,2048]{0,1:T(8,128)(2,1)} collective-permute-done((bf16[128,2048]{0,1:T(8,128)(2,1)}, bf16[128,2048]{0,1:T(8,128)(2,1)}, u32[]{:S(2)}, u32[]{:S(2)}) %collective-permute-start.12) | collective-permute-done | bytes 524320 | tf_op jit(solution)/shard_map/ppermute | solution.py:16
  836.9 7.0 rev.13
  849.0 51.3 %reduce-scatter.2.cloned.1.call-done = f32[64,128]{1,0:T(8,128)} async-done(((f32[64,1024]{1,0:T(8,128)}), f32[64,128]{1,0:T(8,128)}) %reduce-scatter.2.cloned.1.call-update) | async-done | bytes 32784 | tf_op jit(solution)/shard_map/reduce_scatter | solution.py:191
  (281 shorter events, 197.7 us)
Async XLA Ops:
  24.2 136.6 %copy-start.33 = (f32[64,128]{1,0:T(8,128)S(1)}, f32[64,128]{1,0:T(8,128)}, u32[]{:S(2)}) copy-start(f32[64,128]{1,0:T(8,128)} %param.11) | copy-start | bytes 98308
  24.2 25.0 %collective-permute-start = (bf16[2,128,2048]{1,2,0:T(8,128)(2,1)S(1)}, bf16[2,128,2048]{1,2,0:T(8,128)(2,1)S(1)}, u32[]{:S(2)}, u32[]{:S(2)}) collective-permute-start(bf16[2,128,2048]{1,2,0:T(8,128)(2,1)S(1)} %pad_maximum_fusion), channel_id=1, source_target_pairs={{0,32},{32,0},{64,96},{96,64},{128,160},{160,128},{192,224},{224,1... | collective-permute-start | bytes 3145736 | tf_op jit(solution)/shard_map/ppermute | solution.py:16
  49.2 25.5 %collective-permute-start.1 = (bf16[2,128,2048]{1,2,0:T(8,128)(2,1)S(1)}, bf16[2,128,2048]{1,2,0:T(8,128)(2,1)S(1)}, u32[]{:S(2)}, u32[]{:S(2)}) collective-permute-start(bf16[2,128,2048]{1,2,0:T(8,128)(2,1)S(1)} %collective-permute-done), channel_id=1, source_target_pairs={{0,64},{64,0},{32,96},{96,32},{128,192},{192,128},{160,224},{224,1... | collective-permute-start | bytes 3145736 | tf_op jit(solution)/shard_map/ppermute | solution.py:16
  74.7 24.6 %collective-permute-start.2 = (bf16[2,128,2048]{1,2,0:T(8,128)(2,1)S(1)}, bf16[2,128,2048]{1,2,0:T(8,128)(2,1)S(1)}, u32[]{:S(2)}, u32[]{:S(2)}) collective-permute-start(bf16[2,128,2048]{1,2,0:T(8,128)(2,1)S(1)} %collective-permute-done.1), channel_id=1, source_target_pairs={{0,128},{128,0},{32,160},{160,32},{64,192},{192,64},{96,224},{224,... | collective-permute-start | bytes 3145736 | tf_op jit(solution)/shard_map/ppermute | solution.py:16
  132.5 26.9 %collective-permute-start.3 = (bf16[128,32,2,64]{0,3,2,1:T(8,128)(2,1)S(1)}, bf16[128,32,2,64]{0,3,2,1:T(8,128)(2,1)}, u32[]{:S(2)}, u32[]{:S(2)}) collective-permute-start(bf16[128,32,2,64]{0,3,2,1:T(8,128)(2,1)S(1)} %all_to_all.15), channel_id=1, source_target_pairs={{32,0},{64,32},{96,64},{128,96},{160,128},{192,160},{224,192},{33,... | collective-permute-start | bytes 3145736 | tf_op jit(solution)/shard_map/ppermute | solution.py:22
  159.4 64.8 %collective-permute-start.4 = (bf16[128,32,2,64]{0,3,2,1:T(8,128)(2,1)}, bf16[128,32,2,64]{0,3,2,1:T(8,128)(2,1)}, u32[]{:S(2)}, u32[]{:S(2)}) collective-permute-start(bf16[128,32,2,64]{0,3,2,1:T(8,128)(2,1)} %collective-permute-done.3), channel_id=1, source_target_pairs={{32,0},{64,32},{96,64},{128,96},{160,128},{192,160},{224,192},{33,... | collective-permute-start | bytes 3145736 | tf_op jit(solution)/shard_map/ppermute | solution.py:22
  215.1 49.8 %all-to-all-start.2 = ((bf16[128,32,2,64]{0,3,2,1:T(8,128)(2,1)}), bf16[128,32,2,64]{0,3,2,1:T(8,128)(2,1)S(1)}, u32[]{:S(2)}, u32[]{:S(2)}) async-start(bf16[128,32,2,64]{0,3,2,1:T(8,128)(2,1)} %copy.128), calls=%async_computation.2 | async-start | bytes 2097152 | tf_op jit(solution)/shard_map/all_to_all | solution.py:178
  224.2 31.2 %collective-permute-start.5 = (bf16[128,32,2,64]{0,3,2,1:T(8,128)(2,1)}, bf16[128,32,2,64]{0,3,2,1:T(8,128)(2,1)}, u32[]{:S(2)}, u32[]{:S(2)}) collective-permute-start(bf16[128,32,2,64]{0,3,2,1:T(8,128)(2,1)} %collective-permute-done.4), channel_id=1, source_target_pairs={{32,0},{64,32},{96,64},{128,96},{160,128},{192,160},{224,192},{33,... | collective-permute-start | bytes 3145736 | tf_op jit(solution)/shard_map/ppermute | solution.py:22
  244.0 12.9 %copy-start.36 = (f32[129]{0:T(256)}, f32[129]{0:T(256)S(1)}, u32[]{:S(2)}) copy-start(f32[129]{0:T(256)S(1)} %fusion.138) | copy-start | bytes 1552
  255.4 41.3 %collective-permute-start.6 = (bf16[128,32,2,64]{0,3,2,1:T(8,128)(2,1)}, bf16[128,32,2,64]{0,3,2,1:T(8,128)(2,1)}, u32[]{:S(2)}, u32[]{:S(2)}) collective-permute-start(bf16[128,32,2,64]{0,3,2,1:T(8,128)(2,1)} %collective-permute-done.5), channel_id=1, source_target_pairs={{32,0},{64,32},{96,64},{128,96},{160,128},{192,160},{224,192},{33,... | collective-permute-start | bytes 3145736 | tf_op jit(solution)/shard_map/ppermute | solution.py:22
  318.5 16.9 %slice-start.22 = ((s8[4227072]{0:T(1024)(128)(4,1)}), s8[32768]{0:T(1024)(128)(4,1)S(1)}, s32[]{:S(2)}) async-start(s8[4227072]{0:T(1024)(128)(4,1)} %bitcast.212), calls=%async_computation.27 | async-start | bytes 65536
  323.5 11.9 %slice-start.23 = ((s8[4227072]{0:T(1024)(128)(4,1)}), s8[4194304]{0:T(1024)(128)(4,1)S(1)}, s32[]{:S(2)}) async-start(s8[4227072]{0:T(1024)(128)(4,1)} %bitcast.212), calls=%async_computation.28 | async-start | bytes 8388608
  323.5 11.9 %copy-start.5 = (f32[1,129,32,2,64]{4,3,2,1,0:T(2,128)S(1)}, f32[1,129,32,2,64]{4,3,2,1,0:T(2,128)}, u32[]{:S(2)}) copy-start(f32[1,129,32,2,64]{4,3,2,1,0:T(2,128)} %squeeze.123) | copy-start | bytes 6340612
  323.5 11.9 %copy-start.27 = (f32[129,64]{1,0:T(8,128)S(1)}, f32[129,64]{1,0:T(8,128)}, u32[]{:S(2)}) copy-start(f32[129,64]{1,0:T(8,128)} %copy.117) | copy-start | bytes 99076
  323.6 11.9 %copy-start.28 = (f32[129,64]{1,0:T(8,128)S(1)}, f32[129,64]{1,0:T(8,128)}, u32[]{:S(2)}) copy-start(f32[129,64]{1,0:T(8,128)} %copy.118) | copy-start | bytes 99076
  323.6 39.7 %slice-start = ((s8[4325376]{0:T(1024)(128)(4,1)}), s8[4194304]{0:T(1024)(128)(4,1)S(1)}, s32[]{:S(2)}) async-start(s8[4325376]{0:T(1024)(128)(4,1)} %bitcast.188), calls=%async_computation.5 | async-start | bytes 8388608
  323.6 39.7 %slice-start.10 = ((s8[4325376]{0:T(1024)(128)(4,1)}), s8[4194304]{0:T(1024)(128)(4,1)S(1)}, s32[]{:S(2)}) async-start(s8[4325376]{0:T(1024)(128)(4,1)} %bitcast.198), calls=%async_computation.15 | async-start | bytes 8388608
  334.0 29.3 %slice-start.1 = ((s8[4325376]{0:T(1024)(128)(4,1)}), s8[131072]{0:T(1024)(128)(4,1)S(1)}, s32[]{:S(2)}) async-start(s8[4325376]{0:T(1024)(128)(4,1)} %bitcast.188), calls=%async_computation.6 | async-start | bytes 262144
  334.0 29.3 %slice-start.11 = ((s8[4325376]{0:T(1024)(128)(4,1)}), s8[131072]{0:T(1024)(128)(4,1)S(1)}, s32[]{:S(2)}) async-start(s8[4325376]{0:T(1024)(128)(4,1)} %bitcast.198), calls=%async_computation.16 | async-start | bytes 262144
  334.0 27.6 %collective-permute-start.7 = (bf16[128,32,2,64]{0,3,2,1:T(8,128)(2,1)}, bf16[128,32,2,64]{0,3,2,1:T(8,128)(2,1)S(1)}, u32[]{:S(2)}, u32[]{:S(2)}) collective-permute-start(bf16[128,32,2,64]{0,3,2,1:T(8,128)(2,1)} %collective-permute-done.6), channel_id=1, source_target_pairs={{32,0},{64,32},{96,64},{128,96},{160,128},{192,160},{224,192},{33,... | collective-permute-start | bytes 3145736 | tf_op jit(solution)/shard_map/ppermute | solution.py:22
  381.0 17.2 %slice-start.24 = ((s8[4227072]{0:T(1024)(128)(4,1)}), s8[32768]{0:T(1024)(128)(4,1)S(1)}, s32[]{:S(2)}) async-start(s8[4227072]{0:T(1024)(128)(4,1)} %bitcast.214), calls=%async_computation.29 | async-start | bytes 65536
  386.0 12.1 %slice-start.25 = ((s8[4227072]{0:T(1024)(128)(4,1)}), s8[4194304]{0:T(1024)(128)(4,1)S(1)}, s32[]{:S(2)}) async-start(s8[4227072]{0:T(1024)(128)(4,1)} %bitcast.214), calls=%async_computation.30 | async-start | bytes 8388608
  386.0 12.2 %copy-start.6 = (f32[1,129,32,2,64]{4,3,2,1,0:T(2,128)S(1)}, f32[1,129,32,2,64]{4,3,2,1,0:T(2,128)}, u32[]{:S(2)}) copy-start(f32[1,129,32,2,64]{4,3,2,1,0:T(2,128)} %squeeze.131) | copy-start | bytes 6340612
  386.0 12.2 %copy-start.23 = (f32[129,64]{1,0:T(8,128)S(1)}, f32[129,64]{1,0:T(8,128)}, u32[]{:S(2)}) copy-start(f32[129,64]{1,0:T(8,128)} %copy.121) | copy-start | bytes 99076
  386.1 12.2 %copy-start.24 = (f32[129,64]{1,0:T(8,128)S(1)}, f32[129,64]{1,0:T(8,128)}, u32[]{:S(2)}) copy-start(f32[129,64]{1,0:T(8,128)} %copy.122) | copy-start | bytes 99076
  386.1 40.7 %slice-start.2 = ((s8[4325376]{0:T(1024)(128)(4,1)}), s8[4194304]{0:T(1024)(128)(4,1)S(1)}, s32[]{:S(2)}) async-start(s8[4325376]{0:T(1024)(128)(4,1)} %bitcast.190), calls=%async_computation.7 | async-start | bytes 8388608
  386.1 40.7 %slice-start.8 = ((s8[4325376]{0:T(1024)(128)(4,1)}), s8[4194304]{0:T(1024)(128)(4,1)S(1)}, s32[]{:S(2)}) async-start(s8[4325376]{0:T(1024)(128)(4,1)} %bitcast.196), calls=%async_computation.13 | async-start | bytes 8388608
  396.5 30.3 %slice-start.3 = ((s8[4325376]{0:T(1024)(128)(4,1)}), s8[131072]{0:T(1024)(128)(4,1)S(1)}, s32[]{:S(2)}) async-start(s8[4325376]{0:T(1024)(128)(4,1)} %bitcast.190), calls=%async_computation.8 | async-start | bytes 262144
  396.5 30.3 %slice-start.9 = ((s8[4325376]{0:T(1024)(128)(4,1)}), s8[131072]{0:T(1024)(128)(4,1)S(1)}, s32[]{:S(2)}) async-start(s8[4325376]{0:T(1024)(128)(4,1)} %bitcast.196), calls=%async_computation.14 | async-start | bytes 262144
  396.5 28.5 %collective-permute-start.8 = (bf16[128,32,2,64]{0,3,2,1:T(8,128)(2,1)}, bf16[128,32,2,64]{0,3,2,1:T(8,128)(2,1)S(1)}, u32[]{:S(2)}, u32[]{:S(2)}) collective-permute-start(bf16[128,32,2,64]{0,3,2,1:T(8,128)(2,1)} %copy-done.12), channel_id=1, source_target_pairs={{32,0},{64,32},{96,64},{128,96},{160,128},{192,160},{224,192},{33,... | collective-permute-start | bytes 3145736 | tf_op jit(solution)/shard_map/ppermute | solution.py:22
  444.6 17.4 %slice-start.26 = ((s8[4227072]{0:T(1024)(128)(4,1)}), s8[32768]{0:T(1024)(128)(4,1)S(1)}, s32[]{:S(2)}) async-start(s8[4227072]{0:T(1024)(128)(4,1)} %bitcast.216), calls=%async_computation.31 | async-start | bytes 65536
  449.6 12.4 %slice-start.27 = ((s8[4227072]{0:T(1024)(128)(4,1)}), s8[4194304]{0:T(1024)(128)(4,1)S(1)}, s32[]{:S(2)}) async-start(s8[4227072]{0:T(1024)(128)(4,1)} %bitcast.216), calls=%async_computation.32 | async-start | bytes 8388608
  449.6 12.4 %copy-start.7 = (f32[1,129,32,2,64]{4,3,2,1,0:T(2,128)S(1)}, f32[1,129,32,2,64]{4,3,2,1,0:T(2,128)}, u32[]{:S(2)}) copy-start(f32[1,129,32,2,64]{4,3,2,1,0:T(2,128)} %squeeze.135) | copy-start | bytes 6340612
  449.6 12.4 %copy-start.19 = (f32[129,64]{1,0:T(8,128)S(1)}, f32[129,64]{1,0:T(8,128)}, u32[]{:S(2)}) copy-start(f32[129,64]{1,0:T(8,128)} %copy.123) | copy-start | bytes 99076
  449.6 12.4 %copy-start.20 = (f32[129,64]{1,0:T(8,128)S(1)}, f32[129,64]{1,0:T(8,128)}, u32[]{:S(2)}) copy-start(f32[129,64]{1,0:T(8,128)} %copy.124) | copy-start | bytes 99076
  449.6 46.4 %slice-start.4 = ((s8[4325376]{0:T(1024)(128)(4,1)}), s8[4194304]{0:T(1024)(128)(4,1)S(1)}, s32[]{:S(2)}) async-start(s8[4325376]{0:T(1024)(128)(4,1)} %bitcast.192), calls=%async_computation.9 | async-start | bytes 8388608
  449.6 46.4 %slice-start.6 = ((s8[4325376]{0:T(1024)(128)(4,1)}), s8[4194304]{0:T(1024)(128)(4,1)S(1)}, s32[]{:S(2)}) async-start(s8[4325376]{0:T(1024)(128)(4,1)} %bitcast.194), calls=%async_computation.11 | async-start | bytes 8388608
  460.1 35.9 %slice-start.5 = ((s8[4325376]{0:T(1024)(128)(4,1)}), s8[131072]{0:T(1024)(128)(4,1)S(1)}, s32[]{:S(2)}) async-start(s8[4325376]{0:T(1024)(128)(4,1)} %bitcast.192), calls=%async_computation.10 | async-start | bytes 262144
  460.1 35.9 %slice-start.7 = ((s8[4325376]{0:T(1024)(128)(4,1)}), s8[131072]{0:T(1024)(128)(4,1)S(1)}, s32[]{:S(2)}) async-start(s8[4325376]{0:T(1024)(128)(4,1)} %bitcast.194), calls=%async_computation.12 | async-start | bytes 262144
  460.1 35.1 %collective-permute-start.9 = (bf16[128,32,2,64]{0,3,2,1:T(8,128)(2,1)}, bf16[128,32,2,64]{0,3,2,1:T(8,128)(2,1)S(1)}, u32[]{:S(2)}, u32[]{:S(2)}) collective-permute-start(bf16[128,32,2,64]{0,3,2,1:T(8,128)(2,1)} %copy-done.13), channel_id=1, source_target_pairs={{32,0},{64,32},{96,64},{128,96},{160,128},{192,160},{224,192},{33,... | collective-permute-start | bytes 3145736 | tf_op jit(solution)/shard_map/ppermute | solution.py:22
  513.1 16.4 %copy-start.16 = (f32[129,64]{1,0:T(8,128)S(1)}, f32[129,64]{1,0:T(8,128)}, u32[]{:S(2)}) copy-start(f32[129,64]{1,0:T(8,128)} %copy.125) | copy-start | bytes 99076
  513.1 16.4 %copy-start.17 = (f32[129,64]{1,0:T(8,128)S(1)}, f32[129,64]{1,0:T(8,128)}, u32[]{:S(2)}) copy-start(f32[129,64]{1,0:T(8,128)} %copy.126) | copy-start | bytes 99076
  519.0 20.8 %slice-start.12 = ((s8[4227072]{0:T(1024)(128)(4,1)}), s8[4194304]{0:T(1024)(128)(4,1)S(1)}, s32[]{:S(2)}) async-start(s8[4227072]{0:T(1024)(128)(4,1)} %bitcast.202), calls=%async_computation.17 | async-start | bytes 8388608
  519.0 20.8 %slice-start.14 = ((s8[4227072]{0:T(1024)(128)(4,1)}), s8[4194304]{0:T(1024)(128)(4,1)S(1)}, s32[]{:S(2)}) async-start(s8[4227072]{0:T(1024)(128)(4,1)} %bitcast.204), calls=%async_computation.19 | async-start | bytes 8388608
  519.0 20.8 %slice-start.16 = ((s8[4227072]{0:T(1024)(128)(4,1)}), s8[4194304]{0:T(1024)(128)(4,1)S(1)}, s32[]{:S(2)}) async-start(s8[4227072]{0:T(1024)(128)(4,1)} %bitcast.206), calls=%async_computation.21 | async-start | bytes 8388608
  519.1 20.8 %slice-start.18 = ((s8[4227072]{0:T(1024)(128)(4,1)}), s8[4194304]{0:T(1024)(128)(4,1)S(1)}, s32[]{:S(2)}) async-start(s8[4227072]{0:T(1024)(128)(4,1)} %bitcast.208), calls=%async_computation.23 | async-start | bytes 8388608
  519.1 20.8 %slice-start.20 = ((s8[4227072]{0:T(1024)(128)(4,1)}), s8[4194304]{0:T(1024)(128)(4,1)S(1)}, s32[]{:S(2)}) async-start(s8[4227072]{0:T(1024)(128)(4,1)} %bitcast.210), calls=%async_computation.25 | async-start | bytes 8388608
  529.5 10.4 %slice-start.13 = ((s8[4227072]{0:T(1024)(128)(4,1)}), s8[32768]{0:T(1024)(128)(4,1)S(1)}, s32[]{:S(2)}) async-start(s8[4227072]{0:T(1024)(128)(4,1)} %bitcast.202), calls=%async_computation.18 | async-start | bytes 65536
  529.5 10.4 %slice-start.15 = ((s8[4227072]{0:T(1024)(128)(4,1)}), s8[32768]{0:T(1024)(128)(4,1)S(1)}, s32[]{:S(2)}) async-start(s8[4227072]{0:T(1024)(128)(4,1)} %bitcast.204), calls=%async_computation.20 | async-start | bytes 65536
  529.5 10.4 %slice-start.17 = ((s8[4227072]{0:T(1024)(128)(4,1)}), s8[32768]{0:T(1024)(128)(4,1)S(1)}, s32[]{:S(2)}) async-start(s8[4227072]{0:T(1024)(128)(4,1)} %bitcast.206), calls=%async_computation.22 | async-start | bytes 65536
  529.5 10.4 %slice-start.19 = ((s8[4227072]{0:T(1024)(128)(4,1)}), s8[32768]{0:T(1024)(128)(4,1)S(1)}, s32[]{:S(2)}) async-start(s8[4227072]{0:T(1024)(128)(4,1)} %bitcast.208), calls=%async_computation.24 | async-start | bytes 65536
  529.5 10.4 %slice-start.21 = ((s8[4227072]{0:T(1024)(128)(4,1)}), s8[32768]{0:T(1024)(128)(4,1)S(1)}, s32[]{:S(2)}) async-start(s8[4227072]{0:T(1024)(128)(4,1)} %bitcast.210), calls=%async_computation.26 | async-start | bytes 65536
  598.1 178.8 %all-to-all-start.1 = ((bf16[128,32,2,64]{0,3,2,1:T(8,128)(2,1)}), bf16[128,32,2,64]{0,3,2,1:T(8,128)(2,1)}, u32[]{:S(2)}, u32[]{:S(2)}) async-start(bf16[128,32,2,64]{0,3,2,1:T(8,128)(2,1)} %convolution_convert_fusion), calls=%async_computation.1 | async-start | bytes 2097152 | tf_op jit(solution)/shard_map/all_to_all | solution.py:182
  605.1 295.2 %reduce-scatter.2.cloned.1.call-start = ((), (), s32[]{:S(2)}) async-start(), calls=%async_computation.4 | async-start | bytes 294912 | tf_op jit(solution)/shard_map/reduce_scatter | solution.py:191
  642.8 11.6 %copy-start.35 = (f32[129]{0:T(256)S(1)}, f32[129]{0:T(256)}, u32[]{:S(2)}) copy-start(f32[129]{0:T(256)} %copy-done.34) | copy-start | bytes 1552
  642.8 11.6 %copy-start.37 = (f32[129]{0:T(256)S(1)}, f32[129]{0:T(256)}, u32[]{:S(2)}) copy-start(f32[129]{0:T(256)} %copy-done.36) | copy-start | bytes 1552
  779.0 18.7 %collective-permute-start.10 = (bf16[128,2048]{0,1:T(8,128)(2,1)}, bf16[128,2048]{0,1:T(8,128)(2,1)}, u32[]{:S(2)}, u32[]{:S(2)}) collective-permute-start(bf16[128,2048]{0,1:T(8,128)(2,1)} %bitcast.40), channel_id=1, source_target_pairs={{0,32},{32,0},{64,96},{96,64},{128,160},{160,128},{192,224},{224,1... | collective-permute-start | bytes 1572872 | tf_op jit(solution)/shard_map/ppermute | solution.py:16
  797.7 11.9 %copy-start.31 = (f32[64,8,128]{2,0,1:T(8,128)}, f32[64,8,128]{2,0,1:T(8,128)S(1)}, u32[]{:S(2)}) copy-start(f32[64,8,128]{2,0,1:T(8,128)S(1)} %fusion.54) | copy-start | bytes 786436
  797.7 23.9 %collective-permute-start.11 = (bf16[128,2048]{0,1:T(8,128)(2,1)}, bf16[128,2048]{0,1:T(8,128)(2,1)}, u32[]{:S(2)}, u32[]{:S(2)}) collective-permute-start(bf16[128,2048]{0,1:T(8,128)(2,1)} %collective-permute-done.10), channel_id=1, source_target_pairs={{0,64},{64,0},{32,96},{96,32},{128,192},{192,128},{160,224},{224,1... | collective-permute-start | bytes 1572872 | tf_op jit(solution)/shard_map/ppermute | solution.py:16
  809.5 11.0 %copy-start.38 = (f32[64,128]{1,0:T(8,128)S(1)}, f32[64,128]{1,0:T(8,128)}, u32[]{:S(2)}) copy-start(f32[64,128]{1,0:T(8,128)} %fusion.89) | copy-start | bytes 98308
  809.5 11.5 %copy-start.39 = (f32[64,128]{1,0:T(8,128)S(1)}, f32[64,128]{1,0:T(8,128)}, u32[]{:S(2)}) copy-start(f32[64,128]{1,0:T(8,128)} %fusion.84) | copy-start | bytes 98308
  814.6 29.3 %copy-start.9 = (bf16[1,128,4096]{1,2,0:T(8,128)(2,1)S(1)}, bf16[1,128,4096]{1,2,0:T(8,128)(2,1)}, u32[]{:S(2)}) copy-start(bf16[1,128,4096]{1,2,0:T(8,128)(2,1)} %copy-done.8) | copy-start | bytes 3145732
  814.6 29.3 %copy-start.11 = (bf16[1,128,4096]{1,2,0:T(8,128)(2,1)S(1)}, bf16[1,128,4096]{1,2,0:T(8,128)(2,1)}, u32[]{:S(2)}) copy-start(bf16[1,128,4096]{1,2,0:T(8,128)(2,1)} %copy-done.10) | copy-start | bytes 3145732
  821.5 15.3 %collective-permute-start.12 = (bf16[128,2048]{0,1:T(8,128)(2,1)}, bf16[128,2048]{0,1:T(8,128)(2,1)}, u32[]{:S(2)}, u32[]{:S(2)}) collective-permute-start(bf16[128,2048]{0,1:T(8,128)(2,1)} %collective-permute-done.11), channel_id=1, source_target_pairs={{0,128},{128,0},{32,160},{160,32},{64,192},{192,64},{96,224},{224,... | collective-permute-start | bytes 1572872 | tf_op jit(solution)/shard_map/ppermute | solution.py:16
  (20 other events, 85.9 us)
Sparse Core Ops, SparseCore 0:
  823.5 76.6 reduce-scatter.1
where the time goes:
time: 920 us; the launch traced here: 907 us
  local copies, waits for them, and re-layouts  261 us (28%)
  waiting for transfers between devices  234 us (25%)
  other arithmetic  228 us (25%)
  blocking collectives  85.3 us (9%)
  starting transfers between devices  48.1 us (5%)
  matrix products  35.3 us (4%)
  between operations  15.7 us (2%)
    ppermute x7, waiting for transfers between devices, passed_along(): return lax.ppermute(block, axis, route)  102 us
    ppermute x6, waiting for transfers between devices, swapped(): return lax.ppermute(block, axis, route)  80.7 us
    sub x8, other arithmetic, strand_core(): coef_re * real_part - coef_im * neg_imag  71.7 us
    all_gather x1, blocking collectives, local(): lag_filter = lax.all_gather(filters, 'ctx', axis=1, tiled=True)  52.4 us
    reduce_scatter x1, waiting for transfers between devices, local(): lax.psum_scatter(lag_grad, 'ctx', scatter_dimension=1, tiled=True)  51.3 us
    add x8, local copies, waits for them, and re-layouts, strand_core(): real_part * mixed_real + neg_imag * mixed_negim  48.1 us
    sub x8, local copies, waits for them, and re-layouts, strand_core(): real_part * mixed_negim - neg_imag * mixed_real  46.9 us
    reduce_sum x8, other arithmetic, strand_core(): jnp.sum(real_part * mixed_negim - neg_imag * mixed_real, axis=(1, 2))  45.3 us
  transfers between devices with their start and end apart: 16, of which 10 were waited for; matrix products, arithmetic and copies ran while one was open for 32% of the time, Pallas kernels for 0%

commit v1 on v0

v1 whole, which is shorter than its diff:
```python
import functools

import jax
import jax.numpy as jnp
import numpy as np
from jax import lax
from jax.experimental import pallas as pl
from jax.experimental.pallas import tpu as pltpu
from jax.sharding import Mesh
from jax.sharding import PartitionSpec as P

CTX = ("xh", "y")
PLANE = ("xh", "y", "xl", "core")
CTX_Z = ("xh", "y", "z")
SEQ = 1024
BLOCK = 128
LANES = 128
SPLIT = 4
FREQ = 128
MIB = 1024 * 1024
F32 = jnp.float32
BF16 = jnp.bfloat16


def half_tables():
    odd = 2 * np.arange(SEQ, dtype=np.int64) + 1
    phase = np.multiply.outer(odd, odd) % (8 * SEQ)
    angle = phase.astype(np.float64) * (np.pi / (4 * SEQ))
    return np.cos(angle), np.sin(angle)


def half_turn():
    angle = np.pi * (2 * np.arange(SEQ) + 1) / (4 * SEQ)
    return np.cos(angle), np.sin(angle)


def dot(a, b):
    return jnp.dot(a, b, preferred_element_type=F32)


def dot_nt(a, b):
    return lax.dot_general(a, b, (((1,), (1,)), ((), ())), preferred_element_type=F32)


def dot_tn(a, b):
    return lax.dot_general(a, b, (((0,), (0,)), ((), ())), preferred_element_type=F32)


def pack_kernel(*refs):
    out_ref = refs[8]
    tiles = refs[0].shape[1] // LANES
    low = lax.broadcasted_iota(jnp.int32, (BLOCK, LANES), 1) < LANES // 2
    for t in range(tiles):
        ahead = pl.ds(t * LANES, LANES)
        behind = pl.ds((tiles - 1 - t) * LANES, LANES)
        for kind in range(2):
            a, b = refs[2 * kind], refs[2 * kind + 1]
            c, d = refs[4 + 2 * kind], refs[5 + 2 * kind]
            f = a[:, ahead].astype(F32) * b[:, ahead].astype(F32)
            r = c[:, behind].astype(F32) * d[:, behind].astype(F32)
            out_ref[2 * t, kind] = jnp.where(low, f, r).astype(BF16)
            out_ref[2 * t + 1, kind] = jnp.where(low, r, f).astype(BF16)


def pack(q, g, k, v):
    steps = 4
    width = q.shape[1] // (2 * steps)
    ahead = pl.BlockSpec((BLOCK, width), lambda j: (0, j))
    behind = pl.BlockSpec((BLOCK, width), lambda j: (0, 2 * steps - 1 - j))
    return pl.pallas_call(
        pack_kernel,
        grid=(steps,),
        in_specs=[ahead] * 4 + [behind] * 4,
        out_specs=pl.BlockSpec((8, 2, BLOCK, LANES), lambda j: (j, 0, 0, 0)),
        out_shape=jax.ShapeDtypeStruct((32, 2, BLOCK, LANES), BF16),
        compiler_params=pltpu.CompilerParams(vmem_limit_bytes=16 * MIB),
        cost_estimate=pl.CostEstimate(flops=2 * MIB, bytes_accessed=6 * MIB, transcendentals=0),
        name="pack",
    )(q, g, k, v, q, g, k, v)


def filter_kernel(rows_ref, cos_ref, sin_ref, turn_cos_ref, turn_sin_ref, sign_ref, out_ref):
    rows = rows_ref[...]
    fc = dot_nt(cos_ref[...], rows)
    fs = dot_nt(sin_ref[...], rows)
    tc, ts = turn_cos_ref[...], turn_sin_ref[...]
    out_ref[0] = fc * tc + fs * ts
    out_ref[1] = (fc * ts - fs * tc) * sign_ref[...]


def filter_spectrum(rows, cos, sin, turn_cos, turn_sin, sign):
    return pl.pallas_call(
        filter_kernel,
        out_shape=jax.ShapeDtypeStruct((2, SEQ, LANES), F32),
        compiler_params=pltpu.CompilerParams(vmem_limit_bytes=24 * MIB),
        cost_estimate=pl.CostEstimate(flops=512 * MIB, bytes_accessed=5 * MIB, transcendentals=0),
        name="filter_spectrum",
    )(rows, cos, sin, turn_cos, turn_sin, sign)


def spectrum_kernel(x_ref, cos_ref, sin_ref, filt_ref, turn_cos_ref, turn_sin_ref, sign_ref, fold_ref,
                    uv_ref, fg_ref, cols, prod):
    width = SPLIT * LANES
    for i in range(SEQ // BLOCK):
        for q in range(SPLIT):
            for kind in range(2):
                cols[pl.ds(i * BLOCK, BLOCK), pl.ds(kind * width + q * LANES, LANES)] = x_ref[SPLIT * i + q, kind]
    sign = sign_ref[...]

    def step(n, _):
        at = pl.multiple_of(n * FREQ, FREQ)
        rows = pl.ds(at, FREQ)
        values = cols[...]
        c = dot(cos_ref[rows, :], values)
        s = dot(sin_ref[rows, :], values)
        re, im = filt_ref[0, rows, :], filt_ref[1, rows, :]
        sum_re = sum_im = None
        for q in range(SPLIT):
            lanes = slice(q * LANES, (q + 1) * LANES)
            other = slice(width + q * LANES, width + (q + 1) * LANES)
            cg, sg, cm, sm = c[:, lanes], s[:, lanes], c[:, other], s[:, other]
            uv_ref[rows, lanes] = (cg * re + sg * im).astype(BF16)
            uv_ref[pl.ds(pl.multiple_of(SEQ + at, FREQ), FREQ), lanes] = (sg * re - cg * im).astype(BF16)
            a, b = cg * cm + sg * sm, cg * sm - sg * cm
            sum_re = a if sum_re is None else sum_re + a
            sum_im = b if sum_im is None else sum_im + b
        sum_im = -sum_im * sign
        tc, ts = turn_cos_ref[rows, :], turn_sin_ref[rows, :]
        prod[rows, :] = (sum_re * tc + sum_im * ts).astype(BF16)
        prod[pl.ds(pl.multiple_of(SEQ + at, FREQ), FREQ), :] = (sum_re * ts - sum_im * tc).astype(BF16)
        return 0

    lax.fori_loop(0, SEQ // FREQ, step, 0)
    lags = dot_tn(prod[:SEQ, :], cos_ref[...]) + dot_tn(prod[SEQ:, :], sin_ref[...])
    fg_ref[...] = jnp.dot(fold_ref[...], lags * (1.0 / SEQ), precision=lax.Precision.HIGHEST,
                          preferred_element_type=F32)


def spectra(x, cos, sin, filt, turn_cos, turn_sin, sign, fold):
    return pl.pallas_call(
        spectrum_kernel,
        out_shape=(
            jax.ShapeDtypeStruct((2 * SEQ, SPLIT * LANES), BF16),
            jax.ShapeDtypeStruct((LANES // 2, SEQ), F32),
        ),
        scratch_shapes=[
            pltpu.VMEM((SEQ, 2 * SPLIT * LANES), BF16),
            pltpu.VMEM((2 * SEQ, LANES), BF16),
        ],
        compiler_params=pltpu.CompilerParams(vmem_limit_bytes=40 * MIB),
        cost_estimate=pl.CostEstimate(flops=4300 * MIB, bytes_accessed=9 * MIB, transcendentals=0),
        name="spectra",
    )(x, cos, sin, filt, turn_cos, turn_sin, sign, fold)


def back_kernel(uv_ref, cos_ref, sin_ref, out_ref):
    for i in range(SEQ // BLOCK):
        rows = pl.ds(i * BLOCK, BLOCK)
        conv = dot(cos_ref[rows, :], uv_ref[:SEQ, :]) + dot(sin_ref[rows, :], uv_ref[SEQ:, :])
        conv = (conv * (1.0 / SEQ)).astype(BF16)
        for q in range(SPLIT):
            out_ref[SPLIT * i + q] = conv[:, q * LANES:(q + 1) * LANES]


def back(uv, cos, sin):
    return pl.pallas_call(
        back_kernel,
        out_shape=jax.ShapeDtypeStruct((32, BLOCK, LANES), BF16),
        compiler_params=pltpu.CompilerParams(vmem_limit_bytes=32 * MIB),
        cost_estimate=pl.CostEstimate(flops=2100 * MIB, bytes_accessed=7 * MIB, transcendentals=0),
        name="back",
    )(uv, cos, sin)


def unpack_kernel(conv_ref, ka_ref, va_ref, kb_ref, vb_ref, key_ref, value_ref):
    tiles = ka_ref.shape[1] // LANES
    low = lax.broadcasted_iota(jnp.int32, (BLOCK, LANES), 1) < LANES // 2
    strand = pl.program_id(1)

    def run(k_ref, v_ref, ahead):
        for t in range(tiles):
            even, odd = conv_ref[2 * t].astype(F32), conv_ref[2 * t + 1].astype(F32)
            at = t if ahead else tiles - 1 - t
            lanes = pl.ds(at * LANES, LANES)
            conv = jnp.where(low, even, odd) if ahead else jnp.where(low, odd, even)
            key_ref[:, lanes] = (conv * v_ref[:, lanes].astype(F32)).astype(BF16)
            value_ref[:, lanes] = (conv * k_ref[:, lanes].astype(F32)).astype(BF16)

    @pl.when(strand == 0)
    def _():
        run(ka_ref, va_ref, True)

    @pl.when(strand == 1)
    def _():
        run(kb_ref, vb_ref, False)


def unpack(conv, k, v):
    steps = 4
    width = k.shape[1] // (2 * steps)
    ahead = pl.BlockSpec((BLOCK, width), lambda j, s: (0, j))
    behind = pl.BlockSpec((BLOCK, width), lambda j, s: (0, 2 * steps - 1 - j))
    either = pl.BlockSpec((BLOCK, width), lambda j, s: (0, jnp.where(s == 0, j, 2 * steps - 1 - j)))
    shape = jax.ShapeDtypeStruct(k.shape, BF16)
    return pl.pallas_call(
        unpack_kernel,
        grid=(steps, 2),
        in_specs=[pl.BlockSpec((8, BLOCK, LANES), lambda j, s: (j, 0, 0)), ahead, ahead, behind, behind],
        out_specs=(either, either),
        out_shape=(shape, shape),
        compiler_params=pltpu.CompilerParams(vmem_limit_bytes=16 * MIB),
        cost_estimate=pl.CostEstimate(flops=2 * MIB, bytes_accessed=5 * MIB, transcendentals=0),
        name="unpack",
    )(conv, k, v, k, v)


def swap_z(block, bit):
    return lax.ppermute(block, "z", [(i, i ^ (1 << bit)) for i in range(8)])


def turned(block, flip):
    route = [(8 * l + a, 8 * a + l) for l in range(8) for a in range(8)]
    if flip:
        route = [(8 * a + l, 8 * (l ^ 1) + a) for l in range(8) for a in range(8)]
    return lax.ppermute(block, CTX_Z, route)


def gathered_lags(filters):
    block = turned(filters.astype(BF16), False)
    z = lax.axis_index("z")
    for bit in range(3):
        other = swap_z(block, bit)
        first = (z >> bit) % 2 == 0
        block = jnp.concatenate([jnp.where(first, block, other), jnp.where(first, other, block)], axis=1)
    return block


def reduced_lags(partial):
    z = lax.axis_index("z")
    for bit in (2, 1):
        half = partial.shape[1] // 2
        low, high = partial[:, :half], partial[:, half:]
        first = (z >> bit) % 2 == 0
        kept, given = jnp.where(first, low, high), jnp.where(first, high, low)
        partial = kept + swap_z(given, bit)
    first = z % 2 == 0
    low, high = partial[:, :BLOCK], partial[:, BLOCK:]
    own, other = jnp.where(first, low, high), jnp.where(first, high, low)
    return turned(own, False) + turned(other, True)


def local(query_gate, key_gate, value_in, conv_out, out_grad, filters):
    cos64, sin64 = half_tables()
    cos, sin = jnp.asarray(cos64, BF16), jnp.asarray(sin64, BF16)
    turn_cos, turn_sin = (jnp.asarray(np.tile(t[:, None], (1, LANES)), F32) for t in half_turn())
    odd = lax.axis_index("core") == 1
    lane = np.arange(LANES)
    sign = np.where(lane < LANES // 2, -1.0, 1.0).astype(np.float32)[None]
    sign = jnp.where(odd, -sign, sign)
    row = np.arange(LANES // 2)[:, None]
    fold_even = ((lane == row) | (lane == LANES - 1 - row)).astype(np.float32)
    fold = jnp.where(odd, fold_even[::-1], fold_even)

    q, k, v, g = query_gate[0], key_gate[0], value_in[0], out_grad[0]
    x = pack(q, g, k, v)
    x = lax.all_to_all(x, PLANE, split_axis=0, concat_axis=0, tiled=True)

    query_grad = (out_grad.astype(F32) * conv_out.astype(F32)).astype(BF16)
    lags = gathered_lags(filters)
    mirrored = lags[::-1]
    rows = jnp.concatenate([jnp.where(odd, mirrored, lags), jnp.where(odd, lags, mirrored)], axis=0)
    filt = filter_spectrum(rows, cos, sin, turn_cos, turn_sin, sign)

    uv, partial = spectra(x, cos, sin, filt, turn_cos, turn_sin, sign, fold)
    conv = back(uv, cos, sin)
    conv = lax.all_to_all(conv, PLANE, split_axis=0, concat_axis=0, tiled=True)
    filter_grad = reduced_lags(partial)
    key_grad, value_grad = unpack(conv, k, v)
    return query_grad, key_grad[None], value_grad[None], filter_grad


def solution(mesh):
    fine = Mesh(mesh.devices.reshape(2, 4, 8, 2, 2), ("xh", "y", "z", "xl", "core"))
    wide = P(("z", "xl", "core"), CTX, None)
    narrow = P(("z", "xl", "core"), CTX)
    return jax.shard_map(
        local,
        mesh=fine,
        in_specs=(wide,) * 5 + (narrow,),
        out_specs=(wide, wide, wide, narrow),
        check_vma=False,
    )
```

time: 920 us -> 119 us (0.13); the launches traced: 907 us -> 118 us
  local copies, waits for them, and re-layouts: 261 us -> 18 us
  other arithmetic: 228 us -> 3.3 us
  waiting for transfers between devices: 234 us -> 43.8 us
  blocking collectives: 85.3 us -> 0 us
  matrix products: 35.3 us -> 0 us
  Pallas kernels: 0 us -> 20.9 us
  starting transfers between devices: 48.1 us -> 30.5 us
  between operations: 15.7 us -> 0.99 us
    ppermute x13 -> x8, waiting for transfers between devices: 183 us -> 42.2 us  [the longest x5 26.3 us: swap_z(): return lax.ppermute(block, 'z', [(i, i ^ 1 << bit) for i in range(8)])]
    sub x12 -> x0, other arithmetic: 96.3 us -> none  [the longest x8 71.7 us: strand_core(): coef_re * real_part - coef_im * neg_imag]
    reduce_sum x16 -> x0, other arithmetic: 90.4 us -> none  [the longest x8 45.3 us: strand_core(): jnp.sum(real_part * mixed_negim - neg_imag * mixed_real, axis=(1, 2))]
    squeeze x16 -> x0, local copies, waits for them, and re-layouts: 88.3 us -> none  [the longest x8 44.4 us: strand_core(): neg_imag = spec[1]]
    add x23 -> x0, local copies, waits for them, and re-layouts: 75.7 us -> none  [the longest x8 48.1 us: strand_core(): real_part * mixed_real + neg_imag * mixed_negim]
    all_gather x1 -> x0, blocking collectives: 52.4 us -> none  [local(): lag_filter = lax.all_gather(filters, 'ctx', axis=1, tiled=True)]
    reduce_scatter x1 -> x0, waiting for transfers between devices: 51.3 us -> none  [local(): lax.psum_scatter(lag_grad, 'ctx', scatter_dimension=1, tiled=True)]
    sub x8 -> x0, local copies, waits for them, and re-layouts: 46.9 us -> none  [strand_core(): real_part * mixed_negim - neg_imag * mixed_real]
  transfers between devices with their start and end apart: 16 -> 10, of which waited for: 10 -> 8; matrix products, arithmetic and copies ran while one was open for 32% -> 3% of each run, Pallas kernels for 0% -> 3%
where the time goes in v1:
time: 119 us; the launch traced here: 118 us
  waiting for transfers between devices  43.8 us (37%)
  starting transfers between devices  30.5 us (26%)
  Pallas kernels  20.9 us (18%)
  local copies, waits for them, and re-layouts  18 us (15%)
  other arithmetic  3.3 us (3%)
    ppermute x5, waiting for transfers between devices, swap_z(): return lax.ppermute(block, 'z', [(i, i ^ 1 << bit) for i in range(8)])  26.3 us
    unnamed x46, local copies, waits for them, and re-layouts  17.8 us
    ppermute x3, waiting for transfers between devices, turned(): return lax.ppermute(block, CTX_Z, route)  16 us
    ppermute x3, starting transfers between devices, turned(): return lax.ppermute(block, CTX_Z, route)  15.6 us
    pallas_call x1, Pallas kernels, spectra(): pl.pallas_call(spectrum_kernel, out_shape=(jax.ShapeDtypeStruct((2 * SEQ,...  9.63 us
    all_to_all x1, starting transfers between devices, local(): x = lax.all_to_all(x, PLANE, split_axis=0, concat_axis=0, tiled=True)  7.59 us
    pallas_call x1, Pallas kernels, unpack(): pl.pallas_call(unpack_kernel, grid=(steps, 2), in_specs=[pl.BlockSpec((8,...  5.36 us
    all_to_all x1, starting transfers between devices, local(): conv = lax.all_to_all(conv, PLANE, split_axis=0, concat_axis=0, tiled=True)  4.8 us
  transfers between devices with their start and end apart: 10, of which 8 were waited for; matrix products, arithmetic and copies ran while one was open for 3% of the time, Pallas kernels for 3%

profile of v1, /device:TPU:192, one launch (start us, length us, event | category | flops | bytes accessed | tf_op | source)
XLA Modules:
  0.0 117.5 jit_solution(11266185087428155891)
XLA Ops:
  0.6 0.0 copy-start
  0.6 1.2 %copy-done = bf16[1,128,4096]{2,1,0:T(8,128)(2,1)S(1)} copy-done((bf16[1,128,4096]{2,1,0:T(8,128)(2,1)S(1)}, bf16[1,128,4096]{2,1,0:T(8,128)(2,1)}, u32[]{:S(2)}) %copy-start) | copy-done | bytes 1048600
  1.9 0.0 copy-start.2
  1.9 1.2 %copy-done.2 = bf16[1,128,4096]{2,1,0:T(8,128)(2,1)S(1)} copy-done((bf16[1,128,4096]{2,1,0:T(8,128)(2,1)S(1)}, bf16[1,128,4096]{2,1,0:T(8,128)(2,1)}, u32[]{:S(2)}) %copy-start.2) | copy-done | bytes 1048600
  3.1 0.0 copy-start.4
  3.1 1.2 %copy-done.4 = bf16[1,128,4096]{2,1,0:T(8,128)(2,1)S(1)} copy-done((bf16[1,128,4096]{2,1,0:T(8,128)(2,1)S(1)}, bf16[1,128,4096]{2,1,0:T(8,128)(2,1)}, u32[]{:S(2)}) %copy-start.4) | copy-done | bytes 1048600
  4.3 0.0 copy-start.6
  4.3 1.2 %copy-done.6 = bf16[1,128,4096]{2,1,0:T(8,128)(2,1)S(1)} copy-done((bf16[1,128,4096]{2,1,0:T(8,128)(2,1)S(1)}, bf16[1,128,4096]{2,1,0:T(8,128)(2,1)}, u32[]{:S(2)}) %copy-start.6) | copy-done | bytes 1048600
  5.5 2.4 %pack.1 = bf16[32,2,128,128]{3,2,1,0:T(8,128)(2,1)} custom-call(bf16[128,4096]{1,0:T(8,128)(2,1)S(1)} %bitcast.16, bf16[128,4096]{1,0:T(8,128)(2,1)S(1)} %bitcast.14, bf16[128,4096]{1,0:T(8,128)(2,1)S(1)} %bitcast.6, bf16[128,4096]{1,0:T(8,128)(2,1)S(1)} %bitcast.10, bf16[128,4096]{1,0:T(8,128)(2,1)S(1)} %bitcast.17, bf16[128,4096]{1,0:T(8,128)(2,1)S(1)} %bitcast.15, ...), custom_call_target="tpu_custom_call" | custom-call | flops 2097152 | bytes 6291456 | tf_op jit(solution)/shard_map/pack/pallas_call | solution.py:70
  7.9 0.0 copy-start.20
  7.9 0.0 copy-start.22
  7.9 7.6 %all-to-all-start = ((bf16[32,2,128,128]{3,2,1,0:T(8,128)(2,1)}), bf16[32,2,128,128]{3,2,1,0:T(8,128)(2,1)}, u32[]{:S(2)}, u32[]{:S(2)}) async-start(bf16[32,2,128,128]{3,2,1,0:T(8,128)(2,1)} %pack.1), calls=%async_computation | async-start | bytes 4194304 | tf_op jit(solution)/shard_map/all_to_all | solution.py:266
  15.5 0.0 copy-done.20
  15.5 0.0 copy-start.7
  15.6 5.0 %collective-permute-start = (bf16[64,128]{1,0:T(8,128)(2,1)S(1)}, bf16[64,128]{1,0:T(8,128)(2,1)S(1)}, u32[]{:S(2)}, u32[]{:S(2)}) collective-permute-start(bf16[64,128]{1,0:T(8,128)(2,1)S(1)} %convert_element_type.15), channel_id=1, source_target_pairs={{0,0},{4,32},{8,64},{12,96},{16,128},{20,160},{24,192},{28,224},{3... | collective-permute-start | bytes 49160 | tf_op jit(solution)/shard_map/ppermute | solution.py:225
  20.6 9.3 %collective-permute-done = bf16[64,128]{1,0:T(8,128)(2,1)S(1)} collective-permute-done((bf16[64,128]{1,0:T(8,128)(2,1)S(1)}, bf16[64,128]{1,0:T(8,128)(2,1)S(1)}, u32[]{:S(2)}, u32[]{:S(2)}) %collective-permute-start) | collective-permute-done | bytes 16416 | tf_op jit(solution)/shard_map/ppermute | solution.py:225
  29.8 0.0 collective-permute-start.1
  29.8 3.9 %collective-permute-done.1 = bf16[64,128]{1,0:T(8,128)(2,1)S(1)} collective-permute-done((bf16[64,128]{1,0:T(8,128)(2,1)S(1)}, bf16[64,128]{1,0:T(8,128)(2,1)S(1)}, u32[]{:S(2)}, u32[]{:S(2)}) %collective-permute-start.1) | collective-permute-done | bytes 16416 | tf_op jit(solution)/shard_map/ppermute | solution.py:218
  33.8 0.1 collective-permute-start.2
  33.9 0.0 copy-done.18
  33.9 0.0 copy-done.19
  33.9 4.8 %collective-permute-done.2 = bf16[64,256]{1,0:T(8,128)(2,1)S(1)} collective-permute-done((bf16[64,256]{1,0:T(8,128)(2,1)S(1)}, bf16[64,256]{1,0:T(8,128)(2,1)S(1)}, u32[]{:S(2)}, u32[]{:S(2)}) %collective-permute-start.2) | collective-permute-done | bytes 32800 | tf_op jit(solution)/shard_map/ppermute | solution.py:218
  38.7 0.1 collective-permute-start.3
  38.8 0.0 copy-done.21
  38.8 0.0 copy-done.22
  38.9 8.1 %collective-permute-done.3 = bf16[64,512]{1,0:T(8,128)(2,1)S(1)} collective-permute-done((bf16[64,512]{1,0:T(8,128)(2,1)S(1)}, bf16[64,512]{1,0:T(8,128)(2,1)S(1)}, u32[]{:S(2)}, u32[]{:S(2)}) %collective-permute-start.3) | collective-permute-done | bytes 65568 | tf_op jit(solution)/shard_map/ppermute | solution.py:218
  47.0 0.3 rev.3
  47.4 0.0 copy-done.7
  47.4 0.0 copy-start.8
  47.4 1.6 %copy-done.8 = bf16[1024,1024]{1,0:T(8,128)(2,1)S(1)} copy-done((bf16[1024,1024]{1,0:T(8,128)(2,1)S(1)}, bf16[1024,1024]{1,0:T(8,128)(2,1)}, u32[]{:S(2)}) %copy-start.8) | copy-done | bytes 2097176
  49.0 1.0 copy-done.12
  50.0 1.0 copy-done.14
  51.1 1.2 %filter_spectrum.1.filt_ref = f32[2,1024,128]{2,1,0:T(8,128)S(1)} custom-call(bf16[128,1024]{1,0:T(8,128)(2,1)S(1)} %pad_maximum_fusion.rows_ref, bf16[1024,1024]{1,0:T(8,128)(2,1)S(1)} %copy-done.7, bf16[1024,1024]{1,0:T(8,128)(2,1)S(1)} %copy-done.8, f32[1024,128]{1,0:T(8,128)S(1)} %copy-done.12, f32[1024,128]{1,0:T(8,128)S(1)} %copy-done.14, ...), custom_call_target="tpu_custom_call" | custom-call | flops 536870912 | bytes 5242880 | tf_op jit(solution)/shard_map/filter_spectrum/pallas_call | solution.py:92
  52.3 0.0 all-to-all-done.x_ref
  52.3 0.0 copy-start.9
  52.3 1.6 %copy-done.9 = bf16[1024,1024]{1,0:T(8,128)(2,1)S(1)} copy-done((bf16[1024,1024]{1,0:T(8,128)(2,1)S(1)}, bf16[1024,1024]{1,0:T(8,128)(2,1)}, u32[]{:S(2)}) %copy-start.9) | copy-done | bytes 2097176
  53.9 1.0 copy-done.13
  55.0 1.0 copy-done.15
  56.0 9.6 %spectra.1 = (bf16[2048,512]{1,0:T(8,128)(2,1)S(1)}, f32[64,1024]{1,0:T(8,128)S(1)}) custom-call(bf16[32,2,128,128]{3,2,1,0:T(8,128)(2,1)} %all-to-all-done.x_ref, bf16[1024,1024]{1,0:T(8,128)(2,1)S(1)} %copy-done.7, bf16[1024,1024]{1,0:T(8,128)(2,1)S(1)} %copy-done.9, f32[2,1024,128]{2,1,0:T(8,128)S(1)} %filter_spectrum.1.filt_ref, ...), custom_call_target="tpu_custom_call" | custom-call | flops 4508876800 | bytes 9437184 | tf_op jit(solution)/shard_map/spectra/pallas_call | solution.py:140
  65.6 0.0 copy-start.16
  65.6 1.3 %copy-done.16 = bf16[2048,512]{1,0:T(8,128)(2,1)} copy-done((bf16[2048,512]{1,0:T(8,128)(2,1)}, bf16[2048,512]{1,0:T(8,128)(2,1)S(1)}, u32[]{:S(2)}) %copy-start.16) | copy-done | bytes 2097176
  67.0 0.6 collective-permute-start.4
  67.6 9.5 %collective-permute-done.4 = f32[64,512]{1,0:T(8,128)S(1)} collective-permute-done((f32[64,512]{1,0:T(8,128)S(1)}, f32[64,512]{1,0:T(8,128)S(1)}, u32[]{:S(2)}, u32[]{:S(2)}) %collective-permute-start.4) | collective-permute-done | bytes 131104 | tf_op jit(solution)/shard_map/ppermute | solution.py:218
  77.1 1.7 %collective-permute-start.5 = (f32[64,256]{1,0:T(8,128)S(1)}, f32[64,256]{1,0:T(8,128)S(1)}, u32[]{:S(2)}, u32[]{:S(2)}) collective-permute-start(f32[64,256]{1,0:T(8,128)S(1)} %slice_select_fusion.1), channel_id=1, source_target_pairs={{0,8},{4,12},{8,0},{12,4},{16,24},{20,28},{24,16},{28,20},{1,9},{5... | collective-permute-start | bytes 196616 | tf_op jit(solution)/shard_map/ppermute | solution.py:218
  78.8 1.6 %copy-done.10 = bf16[1024,1024]{1,0:T(8,128)(2,1)S(1)} copy-done((bf16[1024,1024]{1,0:T(8,128)(2,1)S(1)}, bf16[1024,1024]{1,0:T(8,128)(2,1)}, u32[]{:S(2)}) %copy-start.10) | copy-done | bytes 2097176
  80.4 1.6 %copy-done.17 = bf16[2048,512]{1,0:T(8,128)(2,1)S(1)} copy-done((bf16[2048,512]{1,0:T(8,128)(2,1)S(1)}, bf16[2048,512]{1,0:T(8,128)(2,1)}, u32[]{:S(2)}) %copy-start.17) | copy-done | bytes 2097176
  82.0 2.3 %back.1 = bf16[32,128,128]{2,1,0:T(8,128)(2,1)S(1)} custom-call(bf16[2048,512]{1,0:T(8,128)(2,1)S(1)} %copy-done.17, bf16[1024,1024]{1,0:T(8,128)(2,1)S(1)} %copy-done.7, bf16[1024,1024]{1,0:T(8,128)(2,1)S(1)} %copy-done.10), custom_call_target="tpu_custom_call" | custom-call | flops 2202009600 | bytes 7340032 | tf_op jit(solution)/shard_map/back/pallas_call | solution.py:166
  84.3 0.0 copy-start.11
  84.4 1.0 copy-done.11
  85.3 4.8 %all-to-all-start.1 = ((bf16[32,128,128]{2,1,0:T(8,128)(2,1)}), bf16[32,128,128]{2,1,0:T(8,128)(2,1)}, u32[]{:S(2)}, u32[]{:S(2)}) async-start(bf16[32,128,128]{2,1,0:T(8,128)(2,1)} %copy-done.11), calls=%async_computation.1 | async-start | bytes 2097152 | tf_op jit(solution)/shard_map/all_to_all | solution.py:276
  90.1 0.0 copy-start.1
  90.1 0.0 copy-start.3
  90.1 0.0 collective-permute-done.5
  90.2 7.8 %collective-permute-start.6 = (f32[64,128]{1,0:T(8,128)S(1)}, f32[64,128]{1,0:T(8,128)S(1)}, u32[]{:S(2)}, u32[]{:S(2)}) collective-permute-start(f32[64,128]{1,0:T(8,128)S(1)} %get-tuple-element.17), channel_id=1, source_target_pairs={{0,0},{4,32},{8,64},{12,96},{16,128},{20,160},{24,192},{28,224},{3... | collective-permute-start | bytes 98312 | tf_op jit(solution)/shard_map/ppermute | solution.py:225
  98.0 2.9 %collective-permute-start.7 = (f32[64,128]{1,0:T(8,128)S(1)}, f32[64,128]{1,0:T(8,128)S(1)}, u32[]{:S(2)}, u32[]{:S(2)}) collective-permute-start(f32[64,128]{1,0:T(8,128)S(1)} %get-tuple-element.16), channel_id=1, source_target_pairs={{0,32},{32,36},{64,40},{96,44},{128,48},{160,52},{192,56},{224,60}... | collective-permute-start | bytes 98312 | tf_op jit(solution)/shard_map/ppermute | solution.py:225
  100.8 0.0 copy-done.5
  100.8 2.4 %multiply_convert_fusion = bf16[1,128,4096]{2,1,0:T(8,128)(2,1)} fusion(bf16[1,128,4096]{2,1,0:T(8,128)(2,1)} %param.17, bf16[1,128,4096]{2,1,0:T(8,128)(2,1)S(1)} %copy-done.5), kind=kLoop, calls=%fused_computation | loop fusion | flops 2097152 | bytes 3145728 | tf_op jit(solution)/shard_map/convert_element_type | solution.py:268
  103.3 0.8 collective-permute-done.6
  104.1 5.9 %collective-permute-done.7 = f32[64,128]{1,0:T(8,128)S(1)} collective-permute-done((f32[64,128]{1,0:T(8,128)S(1)}, f32[64,128]{1,0:T(8,128)S(1)}, u32[]{:S(2)}, u32[]{:S(2)}) %collective-permute-start.7) | collective-permute-done | bytes 32800 | tf_op jit(solution)/shard_map/ppermute | solution.py:225
  110.0 0.6 add.30
  110.6 1.5 %all-to-all-done.1.conv_ref = bf16[32,128,128]{2,1,0:T(8,128)(2,1)} async-done(((bf16[32,128,128]{2,1,0:T(8,128)(2,1)}), bf16[32,128,128]{2,1,0:T(8,128)(2,1)}, u32[]{:S(2)}, u32[]{:S(2)}) %all-to-all-start.1) | async-done | bytes 1048608 | tf_op jit(solution)/shard_map/all_to_all | solution.py:276
  112.2 0.0 copy-done.1
  112.2 0.0 copy-done.3
  112.2 5.4 %unpack.1 = (bf16[128,4096]{1,0:T(8,128)(2,1)}, bf16[128,4096]{1,0:T(8,128)(2,1)}) custom-call(bf16[32,128,128]{2,1,0:T(8,128)(2,1)} %all-to-all-done.1.conv_ref, bf16[128,4096]{1,0:T(8,128)(2,1)S(1)} %bitcast.8, bf16[128,4096]{1,0:T(8,128)(2,1)S(1)} %bitcast.12, bf16[128,4096]{1,0:T(8,128)(2,1)S(1)} %bitcast.9, bf16[128,4096]{1,0:T(8,128)(2,1)S(1)} %bitcast.13), custom_call_target="tpu_custom_call" | custom-call | flops 2097152 | bytes 5242880 | tf_op jit(solution)/shard_map/unpack/pallas_call | solution.py:205
  (26 shorter events, 0.3 us)
Async XLA Ops:
  0.6 1.2 %copy-start = (bf16[1,128,4096]{2,1,0:T(8,128)(2,1)S(1)}, bf16[1,128,4096]{2,1,0:T(8,128)(2,1)}, u32[]{:S(2)}) copy-start(bf16[1,128,4096]{2,1,0:T(8,128)(2,1)} %param.15) | copy-start | bytes 3145732
  1.9 1.2 %copy-start.2 = (bf16[1,128,4096]{2,1,0:T(8,128)(2,1)S(1)}, bf16[1,128,4096]{2,1,0:T(8,128)(2,1)}, u32[]{:S(2)}) copy-start(bf16[1,128,4096]{2,1,0:T(8,128)(2,1)} %param.16) | copy-start | bytes 3145732
  3.1 1.2 %copy-start.4 = (bf16[1,128,4096]{2,1,0:T(8,128)(2,1)S(1)}, bf16[1,128,4096]{2,1,0:T(8,128)(2,1)}, u32[]{:S(2)}) copy-start(bf16[1,128,4096]{2,1,0:T(8,128)(2,1)} %param.18) | copy-start | bytes 3145732
  4.3 1.2 %copy-start.6 = (bf16[1,128,4096]{2,1,0:T(8,128)(2,1)S(1)}, bf16[1,128,4096]{2,1,0:T(8,128)(2,1)}, u32[]{:S(2)}) copy-start(bf16[1,128,4096]{2,1,0:T(8,128)(2,1)} %param.14) | copy-start | bytes 3145732
  7.9 7.6 %copy-start.20 = (f32[64,128]{1,0:T(8,128)S(1)}, f32[64,128]{1,0:T(8,128)}, u32[]{:S(2)}) copy-start(f32[64,128]{1,0:T(8,128)} %param.19) | copy-start | bytes 98308
  7.9 26.0 %copy-start.18 = (f32[64,128]{1,0:T(8,128)S(1)}, f32[64,128]{1,0:T(8,128)}, u32[]{:S(2)}) copy-start(f32[64,128]{1,0:T(8,128)} %constant.63.clone) | copy-start | bytes 98308
  7.9 26.0 %copy-start.19 = (f32[64,128]{1,0:T(8,128)S(1)}, f32[64,128]{1,0:T(8,128)}, u32[]{:S(2)}) copy-start(f32[64,128]{1,0:T(8,128)} %constant.64.clone) | copy-start | bytes 98308
  7.9 30.9 %copy-start.21 = (f32[1,128]{1,0:T(1,128)S(1)}, f32[1,128]{1,0:T(1,128)}, u32[]{:S(2)}) copy-start(f32[1,128]{1,0:T(1,128)} %constant.61.clone) | copy-start | bytes 1540
  7.9 30.9 %copy-start.22 = (f32[1,128]{1,0:T(1,128)S(1)}, f32[1,128]{1,0:T(1,128)}, u32[]{:S(2)}) copy-start(f32[1,128]{1,0:T(1,128)} %constant.62.clone) | copy-start | bytes 1540
  7.9 44.4 %all-to-all-start = ((bf16[32,2,128,128]{3,2,1,0:T(8,128)(2,1)}), bf16[32,2,128,128]{3,2,1,0:T(8,128)(2,1)}, u32[]{:S(2)}, u32[]{:S(2)}) async-start(bf16[32,2,128,128]{3,2,1,0:T(8,128)(2,1)} %pack.1), calls=%async_computation | async-start | bytes 4194304 | tf_op jit(solution)/shard_map/all_to_all | solution.py:266
  15.5 31.8 %copy-start.7 = (bf16[1024,1024]{1,0:T(8,128)(2,1)S(1)}, bf16[1024,1024]{1,0:T(8,128)(2,1)}, u32[]{:S(2)}) copy-start(bf16[1024,1024]{1,0:T(8,128)(2,1)} %constant.57.clone.cos_ref) | copy-start | bytes 6291460
  15.6 14.3 %collective-permute-start = (bf16[64,128]{1,0:T(8,128)(2,1)S(1)}, bf16[64,128]{1,0:T(8,128)(2,1)S(1)}, u32[]{:S(2)}, u32[]{:S(2)}) collective-permute-start(bf16[64,128]{1,0:T(8,128)(2,1)S(1)} %convert_element_type.15), channel_id=1, source_target_pairs={{0,0},{4,32},{8,64},{12,96},{16,128},{20,160},{24,192},{28,224},{3... | collective-permute-start | bytes 49160 | tf_op jit(solution)/shard_map/ppermute | solution.py:225
  29.8 3.9 %collective-permute-start.1 = (bf16[64,128]{1,0:T(8,128)(2,1)S(1)}, bf16[64,128]{1,0:T(8,128)(2,1)S(1)}, u32[]{:S(2)}, u32[]{:S(2)}) collective-permute-start(bf16[64,128]{1,0:T(8,128)(2,1)S(1)} %collective-permute-done), channel_id=1, source_target_pairs={{0,4},{4,0},{8,12},{12,8},{16,20},{20,16},{24,28},{28,24},{1,5},{5... | collective-permute-start | bytes 49160 | tf_op jit(solution)/shard_map/ppermute | solution.py:218
  33.8 4.9 %collective-permute-start.2 = (bf16[64,256]{1,0:T(8,128)(2,1)S(1)}, bf16[64,256]{1,0:T(8,128)(2,1)S(1)}, u32[]{:S(2)}, u32[]{:S(2)}) collective-permute-start(bf16[64,256]{1,0:T(8,128)(2,1)S(1)} %pad_maximum_fusion.3), channel_id=1, source_target_pairs={{0,8},{4,12},{8,0},{12,4},{16,24},{20,28},{24,16},{28,20},{1,9},{5... | collective-permute-start | bytes 98312 | tf_op jit(solution)/shard_map/ppermute | solution.py:218
  38.7 8.3 %collective-permute-start.3 = (bf16[64,512]{1,0:T(8,128)(2,1)S(1)}, bf16[64,512]{1,0:T(8,128)(2,1)S(1)}, u32[]{:S(2)}, u32[]{:S(2)}) collective-permute-start(bf16[64,512]{1,0:T(8,128)(2,1)S(1)} %pad_maximum_fusion.2), channel_id=1, source_target_pairs={{0,16},{4,20},{8,24},{12,28},{16,0},{20,4},{24,8},{28,12},{1,17},{... | collective-permute-start | bytes 196616 | tf_op jit(solution)/shard_map/ppermute | solution.py:218
  47.4 1.6 %copy-start.8 = (bf16[1024,1024]{1,0:T(8,128)(2,1)S(1)}, bf16[1024,1024]{1,0:T(8,128)(2,1)}, u32[]{:S(2)}) copy-start(bf16[1024,1024]{1,0:T(8,128)(2,1)} %constant.58.clone.sin_ref) | copy-start | bytes 6291460
  49.0 1.0 copy-start.12
  50.0 1.0 copy-start.14
  52.3 1.6 %copy-start.9 = (bf16[1024,1024]{1,0:T(8,128)(2,1)S(1)}, bf16[1024,1024]{1,0:T(8,128)(2,1)}, u32[]{:S(2)}) copy-start(bf16[1024,1024]{1,0:T(8,128)(2,1)} %constant.58.clone.sin_ref) | copy-start | bytes 6291460
  53.9 1.0 copy-start.13
  55.0 1.0 copy-start.15
  65.6 1.4 %copy-start.16 = (bf16[2048,512]{1,0:T(8,128)(2,1)}, bf16[2048,512]{1,0:T(8,128)(2,1)S(1)}, u32[]{:S(2)}) copy-start(bf16[2048,512]{1,0:T(8,128)(2,1)S(1)} %get-tuple-element.8.uv_ref) | copy-start | bytes 6291460
  67.0 10.1 %collective-permute-start.4 = (f32[64,512]{1,0:T(8,128)S(1)}, f32[64,512]{1,0:T(8,128)S(1)}, u32[]{:S(2)}, u32[]{:S(2)}) collective-permute-start(f32[64,512]{1,0:T(8,128)S(1)} %slice_select_fusion), channel_id=1, source_target_pairs={{0,16},{4,20},{8,24},{12,28},{16,0},{20,4},{24,8},{28,12},{1,17},{... | collective-permute-start | bytes 393224 | tf_op jit(solution)/shard_map/ppermute | solution.py:218
  77.1 13.0 %collective-permute-start.5 = (f32[64,256]{1,0:T(8,128)S(1)}, f32[64,256]{1,0:T(8,128)S(1)}, u32[]{:S(2)}, u32[]{:S(2)}) collective-permute-start(f32[64,256]{1,0:T(8,128)S(1)} %slice_select_fusion.1), channel_id=1, source_target_pairs={{0,8},{4,12},{8,0},{12,4},{16,24},{20,28},{24,16},{28,20},{1,9},{5... | collective-permute-start | bytes 196616 | tf_op jit(solution)/shard_map/ppermute | solution.py:218
  78.8 1.6 %copy-start.10 = (bf16[1024,1024]{1,0:T(8,128)(2,1)S(1)}, bf16[1024,1024]{1,0:T(8,128)(2,1)}, u32[]{:S(2)}) copy-start(bf16[1024,1024]{1,0:T(8,128)(2,1)} %constant.58.clone.sin_ref) | copy-start | bytes 6291460
  80.4 1.6 %copy-start.17 = (bf16[2048,512]{1,0:T(8,128)(2,1)S(1)}, bf16[2048,512]{1,0:T(8,128)(2,1)}, u32[]{:S(2)}) copy-start(bf16[2048,512]{1,0:T(8,128)(2,1)} %copy-done.16) | copy-start | bytes 6291460
  84.3 1.0 copy-start.11
  85.3 15.5 %copy-start.5 = (bf16[1,128,4096]{2,1,0:T(8,128)(2,1)S(1)}, bf16[1,128,4096]{2,1,0:T(8,128)(2,1)}, u32[]{:S(2)}) copy-start(bf16[1,128,4096]{2,1,0:T(8,128)(2,1)} %param.18) | copy-start | bytes 3145732
  85.3 26.8 %all-to-all-start.1 = ((bf16[32,128,128]{2,1,0:T(8,128)(2,1)}), bf16[32,128,128]{2,1,0:T(8,128)(2,1)}, u32[]{:S(2)}, u32[]{:S(2)}) async-start(bf16[32,128,128]{2,1,0:T(8,128)(2,1)} %copy-done.11), calls=%async_computation.1 | async-start | bytes 2097152 | tf_op jit(solution)/shard_map/all_to_all | solution.py:276
  90.1 22.0 %copy-start.1 = (bf16[1,128,4096]{2,1,0:T(8,128)(2,1)S(1)}, bf16[1,128,4096]{2,1,0:T(8,128)(2,1)}, u32[]{:S(2)}) copy-start(bf16[1,128,4096]{2,1,0:T(8,128)(2,1)} %param.15) | copy-start | bytes 3145732
  90.1 22.0 %copy-start.3 = (bf16[1,128,4096]{2,1,0:T(8,128)(2,1)S(1)}, bf16[1,128,4096]{2,1,0:T(8,128)(2,1)}, u32[]{:S(2)}) copy-start(bf16[1,128,4096]{2,1,0:T(8,128)(2,1)} %param.16) | copy-start | bytes 3145732
  90.2 13.9 %collective-permute-start.6 = (f32[64,128]{1,0:T(8,128)S(1)}, f32[64,128]{1,0:T(8,128)S(1)}, u32[]{:S(2)}, u32[]{:S(2)}) collective-permute-start(f32[64,128]{1,0:T(8,128)S(1)} %get-tuple-element.17), channel_id=1, source_target_pairs={{0,0},{4,32},{8,64},{12,96},{16,128},{20,160},{24,192},{28,224},{3... | collective-permute-start | bytes 98312 | tf_op jit(solution)/shard_map/ppermute | solution.py:225
  98.0 12.0 %collective-permute-start.7 = (f32[64,128]{1,0:T(8,128)S(1)}, f32[64,128]{1,0:T(8,128)S(1)}, u32[]{:S(2)}, u32[]{:S(2)}) collective-permute-start(f32[64,128]{1,0:T(8,128)S(1)} %get-tuple-element.16), channel_id=1, source_target_pairs={{0,32},{32,36},{64,40},{96,44},{128,48},{160,52},{192,56},{224,60}... | collective-permute-start | bytes 98312 | tf_op jit(solution)/shard_map/ppermute | solution.py:225

commit v2 on v1

v2 whole, which is shorter than its diff:
```python
import functools

import jax
import jax.numpy as jnp
import numpy as np
from jax import lax
from jax.experimental import pallas as pl
from jax.experimental.pallas import tpu as pltpu
from jax.sharding import Mesh
from jax.sharding import PartitionSpec as P

CTX = ("xh", "y")
PLANE = ("xh", "y", "xl", "core")
CTX_Z = ("xh", "y", "z")
SEQ = 1024
BLOCK = 128
LANES = 128
SPLIT = 4
WIDTH = SPLIT * LANES
GROUPS = 32
STEP = 32
CUTS = 4
MIB = 1024 * 1024
F32 = jnp.float32
BF16 = jnp.bfloat16
OWNER = (3, 0, 2, 1, 5, 6, 4, 7)
LAG_AT = (5, 7, 6, 4, 2, 0, 1, 3)


def chunk_of(block):
    return 4 * OWNER[block // 4] + block % 4


def slot_of(z, lag_block):
    n = z ^ LAG_AT[lag_block]
    return (n & 1) * 4 + (n & 2) + (n >> 2)


def dot(a, b):
    return jnp.dot(a, b, preferred_element_type=F32)


def dot_nt(a, b):
    return lax.dot_general(a, b, (((1,), (1,)), ((), ())), preferred_element_type=F32)


def dot_tn(a, b):
    return lax.dot_general(a, b, (((0,), (0,)), ((), ())), preferred_element_type=F32)


def seeds():
    odd = 2 * np.arange(SEQ, dtype=np.int64) + 1
    coarse = 2 * STEP * np.arange(SEQ // STEP, dtype=np.int64)
    fine = 2 * np.arange(STEP, dtype=np.int64) + 1
    out = []
    for part in (coarse, fine):
        angle = (np.multiply.outer(part, odd) % (8 * SEQ)).astype(np.float64) * (np.pi / (4 * SEQ))
        out += [np.cos(angle), np.sin(angle)]
    return np.stack(out).astype(np.float32)


def fill_tables(seed, cos, sin, turn, first, last):
    for a in range(first // STEP, last // STEP):
        ca, sa = seed[0, a:a + 1, :], seed[1, a:a + 1, :]
        c = ca * seed[2] - sa * seed[3]
        s = sa * seed[2] + ca * seed[3]
        rows = pl.ds(a * STEP, STEP)
        cos[rows, :] = c.astype(BF16)
        sin[rows, :] = s.astype(BF16)
        turn[0, rows, :] = jnp.broadcast_to(c[:, :1], (STEP, LANES))
        turn[1, rows, :] = jnp.broadcast_to(s[:, :1], (STEP, LANES))


def lanes_of(tile):
    return slice(tile * LANES, (tile + 1) * LANES)


def pack_kernel(q_hbm, g_hbm, k_hbm, v_hbm, x_hbm, buf, out, sem_in, sem_out):
    tiles = GROUPS // 2 // CUTS
    width = tiles * LANES
    low = lax.broadcasted_iota(jnp.int32, (BLOCK, LANES), 1) < LANES // 2
    arriving = []
    for j in range(CUTS):
        copies = []
        for i, ref in enumerate((q_hbm, g_hbm, k_hbm, v_hbm)):
            for s, at in enumerate((j, 2 * CUTS - 1 - j)):
                cols = pl.ds(at * width, width)
                copies.append(pltpu.make_async_copy(ref.at[:, cols], buf.at[i, :, cols], sem_in.at[j, i, s]))
        for copy in copies:
            copy.start()
        arriving.append(copies)
    leaving = []
    for j in range(CUTS):
        for copy in arriving[j]:
            copy.wait()
        for t in range(j * tiles, (j + 1) * tiles):
            ahead, behind = lanes_of(t), lanes_of(GROUPS - 1 - t)
            even, odd = chunk_of(2 * t), chunk_of(2 * t + 1)
            for kind in range(2):
                a, b = 2 * kind, 2 * kind + 1
                f = buf[a, :, ahead].astype(F32) * buf[b, :, ahead].astype(F32)
                r = buf[a, :, behind].astype(F32) * buf[b, :, behind].astype(F32)
                out[even, kind] = jnp.where(low, f, r).astype(BF16)
                out[odd, kind] = jnp.where(low, r, f).astype(BF16)
            pair = pl.ds(even, 2)
            copy = pltpu.make_async_copy(out.at[pair], x_hbm.at[pair], sem_out.at[t])
            copy.start()
            leaving.append(copy)
    for copy in leaving:
        copy.wait()


ANY = pl.BlockSpec(memory_space=pl.ANY)
VMEM = pl.BlockSpec(memory_space=pltpu.VMEM)
SMEM = pl.BlockSpec(memory_space=pltpu.SMEM)
HBM = pl.BlockSpec(memory_space=pltpu.HBM)
LIMIT = pltpu.CompilerParams(vmem_limit_bytes=60 * MIB)
SMALL = pltpu.CompilerParams(vmem_limit_bytes=24 * MIB)


def pack(q, g, k, v):
    return pl.pallas_call(
        pack_kernel,
        in_specs=[ANY] * 4,
        out_specs=ANY,
        out_shape=jax.ShapeDtypeStruct((GROUPS, 2, BLOCK, LANES), BF16),
        scratch_shapes=[
            pltpu.VMEM((4,) + q.shape, BF16),
            pltpu.VMEM((GROUPS, 2, BLOCK, LANES), BF16),
            pltpu.SemaphoreType.DMA((CUTS, 4, 2)),
            pltpu.SemaphoreType.DMA((GROUPS // 2,)),
        ],
        compiler_params=LIMIT,
        cost_estimate=pl.CostEstimate(flops=2 * MIB, bytes_accessed=6 * MIB, transcendentals=0),
        name="pack",
    )(q, g, k, v)


def filter_kernel(place_ref, seed, near, far, filt, seed_out, rows_in, cos, sin, turn):
    odd, z = place_ref[0], place_ref[1]
    step = 256
    row = lax.broadcasted_iota(jnp.int32, (LANES, LANES // 2), 0)
    col = lax.broadcasted_iota(jnp.int32, (LANES, LANES // 2), 1)
    ahead = row - jnp.where(odd == 0, 0, LANES // 2)
    behind = jnp.where(odd == 0, LANES, LANES // 2) - 1 - row
    spread = jnp.where((col == ahead) | (col == behind), 1.0, 0.0).astype(BF16)
    for block in range(SEQ // BLOCK):
        slot = slot_of(z, block)
        lags = jnp.where(slot < 4, near[slot % 4], far[slot % 4])
        rows_in[:, lanes_of(block)] = dot(spread, lags).astype(BF16)
    sign = strand_sign(odd)
    for n in range(SEQ // step):
        fill_tables(seed, cos, sin, turn, n * step, (n + 1) * step)
        at = pl.ds(n * step, step)
        fc, fs = dot_nt(cos[at, :], rows_in[...]), dot_nt(sin[at, :], rows_in[...])
        tc, ts = turn[0, at, :], turn[1, at, :]
        filt[0, at, :] = fc * tc + fs * ts
        filt[1, at, :] = (fc * ts - fs * tc) * sign
    seed_out[...] = seed[...]


def filter_spectrum(place, near, far):
    seed = jnp.asarray(seeds())
    return pl.pallas_call(
        filter_kernel,
        in_specs=[SMEM, VMEM, VMEM, VMEM],
        out_specs=(VMEM, VMEM),
        out_shape=(
            jax.ShapeDtypeStruct((2, SEQ, LANES), F32),
            jax.ShapeDtypeStruct(seed.shape, F32),
        ),
        scratch_shapes=[
            pltpu.VMEM((LANES, SEQ), BF16),
            pltpu.VMEM((SEQ, SEQ), BF16),
            pltpu.VMEM((SEQ, SEQ), BF16),
            pltpu.VMEM((2, SEQ, LANES), F32),
        ],
        compiler_params=SMALL,
        cost_estimate=pl.CostEstimate(flops=1, bytes_accessed=1, transcendentals=0),
        name="filter_spectrum",
    )(place, seed, near, far)


def strand_sign(odd):
    lane = lax.broadcasted_iota(jnp.int32, (1, LANES), 1)
    return jnp.where((lane < LANES // 2) == (odd == 0), -1.0, 1.0).astype(F32)


def core_kernel(place_ref, x, filt, seed, conv_hbm, keep, give, cos, sin, turn, uv, prod, conv, folded, sem_out):
    odd, z = place_ref[0], place_ref[1]
    step = 256
    steps = SEQ // step
    sign = strand_sign(odd)
    def columns(kind):
        tiles = [[x[SPLIT * i + q, kind] for i in range(SEQ // BLOCK)] for q in range(SPLIT)]
        return jnp.concatenate([jnp.concatenate(tile, axis=0) for tile in tiles], axis=1)

    def summed(value):
        return (value[:, lanes_of(0)] + value[:, lanes_of(1)]) + (value[:, lanes_of(2)] + value[:, lanes_of(3)])

    for n in range(steps):
        fill_tables(seed, cos, sin, turn, n * step, (n + 1) * step)
        at = pl.ds(n * step, step)
        c_rows, s_rows = cos[at, :], sin[at, :]
        tc, ts = turn[0, at, :], turn[1, at, :]
        re, im = filt[0, at, :], filt[1, at, :]
        grad = columns(0)
        cg, sg = dot(c_rows, grad), dot(s_rows, grad)
        for q in range(SPLIT):
            a, b = cg[:, lanes_of(q)], sg[:, lanes_of(q)]
            uv[0, at, lanes_of(q)] = (a * re + b * im).astype(BF16)
            uv[1, at, lanes_of(q)] = (b * re - a * im).astype(BF16)
        mixed = columns(1)
        cm, sm = dot(c_rows, mixed), dot(s_rows, mixed)
        sum_re = summed(cg * cm + sg * sm)
        sum_im = summed(sg * cm - cg * sm) * sign
        prod[0, at, :] = (sum_re * tc + sum_im * ts).astype(BF16)
        prod[1, at, :] = (sum_re * ts - sum_im * tc).astype(BF16)

    lags = dot_tn(prod[0], cos[...]) + dot_tn(prod[1], sin[...])
    row = lax.broadcasted_iota(jnp.int32, (LANES // 2, LANES), 0)
    col = lax.broadcasted_iota(jnp.int32, (LANES // 2, LANES), 1)
    row = jnp.where(odd == 0, row, LANES // 2 - 1 - row)
    fold = jnp.where((col == row) | (col == LANES - 1 - row), 1.0, 0.0).astype(F32)
    total = jnp.dot(fold, lags * (1.0 / SEQ), precision=lax.Precision.HIGHEST, preferred_element_type=F32)
    for block in range(SEQ // BLOCK):
        folded[slot_of(z, block)] = total[:, lanes_of(block)]
    keep[...] = folded[:4]
    give[...] = folded[4:]

    leaving = []
    size = SPLIT * (step // BLOCK)
    for n in range(steps):
        at = pl.ds(n * step, step)
        value = dot(cos[at, :], uv[0]) + dot(sin[at, :], uv[1])
        value = (value * (1.0 / SEQ)).astype(BF16)
        for i in range(step // BLOCK):
            for q in range(SPLIT):
                conv[n * size + SPLIT * i + q] = value[i * BLOCK:(i + 1) * BLOCK, lanes_of(q)]
        part = pl.ds(n * size, size)
        copy = pltpu.make_async_copy(conv.at[part], conv_hbm.at[part], sem_out.at[n])
        copy.start()
        leaving.append(copy)
    for copy in leaving:
        copy.wait()


def core(place, x, filt, seed):
    part = jax.ShapeDtypeStruct((4, LANES // 2, BLOCK), F32)
    return pl.pallas_call(
        core_kernel,
        in_specs=[SMEM, VMEM, VMEM, VMEM],
        out_specs=(HBM, VMEM, VMEM),
        out_shape=(jax.ShapeDtypeStruct((GROUPS, BLOCK, LANES), BF16), part, part),
        scratch_shapes=[
            pltpu.VMEM((SEQ, SEQ), BF16),
            pltpu.VMEM((SEQ, SEQ), BF16),
            pltpu.VMEM((2, SEQ, LANES), F32),
            pltpu.VMEM((2, SEQ, WIDTH), BF16),
            pltpu.VMEM((2, SEQ, LANES), BF16),
            pltpu.VMEM((GROUPS, BLOCK, LANES), BF16),
            pltpu.VMEM((8, LANES // 2, BLOCK), F32),
            pltpu.SemaphoreType.DMA((4,)),
        ],
        compiler_params=SMALL,
        cost_estimate=pl.CostEstimate(flops=7000 * MIB, bytes_accessed=4 * MIB, transcendentals=0),
        name="core",
    )(place, x, filt, seed)


def unpack_kernel(conv, k_in, v_in, key_hbm, value_hbm, key, value, sem_out):
    tiles = GROUPS // 2 // CUTS
    width = tiles * LANES
    low = lax.broadcasted_iota(jnp.int32, (BLOCK, LANES), 1) < LANES // 2
    leaving = []
    for j in range(CUTS):
        for t in range(j * tiles, (j + 1) * tiles):
            even = conv[chunk_of(2 * t)].astype(F32)
            odd = conv[chunk_of(2 * t + 1)].astype(F32)
            ahead, behind = jnp.where(low, even, odd), jnp.where(low, odd, even)
            for cols, grad in ((lanes_of(t), ahead), (lanes_of(GROUPS - 1 - t), behind)):
                key[:, cols] = (grad * v_in[:, cols].astype(F32)).astype(BF16)
                value[:, cols] = (grad * k_in[:, cols].astype(F32)).astype(BF16)
        for s, at in enumerate((j, 2 * CUTS - 1 - j)):
            cols = pl.ds(at * width, width)
            for m, (src, dst) in enumerate(((key, key_hbm), (value, value_hbm))):
                copy = pltpu.make_async_copy(src.at[:, cols], dst.at[:, cols], sem_out.at[j, s, m])
                copy.start()
                leaving.append(copy)
    for copy in leaving:
        copy.wait()


def unpack(conv, k, v):
    shape = jax.ShapeDtypeStruct(k.shape, BF16)
    whole = pltpu.VMEM(k.shape, BF16)
    return pl.pallas_call(
        unpack_kernel,
        in_specs=[VMEM] * 3,
        out_specs=(ANY, ANY),
        out_shape=(shape, shape),
        scratch_shapes=[whole, whole, pltpu.SemaphoreType.DMA((CUTS, 2, 2))],
        compiler_params=SMALL,
        cost_estimate=pl.CostEstimate(flops=2 * MIB, bytes_accessed=5 * MIB, transcendentals=0),
        name="unpack",
    )(conv, k, v)


def times_kernel(a, b, out):
    out[...] = (a[...].astype(F32) * b[...].astype(F32)).astype(BF16)


def times(a, b):
    block = pl.BlockSpec((BLOCK // 2, a.shape[1]), lambda i: (i, 0))
    return pl.pallas_call(
        times_kernel,
        grid=(2,),
        in_specs=[block, block],
        out_specs=block,
        out_shape=jax.ShapeDtypeStruct(a.shape, BF16),
        compiler_params=SMALL,
        cost_estimate=pl.CostEstimate(flops=1, bytes_accessed=1, transcendentals=0),
        name="times",
    )(a, b)


def swap_z(block, bit):
    return lax.ppermute(block, "z", [(i, i ^ (1 << bit)) for i in range(8)])


def sent_out(filters):
    route = [(8 * l + n, 8 * OWNER[n] + LAG_AT[l]) for l in range(8) for n in range(8)]
    return lax.ppermute(filters[None], CTX_Z, route).astype(BF16)


def gathered_over_z(near):
    near = jnp.concatenate([near, swap_z(near, 2)], axis=0)
    near = jnp.concatenate([near, swap_z(near, 1)], axis=0)
    return near, swap_z(near, 0)


def summed_over_z(keep, give):
    keep = keep + swap_z(give, 0)
    keep = keep[:2] + swap_z(keep[2:], 1)
    return keep[0] + swap_z(keep[1], 2)


def sent_home(lags):
    route = [(8 * OWNER[n] + LAG_AT[l], 8 * l + n) for l in range(8) for n in range(8)]
    return lax.ppermute(lags, CTX_Z, route)


def local(query_gate, key_gate, value_in, conv_out, out_grad, filters):
    place = jnp.stack([lax.axis_index("core"), lax.axis_index("z")]).astype(jnp.int32)
    q, k, v, g = query_gate[0], key_gate[0], value_in[0], out_grad[0]
    x, near = lax.optimization_barrier((pack(q, g, k, v), sent_out(filters)))
    x = lax.all_to_all(x, PLANE, split_axis=0, concat_axis=0, tiled=True)

    near, far = gathered_over_z(near)
    filt, seed = filter_spectrum(place, near, far)
    filt, seed, query_grad = lax.optimization_barrier((filt, seed, times(g, conv_out[0])[None]))

    conv, keep, give = core(place, x, filt, seed)
    conv = lax.all_to_all(conv, PLANE, split_axis=0, concat_axis=0, tiled=True)
    lags, conv = lax.optimization_barrier((summed_over_z(keep, give), conv))
    filter_grad = sent_home(lags)
    key_grad, value_grad = unpack(conv, k, v)
    return query_grad, key_grad[None], value_grad[None], filter_grad


def solution(mesh):
    fine = Mesh(mesh.devices.reshape(2, 4, 8, 2, 2), ("xh", "y", "z", "xl", "core"))
    wide = P(("z", "xl", "core"), CTX, None)
    narrow = P(("z", "xl", "core"), CTX)
    return jax.shard_map(
        local,
        mesh=fine,
        in_specs=(wide,) * 5 + (narrow,),
        out_specs=(wide, wide, wide, narrow),
        check_vma=False,
    )
```

time: 119 us -> 93.9 us (0.79)
  the two profiles are of different devices: /device:TPU:192 before, /device:TPU:2 now
where the time goes in v2:
time: 93.9 us; the launch traced here: 93.4 us
  starting transfers between devices  42.8 us (46%)
  waiting for transfers between devices  24.8 us (26%)
  Pallas kernels  18.1 us (19%)
  local copies, waits for them, and re-layouts  6.07 us (6%)
    ppermute x6, starting transfers between devices, swap_z(): return lax.ppermute(block, 'z', [(i, i ^ 1 << bit) for i in range(8)])  19.2 us
    ppermute x6, waiting for transfers between devices, swap_z(): return lax.ppermute(block, 'z', [(i, i ^ 1 << bit) for i in range(8)])  16.8 us
    pallas_call x1, Pallas kernels, core(): pl.pallas_call(core_kernel, in_specs=[SMEM, VMEM, VMEM, VMEM], out_specs=...  9.75 us
    ppermute x1, starting transfers between devices, sent_out(): return lax.ppermute(filters[None], CTX_Z, route).astype(BF16)  9.2 us
    all_to_all x1, starting transfers between devices, local(): conv = lax.all_to_all(conv, PLANE, split_axis=0, concat_axis=0, tiled=True)  6.43 us
    unnamed x19, local copies, waits for them, and re-layouts  6.05 us
    ppermute x1, waiting for transfers between devices, sent_home(): return lax.ppermute(lags, CTX_Z, route)  4.45 us
    all_to_all x1, starting transfers between devices, local(): x = lax.all_to_all(x, PLANE, split_axis=0, concat_axis=0, tiled=True)  4.35 us
  transfers between devices with their start and end apart: 10, of which 8 were waited for; matrix products, arithmetic and copies ran while one was open for 0% of the time, Pallas kernels for 9%

profile of v2, /device:TPU:2, one launch (start us, length us, event | category | flops | bytes accessed | tf_op | source)
XLA Modules:
  0.0 93.4 jit_solution(7988147064213586271)
XLA Ops:
  0.6 0.8 bitcast_convert_fusion
  1.4 9.2 %collective-permute-start = (bf16[1,64,128]{2,1,0:T(8,128)(2,1)S(1)}, bf16[1,64,128]{2,1,0:T(8,128)(2,1)S(1)}, u32[]{:S(2)}, u32[]{:S(2)}) collective-permute-start(bf16[1,64,128]{2,1,0:T(8,128)(2,1)S(1)} %bitcast_convert_fusion), channel_id=1, source_target_pairs={{0,116},{4,20},{8,84},{12,52},{16,180},{20,212},{24,148},{28,244},... | collective-permute-start | bytes 49160 | tf_op jit(solution)/shard_map/ppermute | solution.py:333
  10.6 3.6 %pack.1 = bf16[32,2,128,128]{3,2,1,0:T(8,128)(2,1)} custom-call(bf16[128,4096]{1,0:T(8,128)(2,1)} %bitcast.26, bf16[128,4096]{1,0:T(8,128)(2,1)} %bitcast.18, bf16[128,4096]{1,0:T(8,128)(2,1)} %bitcast.20, bf16[128,4096]{1,0:T(8,128)(2,1)} %bitcast.22), custom_call_target="tpu_custom_call" | custom-call | flops 2097152 | bytes 6291456 | tf_op jit(solution)/shard_map/pack/pallas_call | solution.py:122
  14.2 0.0 copy-start
  14.2 0.0 collective-permute-done
  14.2 4.3 %all-to-all-start = ((bf16[32,2,128,128]{3,2,1,0:T(8,128)(2,1)}), bf16[32,2,128,128]{3,2,1,0:T(8,128)(2,1)S(1)}, u32[]{:S(2)}, u32[]{:S(2)}) async-start(bf16[32,2,128,128]{3,2,1,0:T(8,128)(2,1)} %pack.1), calls=%async_computation | async-start | bytes 4194304 | tf_op jit(solution)/shard_map/all_to_all | solution.py:357
  18.6 0.0 copy-done
  18.6 0.0 copy-start.3
  18.6 1.2 %copy-done.3 = bf16[1,128,4096]{2,1,0:T(8,128)(2,1)S(1)} copy-done((bf16[1,128,4096]{2,1,0:T(8,128)(2,1)S(1)}, bf16[1,128,4096]{2,1,0:T(8,128)(2,1)}, u32[]{:S(2)}) %copy-start.3) | copy-done | bytes 1048600
  19.8 1.1 %times.1 = bf16[128,4096]{1,0:T(8,128)(2,1)} custom-call(bf16[128,4096]{1,0:T(8,128)(2,1)S(1)} %bitcast.19, bf16[128,4096]{1,0:T(8,128)(2,1)S(1)} %bitcast.24), custom_call_target="tpu_custom_call" | custom-call | flops 1 | bytes 1 | tf_op jit(solution)/shard_map/times/pallas_call | solution.py:315
  20.9 5.4 %collective-permute-start.1 = (bf16[1,64,128]{2,1,0:T(8,128)(2,1)S(1)}, bf16[1,64,128]{2,1,0:T(8,128)(2,1)S(1)}, u32[]{:S(2)}, u32[]{:S(2)}) collective-permute-start(bf16[1,64,128]{2,1,0:T(8,128)(2,1)S(1)} %collective-permute-done), channel_id=1, source_target_pairs={{0,16},{4,20},{8,24},{12,28},{16,0},{20,4},{24,8},{28,12},{1,17},{... | collective-permute-start | bytes 49160 | tf_op jit(solution)/shard_map/ppermute | solution.py:328
  26.3 2.2 %collective-permute-done.1 = bf16[1,64,128]{2,1,0:T(8,128)(2,1)S(1)} collective-permute-done((bf16[1,64,128]{2,1,0:T(8,128)(2,1)S(1)}, bf16[1,64,128]{2,1,0:T(8,128)(2,1)S(1)}, u32[]{:S(2)}, u32[]{:S(2)}) %collective-permute-start.1) | collective-permute-done | bytes 16416 | tf_op jit(solution)/shard_map/ppermute | solution.py:328
  28.5 2.9 %collective-permute-start.2 = (bf16[2,64,128]{2,1,0:T(8,128)(2,1)S(1)}, bf16[2,64,128]{2,1,0:T(8,128)(2,1)S(1)}, u32[]{:S(2)}, u32[]{:S(2)}) collective-permute-start(bf16[2,64,128]{2,1,0:T(8,128)(2,1)S(1)} %pad_maximum_fusion), channel_id=1, source_target_pairs={{0,8},{4,12},{8,0},{12,4},{16,24},{20,28},{24,16},{28,20},{1,9},{5... | collective-permute-start | bytes 98312 | tf_op jit(solution)/shard_map/ppermute | solution.py:328
  31.4 1.9 %collective-permute-done.2 = bf16[2,64,128]{2,1,0:T(8,128)(2,1)S(1)} collective-permute-done((bf16[2,64,128]{2,1,0:T(8,128)(2,1)S(1)}, bf16[2,64,128]{2,1,0:T(8,128)(2,1)S(1)}, u32[]{:S(2)}, u32[]{:S(2)}) %collective-permute-start.2) | collective-permute-done | bytes 32800 | tf_op jit(solution)/shard_map/ppermute | solution.py:328
  33.4 1.9 %collective-permute-start.3 = (bf16[4,64,128]{2,1,0:T(8,128)(2,1)S(1)}, bf16[4,64,128]{2,1,0:T(8,128)(2,1)S(1)}, u32[]{:S(2)}, u32[]{:S(2)}) collective-permute-start(bf16[4,64,128]{2,1,0:T(8,128)(2,1)S(1)} %constant_dynamic-update-slice_fusion.near), channel_id=1, source_target_pairs={{0,4},{4,0},{8,12},{12,8},{16,20},{20,16},{24,28},{28,24},{1,5},{5... | collective-permute-start | bytes 196616 | tf_op jit(solution)/shard_map/ppermute | solution.py:328
  35.2 0.1 pad_add_fusion.place_ref
  35.3 2.3 %collective-permute-done.3.far = bf16[4,64,128]{2,1,0:T(8,128)(2,1)S(1)} collective-permute-done((bf16[4,64,128]{2,1,0:T(8,128)(2,1)S(1)}, bf16[4,64,128]{2,1,0:T(8,128)(2,1)S(1)}, u32[]{:S(2)}, u32[]{:S(2)}) %collective-permute-start.3) | collective-permute-done | bytes 65568 | tf_op jit(solution)/shard_map/ppermute | solution.py:328
  37.6 0.0 copy-start.5
  37.6 1.0 %copy-done.5 = f32[4,32,1024]{2,1,0:T(8,128)S(1)} copy-done((f32[4,32,1024]{2,1,0:T(8,128)S(1)}, f32[4,32,1024]{2,1,0:T(8,128)}, u32[]{:S(2)}) %copy-start.5) | copy-done | bytes 524312
  38.7 2.1 %filter_spectrum.1 = (f32[2,1024,128]{2,1,0:T(8,128)S(1)}, f32[4,32,1024]{2,1,0:T(8,128)S(1)}) custom-call(s32[2]{0:T(128)S(1)} %pad_add_fusion.place_ref, f32[4,32,1024]{2,1,0:T(8,128)S(1)} %copy-done.5, bf16[4,64,128]{2,1,0:T(8,128)(2,1)S(1)} %constant_dynamic-update-slice_fusion.near, bf16[4,64,128]{2,1,0:T(8,128)(2,1)S(1)} %collective-permute-done.3.far), custom_call_target="tpu_custom_call" | custom-call | flops 1 | bytes 1 | tf_op jit(solution)/shard_map/filter_spectrum/pallas_call | solution.py:164
  40.8 0.0 copy-start.6
  40.8 1.0 %copy-done.6 = f32[2,1024,128]{2,1,0:T(8,128)} copy-done((f32[2,1024,128]{2,1,0:T(8,128)}, f32[2,1024,128]{2,1,0:T(8,128)S(1)}, u32[]{:S(2)}) %copy-start.6) | copy-done | bytes 1048600
  41.7 3.6 %all-to-all-done.x = bf16[32,2,128,128]{3,2,1,0:T(8,128)(2,1)S(1)} async-done(((bf16[32,2,128,128]{3,2,1,0:T(8,128)(2,1)}), bf16[32,2,128,128]{3,2,1,0:T(8,128)(2,1)S(1)}, u32[]{:S(2)}, u32[]{:S(2)}) %all-to-all-start) | async-done | bytes 2097184 | tf_op jit(solution)/shard_map/all_to_all | solution.py:357
  45.3 0.0 copy-start.7
  45.3 1.2 %copy-done.7 = f32[2,1024,128]{2,1,0:T(8,128)S(1)} copy-done((f32[2,1024,128]{2,1,0:T(8,128)S(1)}, f32[2,1024,128]{2,1,0:T(8,128)}, u32[]{:S(2)}) %copy-start.7) | copy-done | bytes 1048600
  46.5 9.7 %core.1 = (bf16[32,128,128]{2,1,0:T(8,128)(2,1)S(1)}, f32[4,64,128]{2,1,0:T(8,128)S(1)}, f32[4,64,128]{2,1,0:T(8,128)S(1)}) custom-call(s32[2]{0:T(128)S(1)} %pad_add_fusion.place_ref, bf16[32,2,128,128]{3,2,1,0:T(8,128)(2,1)S(1)} %all-to-all-done.x, f32[2,1024,128]{2,1,0:T(8,128)S(1)} %copy-done.7, f32[4,32,1024]{2,1,0:T(8,128)S(1)} %get-tuple-element.24.seed), custom_call_target="tpu_custom_call" | custom-call | flops 7340032000 | bytes 4194304 | tf_op jit(solution)/shard_map/core/pallas_call | solution.py:250
  56.3 0.0 copy-start.4
  56.3 1.0 %copy-done.4 = bf16[32,128,128]{2,1,0:T(8,128)(2,1)} copy-done((bf16[32,128,128]{2,1,0:T(8,128)(2,1)}, bf16[32,128,128]{2,1,0:T(8,128)(2,1)S(1)}, u32[]{:S(2)}) %copy-start.4) | copy-done | bytes 1048600
  57.3 0.0 copy-start.1
  57.3 0.0 copy-start.2
  57.3 6.4 %all-to-all-start.1 = ((bf16[32,128,128]{2,1,0:T(8,128)(2,1)}), bf16[32,128,128]{2,1,0:T(8,128)(2,1)S(1)}, u32[]{:S(2)}, u32[]{:S(2)}) async-start(bf16[32,128,128]{2,1,0:T(8,128)(2,1)} %copy-done.4), calls=%async_computation.1 | async-start | bytes 2097152 | tf_op jit(solution)/shard_map/all_to_all | solution.py:364
  63.7 0.4 collective-permute-start.4
  64.1 5.2 %collective-permute-done.4 = f32[4,64,128]{2,1,0:T(8,128)S(1)} collective-permute-done((f32[4,64,128]{2,1,0:T(8,128)S(1)}, f32[4,64,128]{2,1,0:T(8,128)S(1)}, u32[]{:S(2)}, u32[]{:S(2)}) %collective-permute-start.4) | collective-permute-done | bytes 131104 | tf_op jit(solution)/shard_map/ppermute | solution.py:328
  69.4 2.9 %collective-permute-start.5 = (f32[2,64,128]{2,1,0:T(8,128)S(1)}, f32[2,64,128]{2,1,0:T(8,128)S(1)}, u32[]{:S(2)}, u32[]{:S(2)}) collective-permute-start(f32[2,64,128]{2,1,0:T(8,128)S(1)} %slice.17), channel_id=1, source_target_pairs={{0,8},{4,12},{8,0},{12,4},{16,24},{20,28},{24,16},{28,20},{1,9},{5... | collective-permute-start | bytes 196616 | tf_op jit(solution)/shard_map/ppermute | solution.py:328
  72.3 2.8 %collective-permute-done.5 = f32[2,64,128]{2,1,0:T(8,128)S(1)} collective-permute-done((f32[2,64,128]{2,1,0:T(8,128)S(1)}, f32[2,64,128]{2,1,0:T(8,128)S(1)}, u32[]{:S(2)}, u32[]{:S(2)}) %collective-permute-start.5) | collective-permute-done | bytes 65568 | tf_op jit(solution)/shard_map/ppermute | solution.py:328
  75.1 5.7 %collective-permute-start.6 = (f32[64,128]{1,0:T(8,128)S(1)}, f32[64,128]{1,0:T(8,128)S(1)}, u32[]{:S(2)}, u32[]{:S(2)}) collective-permute-start(f32[64,128]{1,0:T(8,128)S(1)} %slice_bitcast_fusion), channel_id=1, source_target_pairs={{0,16},{4,20},{8,24},{12,28},{16,0},{20,4},{24,8},{28,12},{1,17},{... | collective-permute-start | bytes 98312 | tf_op jit(solution)/shard_map/ppermute | solution.py:328
  80.8 2.3 %collective-permute-done.6 = f32[64,128]{1,0:T(8,128)S(1)} collective-permute-done((f32[64,128]{1,0:T(8,128)S(1)}, f32[64,128]{1,0:T(8,128)S(1)}, u32[]{:S(2)}, u32[]{:S(2)}) %collective-permute-start.6) | collective-permute-done | bytes 32800 | tf_op jit(solution)/shard_map/ppermute | solution.py:328
  83.2 0.0 all-to-all-done.1.conv
  83.2 3.6 %collective-permute-start.7 = (f32[64,128]{1,0:T(8,128)S(1)}, f32[64,128]{1,0:T(8,128)S(1)}, u32[]{:S(2)}, u32[]{:S(2)}) collective-permute-start(f32[64,128]{1,0:T(8,128)S(1)} %fusion), channel_id=1, source_target_pairs={{116,0},{20,4},{84,8},{52,12},{180,16},{212,20},{148,24},{244,28},... | collective-permute-start | bytes 98312 | tf_op jit(solution)/shard_map/ppermute | solution.py:350
  86.8 0.0 copy-done.1
  86.8 0.0 copy-done.2
  86.8 1.6 %unpack.1 = (bf16[128,4096]{1,0:T(8,128)(2,1)}, bf16[128,4096]{1,0:T(8,128)(2,1)}) custom-call(bf16[32,128,128]{2,1,0:T(8,128)(2,1)S(1)} %all-to-all-done.1.conv, bf16[128,4096]{1,0:T(8,128)(2,1)S(1)} %bitcast.21, bf16[128,4096]{1,0:T(8,128)(2,1)S(1)} %bitcast.23), custom_call_target="tpu_custom_call" | custom-call | flops 2097152 | bytes 5242880 | tf_op jit(solution)/shard_map/unpack/pallas_call | solution.py:297
  88.4 4.4 %collective-permute-done.7 = f32[64,128]{1,0:T(8,128)S(1)} collective-permute-done((f32[64,128]{1,0:T(8,128)S(1)}, f32[64,128]{1,0:T(8,128)S(1)}, u32[]{:S(2)}, u32[]{:S(2)}) %collective-permute-start.7) | collective-permute-done | bytes 32800 | tf_op jit(solution)/shard_map/ppermute | solution.py:350
  92.8 0.6 copy.14
  (9 shorter events, 0.1 us)
Async XLA Ops:
  1.4 12.8 %collective-permute-start = (bf16[1,64,128]{2,1,0:T(8,128)(2,1)S(1)}, bf16[1,64,128]{2,1,0:T(8,128)(2,1)S(1)}, u32[]{:S(2)}, u32[]{:S(2)}) collective-permute-start(bf16[1,64,128]{2,1,0:T(8,128)(2,1)S(1)} %bitcast_convert_fusion), channel_id=1, source_target_pairs={{0,116},{4,20},{8,84},{12,52},{16,180},{20,212},{24,148},{28,244},... | collective-permute-start | bytes 49160 | tf_op jit(solution)/shard_map/ppermute | solution.py:333
  14.2 4.4 %copy-start = (bf16[1,128,4096]{2,1,0:T(8,128)(2,1)S(1)}, bf16[1,128,4096]{2,1,0:T(8,128)(2,1)}, u32[]{:S(2)}) copy-start(bf16[1,128,4096]{2,1,0:T(8,128)(2,1)} %param.11) | copy-start | bytes 3145732
  14.2 31.1 %all-to-all-start = ((bf16[32,2,128,128]{3,2,1,0:T(8,128)(2,1)}), bf16[32,2,128,128]{3,2,1,0:T(8,128)(2,1)S(1)}, u32[]{:S(2)}, u32[]{:S(2)}) async-start(bf16[32,2,128,128]{3,2,1,0:T(8,128)(2,1)} %pack.1), calls=%async_computation | async-start | bytes 4194304 | tf_op jit(solution)/shard_map/all_to_all | solution.py:357
  18.6 1.2 %copy-start.3 = (bf16[1,128,4096]{2,1,0:T(8,128)(2,1)S(1)}, bf16[1,128,4096]{2,1,0:T(8,128)(2,1)}, u32[]{:S(2)}) copy-start(bf16[1,128,4096]{2,1,0:T(8,128)(2,1)} %param.10) | copy-start | bytes 3145732
  20.9 7.6 %collective-permute-start.1 = (bf16[1,64,128]{2,1,0:T(8,128)(2,1)S(1)}, bf16[1,64,128]{2,1,0:T(8,128)(2,1)S(1)}, u32[]{:S(2)}, u32[]{:S(2)}) collective-permute-start(bf16[1,64,128]{2,1,0:T(8,128)(2,1)S(1)} %collective-permute-done), channel_id=1, source_target_pairs={{0,16},{4,20},{8,24},{12,28},{16,0},{20,4},{24,8},{28,12},{1,17},{... | collective-permute-start | bytes 49160 | tf_op jit(solution)/shard_map/ppermute | solution.py:328
  28.5 4.8 %collective-permute-start.2 = (bf16[2,64,128]{2,1,0:T(8,128)(2,1)S(1)}, bf16[2,64,128]{2,1,0:T(8,128)(2,1)S(1)}, u32[]{:S(2)}, u32[]{:S(2)}) collective-permute-start(bf16[2,64,128]{2,1,0:T(8,128)(2,1)S(1)} %pad_maximum_fusion), channel_id=1, source_target_pairs={{0,8},{4,12},{8,0},{12,4},{16,24},{20,28},{24,16},{28,20},{1,9},{5... | collective-permute-start | bytes 98312 | tf_op jit(solution)/shard_map/ppermute | solution.py:328
  33.4 4.3 %collective-permute-start.3 = (bf16[4,64,128]{2,1,0:T(8,128)(2,1)S(1)}, bf16[4,64,128]{2,1,0:T(8,128)(2,1)S(1)}, u32[]{:S(2)}, u32[]{:S(2)}) collective-permute-start(bf16[4,64,128]{2,1,0:T(8,128)(2,1)S(1)} %constant_dynamic-update-slice_fusion.near), channel_id=1, source_target_pairs={{0,4},{4,0},{8,12},{12,8},{16,20},{20,16},{24,28},{28,24},{1,5},{5... | collective-permute-start | bytes 196616 | tf_op jit(solution)/shard_map/ppermute | solution.py:328
  37.6 1.0 %copy-start.5 = (f32[4,32,1024]{2,1,0:T(8,128)S(1)}, f32[4,32,1024]{2,1,0:T(8,128)}, u32[]{:S(2)}) copy-start(f32[4,32,1024]{2,1,0:T(8,128)} %constant.12.clone.seed) | copy-start | bytes 1572868
  40.8 1.0 %copy-start.6 = (f32[2,1024,128]{2,1,0:T(8,128)}, f32[2,1024,128]{2,1,0:T(8,128)S(1)}, u32[]{:S(2)}) copy-start(f32[2,1024,128]{2,1,0:T(8,128)S(1)} %get-tuple-element.23.filt) | copy-start | bytes 3145732
  45.3 1.2 %copy-start.7 = (f32[2,1024,128]{2,1,0:T(8,128)S(1)}, f32[2,1024,128]{2,1,0:T(8,128)}, u32[]{:S(2)}) copy-start(f32[2,1024,128]{2,1,0:T(8,128)} %copy-done.6) | copy-start | bytes 3145732
  56.3 1.0 %copy-start.4 = (bf16[32,128,128]{2,1,0:T(8,128)(2,1)}, bf16[32,128,128]{2,1,0:T(8,128)(2,1)S(1)}, u32[]{:S(2)}) copy-start(bf16[32,128,128]{2,1,0:T(8,128)(2,1)S(1)} %get-tuple-element.27) | copy-start | bytes 3145732
  57.3 29.5 %copy-start.1 = (bf16[1,128,4096]{2,1,0:T(8,128)(2,1)S(1)}, bf16[1,128,4096]{2,1,0:T(8,128)(2,1)}, u32[]{:S(2)}) copy-start(bf16[1,128,4096]{2,1,0:T(8,128)(2,1)} %param.8) | copy-start | bytes 3145732
  57.3 29.5 %copy-start.2 = (bf16[1,128,4096]{2,1,0:T(8,128)(2,1)S(1)}, bf16[1,128,4096]{2,1,0:T(8,128)(2,1)}, u32[]{:S(2)}) copy-start(bf16[1,128,4096]{2,1,0:T(8,128)(2,1)} %param.9) | copy-start | bytes 3145732
  57.3 25.9 %all-to-all-start.1 = ((bf16[32,128,128]{2,1,0:T(8,128)(2,1)}), bf16[32,128,128]{2,1,0:T(8,128)(2,1)S(1)}, u32[]{:S(2)}, u32[]{:S(2)}) async-start(bf16[32,128,128]{2,1,0:T(8,128)(2,1)} %copy-done.4), calls=%async_computation.1 | async-start | bytes 2097152 | tf_op jit(solution)/shard_map/all_to_all | solution.py:364
  63.7 5.6 %collective-permute-start.4 = (f32[4,64,128]{2,1,0:T(8,128)S(1)}, f32[4,64,128]{2,1,0:T(8,128)S(1)}, u32[]{:S(2)}, u32[]{:S(2)}) collective-permute-start(f32[4,64,128]{2,1,0:T(8,128)S(1)} %get-tuple-element.26), channel_id=1, source_target_pairs={{0,4},{4,0},{8,12},{12,8},{16,20},{20,16},{24,28},{28,24},{1,5},{5... | collective-permute-start | bytes 393224 | tf_op jit(solution)/shard_map/ppermute | solution.py:328
  69.4 5.7 %collective-permute-start.5 = (f32[2,64,128]{2,1,0:T(8,128)S(1)}, f32[2,64,128]{2,1,0:T(8,128)S(1)}, u32[]{:S(2)}, u32[]{:S(2)}) collective-permute-start(f32[2,64,128]{2,1,0:T(8,128)S(1)} %slice.17), channel_id=1, source_target_pairs={{0,8},{4,12},{8,0},{12,4},{16,24},{20,28},{24,16},{28,20},{1,9},{5... | collective-permute-start | bytes 196616 | tf_op jit(solution)/shard_map/ppermute | solution.py:328
  75.1 8.0 %collective-permute-start.6 = (f32[64,128]{1,0:T(8,128)S(1)}, f32[64,128]{1,0:T(8,128)S(1)}, u32[]{:S(2)}, u32[]{:S(2)}) collective-permute-start(f32[64,128]{1,0:T(8,128)S(1)} %slice_bitcast_fusion), channel_id=1, source_target_pairs={{0,16},{4,20},{8,24},{12,28},{16,0},{20,4},{24,8},{28,12},{1,17},{... | collective-permute-start | bytes 98312 | tf_op jit(solution)/shard_map/ppermute | solution.py:328
  83.2 9.6 %collective-permute-start.7 = (f32[64,128]{1,0:T(8,128)S(1)}, f32[64,128]{1,0:T(8,128)S(1)}, u32[]{:S(2)}, u32[]{:S(2)}) collective-permute-start(f32[64,128]{1,0:T(8,128)S(1)} %fusion), channel_id=1, source_target_pairs={{116,0},{20,4},{84,8},{52,12},{180,16},{212,20},{148,24},{244,28},... | collective-permute-start | bytes 98312 | tf_op jit(solution)/shard_map/ppermute | solution.py:350

commit v3 on v2

--- a/solution.py
+++ b/solution.py
@@ -1,5 +1,3 @@
-import functools
-
 import jax
 import jax.numpy as jnp
 import numpy as np
@@ -23,16 +21,23 @@
 MIB = 1024 * 1024
 F32 = jnp.float32
 BF16 = jnp.bfloat16
-OWNER = (3, 0, 2, 1, 5, 6, 4, 7)
-LAG_AT = (5, 7, 6, 4, 2, 0, 1, 3)
-
-
-def chunk_of(block):
-    return 4 * OWNER[block // 4] + block % 4
-
-
-def slot_of(z, lag_block):
-    n = z ^ LAG_AT[lag_block]
+
+
+def ring(a, b, size):
+    return min((a - b) % size, (b - a) % size)
+
+
+def lag_homes():
+    homes = []
+    for n in range(8):
+        far = sorted(range(8), key=lambda l: -(2 * (l // 4 != n // 4) + ring(l % 4, n % 4, 4)))
+        near = sorted(range(8), key=lambda z: ring(z, n, 8))
+        homes.append([near[far.index(l)] for l in range(8)])
+    return homes
+
+
+def slot_of(z, home):
+    n = z ^ home
     return (n & 1) * 4 + (n & 2) + (n >> 2)
 
 
@@ -95,7 +100,7 @@
             copy.wait()
         for t in range(j * tiles, (j + 1) * tiles):
             ahead, behind = lanes_of(t), lanes_of(GROUPS - 1 - t)
-            even, odd = chunk_of(2 * t), chunk_of(2 * t + 1)
+            even, odd = 2 * t, 2 * t + 1
             for kind in range(2):
                 a, b = 2 * kind, 2 * kind + 1
                 f = buf[a, :, ahead].astype(F32) * buf[b, :, ahead].astype(F32)
@@ -136,7 +141,7 @@
     )(q, g, k, v)
 
 
-def filter_kernel(place_ref, seed, near, far, filt, seed_out, rows_in, cos, sin, turn):
+def filter_kernel(place_ref, seed, near, far, filt_hbm, seed_out, filt, rows_in, cos, sin, turn, sem):
     odd, z = place_ref[0], place_ref[1]
     step = 256
     row = lax.broadcasted_iota(jnp.int32, (LANES, LANES // 2), 0)
@@ -145,8 +150,8 @@
     behind = jnp.where(odd == 0, LANES, LANES // 2) - 1 - row
     spread = jnp.where((col == ahead) | (col == behind), 1.0, 0.0).astype(BF16)
     for block in range(SEQ // BLOCK):
-        slot = slot_of(z, block)
-        lags = jnp.where(slot < 4, near[slot % 4], far[slot % 4])
+        slot = slot_of(z, place_ref[2 + block])
+        lags = jnp.where(slot < 4, near[slot % 4], far[slot % 4]).astype(BF16)
         rows_in[:, lanes_of(block)] = dot(spread, lags).astype(BF16)
     sign = strand_sign(odd)
     for n in range(SEQ // step):
@@ -156,7 +161,10 @@
         tc, ts = turn[0, at, :], turn[1, at, :]
         filt[0, at, :] = fc * tc + fs * ts
         filt[1, at, :] = (fc * ts - fs * tc) * sign
+    copy = pltpu.make_async_copy(filt, filt_hbm, sem.at[0])
+    copy.start()
     seed_out[...] = seed[...]
+    copy.wait()
 
 
 def filter_spectrum(place, near, far):
@@ -164,16 +172,15 @@
     return pl.pallas_call(
         filter_kernel,
         in_specs=[SMEM, VMEM, VMEM, VMEM],
-        out_specs=(VMEM, VMEM),
-        out_shape=(
-            jax.ShapeDtypeStruct((2, SEQ, LANES), F32),
-            jax.ShapeDtypeStruct(seed.shape, F32),
-        ),
+        out_specs=(HBM, VMEM),
+        out_shape=(pltpu.HBM((2, SEQ, LANES), F32), jax.ShapeDtypeStruct(seed.shape, F32)),
         scratch_shapes=[
+            pltpu.VMEM((2, SEQ, LANES), F32),
             pltpu.VMEM((LANES, SEQ), BF16),
             pltpu.VMEM((SEQ, SEQ), BF16),
             pltpu.VMEM((SEQ, SEQ), BF16),
             pltpu.VMEM((2, SEQ, LANES), F32),
+            pltpu.SemaphoreType.DMA((1,)),
         ],
         compiler_params=SMALL,
         cost_estimate=pl.CostEstimate(flops=1, bytes_accessed=1, transcendentals=0),
@@ -186,11 +193,13 @@
     return jnp.where((lane < LANES // 2) == (odd == 0), -1.0, 1.0).astype(F32)
 
 
-def core_kernel(place_ref, x, filt, seed, conv_hbm, keep, give, cos, sin, turn, uv, prod, conv, folded, sem_out):
+def core_kernel(place_ref, x, filt_hbm, seed, keep, give, uv, cos, sin, filt, turn, prod, folded, sem_in):
     odd, z = place_ref[0], place_ref[1]
     step = 256
     steps = SEQ // step
     sign = strand_sign(odd)
+    filt_copy = pltpu.make_async_copy(filt_hbm, filt, sem_in.at[0])
+    filt_copy.start()
     def columns(kind):
         tiles = [[x[SPLIT * i + q, kind] for i in range(SEQ // BLOCK)] for q in range(SPLIT)]
         return jnp.concatenate([jnp.concatenate(tile, axis=0) for tile in tiles], axis=1)
@@ -203,9 +212,11 @@
         at = pl.ds(n * step, step)
         c_rows, s_rows = cos[at, :], sin[at, :]
         tc, ts = turn[0, at, :], turn[1, at, :]
-        re, im = filt[0, at, :], filt[1, at, :]
         grad = columns(0)
         cg, sg = dot(c_rows, grad), dot(s_rows, grad)
+        if n == 0:
+            filt_copy.wait()
+        re, im = filt[0, at, :], filt[1, at, :]
         for q in range(SPLIT):
             a, b = cg[:, lanes_of(q)], sg[:, lanes_of(q)]
             uv[0, at, lanes_of(q)] = (a * re + b * im).astype(BF16)
@@ -221,13 +232,19 @@
     row = lax.broadcasted_iota(jnp.int32, (LANES // 2, LANES), 0)
     col = lax.broadcasted_iota(jnp.int32, (LANES // 2, LANES), 1)
     row = jnp.where(odd == 0, row, LANES // 2 - 1 - row)
-    fold = jnp.where((col == row) | (col == LANES - 1 - row), 1.0, 0.0).astype(F32)
-    total = jnp.dot(fold, lags * (1.0 / SEQ), precision=lax.Precision.HIGHEST, preferred_element_type=F32)
+    fold = jnp.where((col == row) | (col == LANES - 1 - row), 1.0 / SEQ, 0.0).astype(BF16)
+    upper = lags.astype(BF16)
+    total = dot(fold, upper) + dot(fold, (lags - upper.astype(F32)).astype(BF16))
     for block in range(SEQ // BLOCK):
-        folded[slot_of(z, block)] = total[:, lanes_of(block)]
+        home = place_ref[2 + block]
+        folded[((z ^ home) & 1) * 4 + (home & 2) + (home >> 2)] = total[:, lanes_of(block)]
     keep[...] = folded[:4]
-    give[...] = folded[4:]
-
+    give[...] = folded[4:].astype(BF16)
+
+
+def back_kernel(uv, cos, sin, conv_hbm, conv, sem_out):
+    step = 256
+    steps = SEQ // step
     leaving = []
     size = SPLIT * (step // BLOCK)
     for n in range(steps):
@@ -246,37 +263,55 @@
 
 
 def core(place, x, filt, seed):
-    part = jax.ShapeDtypeStruct((4, LANES // 2, BLOCK), F32)
+    table = pltpu.VMEM((SEQ, SEQ), BF16)
     return pl.pallas_call(
         core_kernel,
-        in_specs=[SMEM, VMEM, VMEM, VMEM],
-        out_specs=(HBM, VMEM, VMEM),
-        out_shape=(jax.ShapeDtypeStruct((GROUPS, BLOCK, LANES), BF16), part, part),
+        in_specs=[SMEM, VMEM, HBM, VMEM],
+        out_specs=(VMEM,) * 5,
+        out_shape=(
+            jax.ShapeDtypeStruct((4, LANES // 2, BLOCK), F32),
+            jax.ShapeDtypeStruct((4, LANES // 2, BLOCK), BF16),
+            pltpu.VMEM((2, SEQ, WIDTH), BF16),
+            table,
+            table,
+        ),
         scratch_shapes=[
-            pltpu.VMEM((SEQ, SEQ), BF16),
-            pltpu.VMEM((SEQ, SEQ), BF16),
             pltpu.VMEM((2, SEQ, LANES), F32),
-            pltpu.VMEM((2, SEQ, WIDTH), BF16),
+            pltpu.VMEM((2, SEQ, LANES), F32),
             pltpu.VMEM((2, SEQ, LANES), BF16),
-            pltpu.VMEM((GROUPS, BLOCK, LANES), BF16),
             pltpu.VMEM((8, LANES // 2, BLOCK), F32),
-            pltpu.SemaphoreType.DMA((4,)),
+            pltpu.SemaphoreType.DMA((1,)),
         ],
         compiler_params=SMALL,
-        cost_estimate=pl.CostEstimate(flops=7000 * MIB, bytes_accessed=4 * MIB, transcendentals=0),
+        cost_estimate=pl.CostEstimate(flops=5000 * MIB, bytes_accessed=4 * MIB, transcendentals=0),
         name="core",
-    )(place, x, filt, seed)
-
-
-def unpack_kernel(conv, k_in, v_in, key_hbm, value_hbm, key, value, sem_out):
+    )(place, x, pltpu.with_memory_space_constraint(filt, pltpu.HBM), seed)
+
+
+def back(uv, cos, sin):
+    return pl.pallas_call(
+        back_kernel,
+        in_specs=[VMEM] * 3,
+        out_specs=HBM,
+        out_shape=pltpu.HBM((GROUPS, BLOCK, LANES), BF16),
+        scratch_shapes=[pltpu.VMEM((GROUPS, BLOCK, LANES), BF16), pltpu.SemaphoreType.DMA((4,))],
+        compiler_params=SMALL,
+        cost_estimate=pl.CostEstimate(flops=2100 * MIB, bytes_accessed=MIB, transcendentals=0),
+        name="back",
+    )(uv, cos, sin)
+
+
+def unpack_kernel(conv, k_in, v_in, lags, key_hbm, value_hbm, lags_hbm, key, value, sem_out, sem_lags):
     tiles = GROUPS // 2 // CUTS
     width = tiles * LANES
+    lags_copy = pltpu.make_async_copy(lags, lags_hbm, sem_lags.at[0])
+    lags_copy.start()
     low = lax.broadcasted_iota(jnp.int32, (BLOCK, LANES), 1) < LANES // 2
     leaving = []
     for j in range(CUTS):
         for t in range(j * tiles, (j + 1) * tiles):
-            even = conv[chunk_of(2 * t)].astype(F32)
-            odd = conv[chunk_of(2 * t + 1)].astype(F32)
+            even = conv[2 * t].astype(F32)
+            odd = conv[2 * t + 1].astype(F32)
             ahead, behind = jnp.where(low, even, odd), jnp.where(low, odd, even)
             for cols, grad in ((lanes_of(t), ahead), (lanes_of(GROUPS - 1 - t), behind)):
                 key[:, cols] = (grad * v_in[:, cols].astype(F32)).astype(BF16)
@@ -287,23 +322,24 @@
                 copy = pltpu.make_async_copy(src.at[:, cols], dst.at[:, cols], sem_out.at[j, s, m])
                 copy.start()
                 leaving.append(copy)
+    lags_copy.wait()
     for copy in leaving:
         copy.wait()
 
 
-def unpack(conv, k, v):
+def unpack(conv, k, v, lags):
     shape = jax.ShapeDtypeStruct(k.shape, BF16)
     whole = pltpu.VMEM(k.shape, BF16)
     return pl.pallas_call(
         unpack_kernel,
-        in_specs=[VMEM] * 3,
-        out_specs=(ANY, ANY),
-        out_shape=(shape, shape),
-        scratch_shapes=[whole, whole, pltpu.SemaphoreType.DMA((CUTS, 2, 2))],
+        in_specs=[VMEM] * 4,
+        out_specs=(ANY,) * 3,
+        out_shape=(shape, shape, jax.ShapeDtypeStruct(lags.shape, F32)),
+        scratch_shapes=[whole, whole, pltpu.SemaphoreType.DMA((CUTS, 2, 2)), pltpu.SemaphoreType.DMA((1,))],
         compiler_params=SMALL,
         cost_estimate=pl.CostEstimate(flops=2 * MIB, bytes_accessed=5 * MIB, transcendentals=0),
         name="unpack",
-    )(conv, k, v)
+    )(conv, k, v, lags)
 
 
 def times_kernel(a, b, out):
@@ -329,8 +365,9 @@
 
 
 def sent_out(filters):
-    route = [(8 * l + n, 8 * OWNER[n] + LAG_AT[l]) for l in range(8) for n in range(8)]
-    return lax.ppermute(filters[None], CTX_Z, route).astype(BF16)
+    homes = lag_homes()
+    route = [(8 * l + n, 8 * n + homes[n][l]) for l in range(8) for n in range(8)]
+    return lax.ppermute(filters, CTX_Z, route)[None]
 
 
 def gathered_over_z(near):
@@ -339,19 +376,22 @@
     return near, swap_z(near, 0)
 
 
-def summed_over_z(keep, give):
-    keep = keep + swap_z(give, 0)
-    keep = keep[:2] + swap_z(keep[2:], 1)
-    return keep[0] + swap_z(keep[1], 2)
+def summed_over_z(lags, bit):
+    low, high = jnp.split(lags, 2, axis=0)
+    first = (lax.axis_index("z") >> bit) % 2 == 0
+    given = jnp.where(first, high, low).astype(BF16)
+    return jnp.where(first, low, high) + swap_z(given, bit).astype(F32)
 
 
 def sent_home(lags):
-    route = [(8 * OWNER[n] + LAG_AT[l], 8 * l + n) for l in range(8) for n in range(8)]
+    homes = lag_homes()
+    route = [(8 * n + homes[n][l], 8 * l + n) for l in range(8) for n in range(8)]
     return lax.ppermute(lags, CTX_Z, route)
 
 
 def local(query_gate, key_gate, value_in, conv_out, out_grad, filters):
-    place = jnp.stack([lax.axis_index("core"), lax.axis_index("z")]).astype(jnp.int32)
+    home = jnp.asarray(lag_homes(), jnp.int32)[lax.axis_index(CTX)]
+    place = jnp.concatenate([jnp.stack([lax.axis_index("core"), lax.axis_index("z")]).astype(jnp.int32), home])
     q, k, v, g = query_gate[0], key_gate[0], value_in[0], out_grad[0]
     x, near = lax.optimization_barrier((pack(q, g, k, v), sent_out(filters)))
     x = lax.all_to_all(x, PLANE, split_axis=0, concat_axis=0, tiled=True)
@@ -360,11 +400,11 @@
     filt, seed = filter_spectrum(place, near, far)
     filt, seed, query_grad = lax.optimization_barrier((filt, seed, times(g, conv_out[0])[None]))
 
-    conv, keep, give = core(place, x, filt, seed)
-    conv = lax.all_to_all(conv, PLANE, split_axis=0, concat_axis=0, tiled=True)
-    lags, conv = lax.optimization_barrier((summed_over_z(keep, give), conv))
-    filter_grad = sent_home(lags)
-    key_grad, value_grad = unpack(conv, k, v)
+    keep, give, uv, cos, sin = core(place, x, filt, seed)
+    lags = keep + swap_z(give, 0).astype(F32)
+    conv = lax.all_to_all(back(uv, cos, sin), PLANE, split_axis=0, concat_axis=0, tiled=True)
+    lags = summed_over_z(summed_over_z(lags, 1), 2)[0]
+    key_grad, value_grad, filter_grad = unpack(conv, k, v, sent_home(lags))
     return query_grad, key_grad[None], value_grad[None], filter_grad
 
 

time: 93.9 us -> 88.1 us (0.938)
  the two profiles are of different devices: /device:TPU:2 before, /device:TPU:30 now
where the time goes in v3:
time: 88.1 us; the launch traced here: 87.6 us
  starting transfers between devices  43.6 us (49%)
  Pallas kernels  20.1 us (23%)
  waiting for transfers between devices  19.9 us (23%)
  local copies, waits for them, and re-layouts  2.99 us (3%)
  between operations  0.93 us (1%)
    ppermute x6, starting transfers between devices, swap_z(): return lax.ppermute(block, 'z', [(i, i ^ 1 << bit) for i in range(8)])  17.3 us
    ppermute x6, waiting for transfers between devices, swap_z(): return lax.ppermute(block, 'z', [(i, i ^ 1 << bit) for i in range(8)])  12.3 us
    pallas_call x1, Pallas kernels, core(): pl.pallas_call(core_kernel, in_specs=[SMEM, VMEM, HBM, VMEM], out_specs=(...  7.71 us
    all_to_all x1, starting transfers between devices, local(): lax.all_to_all(back(uv, cos, sin), PLANE, split_axis=0, concat_axis=0, ti...  7.31 us
    all_to_all x1, starting transfers between devices, local(): x = lax.all_to_all(x, PLANE, split_axis=0, concat_axis=0, tiled=True)  7.1 us
    ppermute x1, starting transfers between devices, sent_out(): return lax.ppermute(filters, CTX_Z, route)[None]  6.43 us
    ppermute x1, starting transfers between devices, sent_home(): return lax.ppermute(lags, CTX_Z, route)  5.44 us
    ppermute x1, waiting for transfers between devices, sent_home(): return lax.ppermute(lags, CTX_Z, route)  4.61 us
  transfers between devices with their start and end apart: 10, of which 7 were waited for; matrix products, arithmetic and copies ran while one was open for 1% of the time, Pallas kernels for 12%

profile of v3, /device:TPU:30, one launch (start us, length us, event | category | flops | bytes accessed | tf_op | source)
XLA Modules:
  0.0 87.6 jit_solution(4742101683104733907)
XLA Ops:
  0.6 6.4 %collective-permute-start = (f32[64,128]{1,0:T(8,128)}, f32[64,128]{1,0:T(8,128)S(1)}, u32[]{:S(2)}, u32[]{:S(2)}) collective-permute-start(f32[64,128]{1,0:T(8,128)} %param.13), channel_id=1, source_target_pairs={{0,16},{4,48},{8,64},{12,96},{16,136},{20,176},{24,216},{28,224},{... | collective-permute-start | bytes 98312 | tf_op jit(solution)/shard_map/ppermute | solution.py:370
  7.1 3.6 %pack.1 = bf16[32,2,128,128]{3,2,1,0:T(8,128)(2,1)} custom-call(bf16[128,4096]{1,0:T(8,128)(2,1)} %bitcast.23, bf16[128,4096]{1,0:T(8,128)(2,1)} %bitcast.15, bf16[128,4096]{1,0:T(8,128)(2,1)} %bitcast.17, bf16[128,4096]{1,0:T(8,128)(2,1)} %bitcast.19), custom_call_target="tpu_custom_call" | custom-call | flops 2097152 | bytes 6291456 | tf_op jit(solution)/shard_map/pack/pallas_call | solution.py:127
  10.7 0.0 collective-permute-done
  10.7 0.0 copy-start
  10.7 7.1 %all-to-all-start = ((bf16[32,2,128,128]{3,2,1,0:T(8,128)(2,1)}), bf16[32,2,128,128]{3,2,1,0:T(8,128)(2,1)S(1)}, u32[]{:S(2)}, u32[]{:S(2)}) async-start(bf16[32,2,128,128]{3,2,1,0:T(8,128)(2,1)} %pack.1), calls=%async_computation | async-start | bytes 4194304 | tf_op jit(solution)/shard_map/all_to_all | solution.py:397
  17.8 5.3 %collective-permute-start.1 = (f32[1,64,128]{2,1,0:T(8,128)S(1)}, f32[1,64,128]{2,1,0:T(8,128)S(1)}, u32[]{:S(2)}, u32[]{:S(2)}) collective-permute-start(f32[1,64,128]{2,1,0:T(8,128)S(1)} %bitcast.24), channel_id=1, source_target_pairs={{0,16},{4,20},{8,24},{12,28},{16,0},{20,4},{24,8},{28,12},{1,17},{... | collective-permute-start | bytes 98312 | tf_op jit(solution)/shard_map/ppermute | solution.py:364
  23.1 2.6 %collective-permute-done.1 = f32[1,64,128]{2,1,0:T(8,128)S(1)} collective-permute-done((f32[1,64,128]{2,1,0:T(8,128)S(1)}, f32[1,64,128]{2,1,0:T(8,128)S(1)}, u32[]{:S(2)}, u32[]{:S(2)}) %collective-permute-start.1) | collective-permute-done | bytes 32800 | tf_op jit(solution)/shard_map/ppermute | solution.py:364
  25.7 2.7 %collective-permute-start.2 = (f32[2,64,128]{2,1,0:T(8,128)S(1)}, f32[2,64,128]{2,1,0:T(8,128)S(1)}, u32[]{:S(2)}, u32[]{:S(2)}) collective-permute-start(f32[2,64,128]{2,1,0:T(8,128)S(1)} %pad_maximum_fusion), channel_id=1, source_target_pairs={{0,8},{4,12},{8,0},{12,4},{16,24},{20,28},{24,16},{28,20},{1,9},{5... | collective-permute-start | bytes 196616 | tf_op jit(solution)/shard_map/ppermute | solution.py:364
  28.5 3.1 %collective-permute-done.2 = f32[2,64,128]{2,1,0:T(8,128)S(1)} collective-permute-done((f32[2,64,128]{2,1,0:T(8,128)S(1)}, f32[2,64,128]{2,1,0:T(8,128)S(1)}, u32[]{:S(2)}, u32[]{:S(2)}) %collective-permute-start.2) | collective-permute-done | bytes 65568 | tf_op jit(solution)/shard_map/ppermute | solution.py:364
  31.6 0.1 collective-permute-start.3
  31.7 0.7 dynamic-slice_bitcast_fusion
  32.4 0.0 copy-done
  32.4 0.0 copy-start.3
  32.4 1.2 %copy-done.3 = bf16[1,128,4096]{2,1,0:T(8,128)(2,1)S(1)} copy-done((bf16[1,128,4096]{2,1,0:T(8,128)(2,1)S(1)}, bf16[1,128,4096]{2,1,0:T(8,128)(2,1)}, u32[]{:S(2)}) %copy-start.3) | copy-done | bytes 1048600
  33.7 1.1 %times.1 = bf16[128,4096]{1,0:T(8,128)(2,1)} custom-call(bf16[128,4096]{1,0:T(8,128)(2,1)S(1)} %bitcast.16, bf16[128,4096]{1,0:T(8,128)(2,1)S(1)} %bitcast.21), custom_call_target="tpu_custom_call" | custom-call | flops 1 | bytes 1 | tf_op jit(solution)/shard_map/times/pallas_call | solution.py:351
  34.7 0.1 pad_add_fusion.place_ref
  34.8 1.8 %collective-permute-done.3.far = f32[4,64,128]{2,1,0:T(8,128)S(1)} collective-permute-done((f32[4,64,128]{2,1,0:T(8,128)S(1)}, f32[4,64,128]{2,1,0:T(8,128)S(1)}, u32[]{:S(2)}, u32[]{:S(2)}) %collective-permute-start.3) | collective-permute-done | bytes 131104 | tf_op jit(solution)/shard_map/ppermute | solution.py:364
  36.6 0.0 copy-start.4
  36.6 1.0 %copy-done.4 = f32[4,32,1024]{2,1,0:T(8,128)S(1)} copy-done((f32[4,32,1024]{2,1,0:T(8,128)S(1)}, f32[4,32,1024]{2,1,0:T(8,128)}, u32[]{:S(2)}) %copy-start.4) | copy-done | bytes 524312
  37.6 3.0 %filter_spectrum.1 = (f32[2,1024,128]{2,1,0:T(8,128)}, f32[4,32,1024]{2,1,0:T(8,128)S(1)}) custom-call(s32[10]{0:T(128)S(1)} %pad_add_fusion.place_ref, f32[4,32,1024]{2,1,0:T(8,128)S(1)} %copy-done.4, f32[4,64,128]{2,1,0:T(8,128)S(1)} %constant_dynamic-update-slice_fusion.near, f32[4,64,128]{2,1,0:T(8,128)S(1)} %collective-permute-done.3.far), custom_call_target="tpu_custom_call" | custom-call | flops 1 | bytes 1 | tf_op jit(solution)/shard_map/filter_spectrum/pallas_call | solution.py:172
  40.7 3.0 %all-to-all-done.x = bf16[32,2,128,128]{3,2,1,0:T(8,128)(2,1)S(1)} async-done(((bf16[32,2,128,128]{3,2,1,0:T(8,128)(2,1)}), bf16[32,2,128,128]{3,2,1,0:T(8,128)(2,1)S(1)}, u32[]{:S(2)}, u32[]{:S(2)}) %all-to-all-start) | async-done | bytes 2097184 | tf_op jit(solution)/shard_map/all_to_all | solution.py:397
  43.7 7.7 %core.1 = (f32[4,64,128]{2,1,0:T(8,128)S(1)}, bf16[4,64,128]{2,1,0:T(8,128)(2,1)S(1)}, bf16[2,1024,512]{2,1,0:T(8,128)(2,1)S(1)}, bf16[1024,1024]{1,0:T(8,128)(2,1)S(1)}, bf16[1024,1024]{1,0:T(8,128)(2,1)S(1)}) custom-call(s32[10]{0:T(128)S(1)} %pad_add_fusion.place_ref, bf16[32,2,128,128]{3,2,1,0:T(8,128)(2,1)S(1)} %all-to-all-done.x, ...), custom_call_target="tpu_custom_call" | custom-call | flops 5242880000 | bytes 4194304 | tf_op jit(solution)/shard_map/core/pallas_call | solution.py:267
  51.4 1.0 %collective-permute-start.4 = (bf16[4,64,128]{2,1,0:T(8,128)(2,1)S(1)}, bf16[4,64,128]{2,1,0:T(8,128)(2,1)S(1)}, u32[]{:S(2)}, u32[]{:S(2)}) collective-permute-start(bf16[4,64,128]{2,1,0:T(8,128)(2,1)S(1)} %get-tuple-element.30), channel_id=1, source_target_pairs={{0,4},{4,0},{8,12},{12,8},{16,20},{20,16},{24,28},{28,24},{1,5},{5... | collective-permute-start | bytes 196616 | tf_op jit(solution)/shard_map/ppermute | solution.py:364
  52.4 3.1 %back.1 = bf16[32,128,128]{2,1,0:T(8,128)(2,1)} custom-call(bf16[2,1024,512]{2,1,0:T(8,128)(2,1)S(1)} %get-tuple-element.26.uv, bf16[1024,1024]{1,0:T(8,128)(2,1)S(1)} %get-tuple-element.27.cos, bf16[1024,1024]{1,0:T(8,128)(2,1)S(1)} %get-tuple-element.28.sin), custom_call_target="tpu_custom_call" | custom-call | flops 2202009600 | bytes 1048576 | tf_op jit(solution)/shard_map/back/pallas_call | solution.py:292
  55.4 0.0 copy-start.1
  55.4 0.0 copy-start.2
  55.4 7.3 %all-to-all-start.1 = ((bf16[32,128,128]{2,1,0:T(8,128)(2,1)}), bf16[32,128,128]{2,1,0:T(8,128)(2,1)S(1)}, u32[]{:S(2)}, u32[]{:S(2)}) async-start(bf16[32,128,128]{2,1,0:T(8,128)(2,1)} %back.1), calls=%async_computation.1 | async-start | bytes 2097152 | tf_op jit(solution)/shard_map/all_to_all | solution.py:405
  62.8 0.0 collective-permute-done.4
  62.8 3.0 %collective-permute-start.5 = (bf16[2,64,128]{2,1,0:T(8,128)(2,1)S(1)}, bf16[2,64,128]{2,1,0:T(8,128)(2,1)S(1)}, u32[]{:S(2)}, u32[]{:S(2)}) collective-permute-start(bf16[2,64,128]{2,1,0:T(8,128)(2,1)S(1)} %select_convert_fusion), channel_id=1, source_target_pairs={{0,8},{4,12},{8,0},{12,4},{16,24},{20,28},{24,16},{28,20},{1,9},{5... | collective-permute-start | bytes 98312 | tf_op jit(solution)/shard_map/ppermute | solution.py:364
  65.8 2.2 %collective-permute-done.5 = bf16[2,64,128]{2,1,0:T(8,128)(2,1)S(1)} collective-permute-done((bf16[2,64,128]{2,1,0:T(8,128)(2,1)S(1)}, bf16[2,64,128]{2,1,0:T(8,128)(2,1)S(1)}, u32[]{:S(2)}, u32[]{:S(2)}) %collective-permute-start.5) | collective-permute-done | bytes 32800 | tf_op jit(solution)/shard_map/ppermute | solution.py:364
  68.1 5.2 %collective-permute-start.6 = (bf16[1,64,128]{2,1,0:T(8,128)(2,1)S(1)}, bf16[1,64,128]{2,1,0:T(8,128)(2,1)S(1)}, u32[]{:S(2)}, u32[]{:S(2)}) collective-permute-start(bf16[1,64,128]{2,1,0:T(8,128)(2,1)S(1)} %select_convert_fusion.1), channel_id=1, source_target_pairs={{0,16},{4,20},{8,24},{12,28},{16,0},{20,4},{24,8},{28,12},{1,17},{... | collective-permute-start | bytes 49160 | tf_op jit(solution)/shard_map/ppermute | solution.py:364
  73.3 2.5 %collective-permute-done.6 = bf16[1,64,128]{2,1,0:T(8,128)(2,1)S(1)} collective-permute-done((bf16[1,64,128]{2,1,0:T(8,128)(2,1)S(1)}, bf16[1,64,128]{2,1,0:T(8,128)(2,1)S(1)}, u32[]{:S(2)}, u32[]{:S(2)}) %collective-permute-start.6) | collective-permute-done | bytes 16416 | tf_op jit(solution)/shard_map/ppermute | solution.py:364
  75.8 5.4 %collective-permute-start.7 = (f32[64,128]{1,0:T(8,128)S(1)}, f32[64,128]{1,0:T(8,128)S(1)}, u32[]{:S(2)}, u32[]{:S(2)}) collective-permute-start(f32[64,128]{1,0:T(8,128)S(1)} %add_bitcast_fusion), channel_id=1, source_target_pairs={{16,0},{48,4},{64,8},{96,12},{136,16},{176,20},{216,24},{224,28},{... | collective-permute-start | bytes 98312 | tf_op jit(solution)/shard_map/ppermute | solution.py:389
  81.3 4.6 %collective-permute-done.7.lags = f32[64,128]{1,0:T(8,128)S(1)} collective-permute-done((f32[64,128]{1,0:T(8,128)S(1)}, f32[64,128]{1,0:T(8,128)S(1)}, u32[]{:S(2)}, u32[]{:S(2)}) %collective-permute-start.7) | collective-permute-done | bytes 32800 | tf_op jit(solution)/shard_map/ppermute | solution.py:389
  85.9 0.0 all-to-all-done.1.conv
  85.9 0.0 copy-done.1
  85.9 0.0 copy-done.2
  85.9 1.6 %unpack.1 = (bf16[128,4096]{1,0:T(8,128)(2,1)}, bf16[128,4096]{1,0:T(8,128)(2,1)}, f32[64,128]{1,0:T(8,128)}) custom-call(bf16[32,128,128]{2,1,0:T(8,128)(2,1)S(1)} %all-to-all-done.1.conv, bf16[128,4096]{1,0:T(8,128)(2,1)S(1)} %bitcast.18, bf16[128,4096]{1,0:T(8,128)(2,1)S(1)} %bitcast.20, f32[64,128]{1,0:T(8,128)S(1)} %collective-permute-done.7.lags), custom_call_target="tpu_custom_call" | custom-call | flops 2097152 | bytes 5242880 | tf_op jit(solution)/shard_map/unpack/pallas_call | solution.py:333
  (9 shorter events, 0.1 us)
Async XLA Ops:
  0.6 10.1 %collective-permute-start = (f32[64,128]{1,0:T(8,128)}, f32[64,128]{1,0:T(8,128)S(1)}, u32[]{:S(2)}, u32[]{:S(2)}) collective-permute-start(f32[64,128]{1,0:T(8,128)} %param.13), channel_id=1, source_target_pairs={{0,16},{4,48},{8,64},{12,96},{16,136},{20,176},{24,216},{28,224},{... | collective-permute-start | bytes 98312 | tf_op jit(solution)/shard_map/ppermute | solution.py:370
  10.7 21.7 %copy-start = (bf16[1,128,4096]{2,1,0:T(8,128)(2,1)S(1)}, bf16[1,128,4096]{2,1,0:T(8,128)(2,1)}, u32[]{:S(2)}) copy-start(bf16[1,128,4096]{2,1,0:T(8,128)(2,1)} %param.12) | copy-start | bytes 3145732
  10.7 33.0 %all-to-all-start = ((bf16[32,2,128,128]{3,2,1,0:T(8,128)(2,1)}), bf16[32,2,128,128]{3,2,1,0:T(8,128)(2,1)S(1)}, u32[]{:S(2)}, u32[]{:S(2)}) async-start(bf16[32,2,128,128]{3,2,1,0:T(8,128)(2,1)} %pack.1), calls=%async_computation | async-start | bytes 4194304 | tf_op jit(solution)/shard_map/all_to_all | solution.py:397
  17.8 7.9 %collective-permute-start.1 = (f32[1,64,128]{2,1,0:T(8,128)S(1)}, f32[1,64,128]{2,1,0:T(8,128)S(1)}, u32[]{:S(2)}, u32[]{:S(2)}) collective-permute-start(f32[1,64,128]{2,1,0:T(8,128)S(1)} %bitcast.24), channel_id=1, source_target_pairs={{0,16},{4,20},{8,24},{12,28},{16,0},{20,4},{24,8},{28,12},{1,17},{... | collective-permute-start | bytes 98312 | tf_op jit(solution)/shard_map/ppermute | solution.py:364
  25.7 5.9 %collective-permute-start.2 = (f32[2,64,128]{2,1,0:T(8,128)S(1)}, f32[2,64,128]{2,1,0:T(8,128)S(1)}, u32[]{:S(2)}, u32[]{:S(2)}) collective-permute-start(f32[2,64,128]{2,1,0:T(8,128)S(1)} %pad_maximum_fusion), channel_id=1, source_target_pairs={{0,8},{4,12},{8,0},{12,4},{16,24},{20,28},{24,16},{28,20},{1,9},{5... | collective-permute-start | bytes 196616 | tf_op jit(solution)/shard_map/ppermute | solution.py:364
  31.6 5.0 %collective-permute-start.3 = (f32[4,64,128]{2,1,0:T(8,128)S(1)}, f32[4,64,128]{2,1,0:T(8,128)S(1)}, u32[]{:S(2)}, u32[]{:S(2)}) collective-permute-start(f32[4,64,128]{2,1,0:T(8,128)S(1)} %constant_dynamic-update-slice_fusion.near), channel_id=1, source_target_pairs={{0,4},{4,0},{8,12},{12,8},{16,20},{20,16},{24,28},{28,24},{1,5},{5... | collective-permute-start | bytes 393224 | tf_op jit(solution)/shard_map/ppermute | solution.py:364
  32.4 1.2 %copy-start.3 = (bf16[1,128,4096]{2,1,0:T(8,128)(2,1)S(1)}, bf16[1,128,4096]{2,1,0:T(8,128)(2,1)}, u32[]{:S(2)}) copy-start(bf16[1,128,4096]{2,1,0:T(8,128)(2,1)} %param.11) | copy-start | bytes 3145732
  36.6 1.0 %copy-start.4 = (f32[4,32,1024]{2,1,0:T(8,128)S(1)}, f32[4,32,1024]{2,1,0:T(8,128)}, u32[]{:S(2)}) copy-start(f32[4,32,1024]{2,1,0:T(8,128)} %constant.46.clone.seed) | copy-start | bytes 1572868
  51.4 11.4 %collective-permute-start.4 = (bf16[4,64,128]{2,1,0:T(8,128)(2,1)S(1)}, bf16[4,64,128]{2,1,0:T(8,128)(2,1)S(1)}, u32[]{:S(2)}, u32[]{:S(2)}) collective-permute-start(bf16[4,64,128]{2,1,0:T(8,128)(2,1)S(1)} %get-tuple-element.30), channel_id=1, source_target_pairs={{0,4},{4,0},{8,12},{12,8},{16,20},{20,16},{24,28},{28,24},{1,5},{5... | collective-permute-start | bytes 196616 | tf_op jit(solution)/shard_map/ppermute | solution.py:364
  55.4 30.4 %copy-start.1 = (bf16[1,128,4096]{2,1,0:T(8,128)(2,1)S(1)}, bf16[1,128,4096]{2,1,0:T(8,128)(2,1)}, u32[]{:S(2)}) copy-start(bf16[1,128,4096]{2,1,0:T(8,128)(2,1)} %param.9) | copy-start | bytes 3145732
  55.4 30.4 %copy-start.2 = (bf16[1,128,4096]{2,1,0:T(8,128)(2,1)S(1)}, bf16[1,128,4096]{2,1,0:T(8,128)(2,1)}, u32[]{:S(2)}) copy-start(bf16[1,128,4096]{2,1,0:T(8,128)(2,1)} %param.10) | copy-start | bytes 3145732
  55.4 30.4 %all-to-all-start.1 = ((bf16[32,128,128]{2,1,0:T(8,128)(2,1)}), bf16[32,128,128]{2,1,0:T(8,128)(2,1)S(1)}, u32[]{:S(2)}, u32[]{:S(2)}) async-start(bf16[32,128,128]{2,1,0:T(8,128)(2,1)} %back.1), calls=%async_computation.1 | async-start | bytes 2097152 | tf_op jit(solution)/shard_map/all_to_all | solution.py:405
  62.8 5.2 %collective-permute-start.5 = (bf16[2,64,128]{2,1,0:T(8,128)(2,1)S(1)}, bf16[2,64,128]{2,1,0:T(8,128)(2,1)S(1)}, u32[]{:S(2)}, u32[]{:S(2)}) collective-permute-start(bf16[2,64,128]{2,1,0:T(8,128)(2,1)S(1)} %select_convert_fusion), channel_id=1, source_target_pairs={{0,8},{4,12},{8,0},{12,4},{16,24},{20,28},{24,16},{28,20},{1,9},{5... | collective-permute-start | bytes 98312 | tf_op jit(solution)/shard_map/ppermute | solution.py:364
  68.1 7.7 %collective-permute-start.6 = (bf16[1,64,128]{2,1,0:T(8,128)(2,1)S(1)}, bf16[1,64,128]{2,1,0:T(8,128)(2,1)S(1)}, u32[]{:S(2)}, u32[]{:S(2)}) collective-permute-start(bf16[1,64,128]{2,1,0:T(8,128)(2,1)S(1)} %select_convert_fusion.1), channel_id=1, source_target_pairs={{0,16},{4,20},{8,24},{12,28},{16,0},{20,4},{24,8},{28,12},{1,17},{... | collective-permute-start | bytes 49160 | tf_op jit(solution)/shard_map/ppermute | solution.py:364
  75.8 10.1 %collective-permute-start.7 = (f32[64,128]{1,0:T(8,128)S(1)}, f32[64,128]{1,0:T(8,128)S(1)}, u32[]{:S(2)}, u32[]{:S(2)}) collective-permute-start(f32[64,128]{1,0:T(8,128)S(1)} %add_bitcast_fusion), channel_id=1, source_target_pairs={{16,0},{48,4},{64,8},{96,12},{136,16},{176,20},{216,24},{224,28},{... | collective-permute-start | bytes 98312 | tf_op jit(solution)/shard_map/ppermute | solution.py:389

commit v4 on v3

--- a/solution.py
+++ b/solution.py
@@ -232,12 +232,12 @@
     row = lax.broadcasted_iota(jnp.int32, (LANES // 2, LANES), 0)
     col = lax.broadcasted_iota(jnp.int32, (LANES // 2, LANES), 1)
     row = jnp.where(odd == 0, row, LANES // 2 - 1 - row)
-    fold = jnp.where((col == row) | (col == LANES - 1 - row), 1.0 / SEQ, 0.0).astype(BF16)
+    fold = jnp.where((col == row) | (col == LANES - 1 - row), 1.0, 0.0).astype(BF16)
     upper = lags.astype(BF16)
     total = dot(fold, upper) + dot(fold, (lags - upper.astype(F32)).astype(BF16))
     for block in range(SEQ // BLOCK):
         home = place_ref[2 + block]
-        folded[((z ^ home) & 1) * 4 + (home & 2) + (home >> 2)] = total[:, lanes_of(block)]
+        folded[((z ^ home) & 2) * 2 + (home & 1) * 2 + (home >> 2)] = total[:, lanes_of(block)]
     keep[...] = folded[:4]
     give[...] = folded[4:].astype(BF16)
 
@@ -376,11 +376,20 @@
     return near, swap_z(near, 0)
 
 
-def summed_over_z(lags, bit):
+def halves(lags, bit):
     low, high = jnp.split(lags, 2, axis=0)
     first = (lax.axis_index("z") >> bit) % 2 == 0
-    given = jnp.where(first, high, low).astype(BF16)
-    return jnp.where(first, low, high) + swap_z(given, bit).astype(F32)
+    kept = lax.optimization_barrier(jnp.where(first, low, high))
+    given = lax.optimization_barrier(jnp.where(first, high, low))
+    return kept, given.astype(BF16)
+
+
+def joined(kept, given, bit):
+    other = lax.optimization_barrier(swap_z(given, bit).astype(F32))
+    total = lax.optimization_barrier(kept + other)
+    for halvings in (3, 2):
+        total = lax.optimization_barrier(total * 0.5**halvings)
+    return total
 
 
 def sent_home(lags):
@@ -401,9 +410,11 @@
     filt, seed, query_grad = lax.optimization_barrier((filt, seed, times(g, conv_out[0])[None]))
 
     keep, give, uv, cos, sin = core(place, x, filt, seed)
-    lags = keep + swap_z(give, 0).astype(F32)
-    conv = lax.all_to_all(back(uv, cos, sin), PLANE, split_axis=0, concat_axis=0, tiled=True)
-    lags = summed_over_z(summed_over_z(lags, 1), 2)[0]
+    kept, given = halves(keep + swap_z(give, 1).astype(F32), 0)
+    conv, kept, given = lax.optimization_barrier((back(uv, cos, sin), kept, given))
+    conv = lax.all_to_all(conv, PLANE, split_axis=0, concat_axis=0, tiled=True)
+    kept, given = halves(joined(kept, given, 0), 2)
+    lags = joined(kept, given, 2)[0]
     key_grad, value_grad, filter_grad = unpack(conv, k, v, sent_home(lags))
     return query_grad, key_grad[None], value_grad[None], filter_grad
 

time: 88.1 us -> 87.4 us (level)
  the two profiles are of different devices: /device:TPU:30 before, /device:TPU:192 now
where the time goes in v4:
time: 87.4 us; the launch traced here: 86.9 us
  waiting for transfers between devices  35.5 us (41%)
  starting transfers between devices  27.1 us (31%)
  Pallas kernels  20.1 us (23%)
  local copies, waits for them, and re-layouts  2.99 us (3%)
  between operations  0.98 us (1%)
    ppermute x6, waiting for transfers between devices, swap_z(): return lax.ppermute(block, 'z', [(i, i ^ 1 << bit) for i in range(8)])  19.2 us
    ppermute x1, waiting for transfers between devices, sent_home(): return lax.ppermute(lags, CTX_Z, route)  11 us
    ppermute x6, starting transfers between devices, swap_z(): return lax.ppermute(block, 'z', [(i, i ^ 1 << bit) for i in range(8)])  8.74 us
    pallas_call x1, Pallas kernels, core(): pl.pallas_call(core_kernel, in_specs=[SMEM, VMEM, HBM, VMEM], out_specs=(...  7.7 us
    all_to_all x1, starting transfers between devices, local(): x = lax.all_to_all(x, PLANE, split_axis=0, concat_axis=0, tiled=True)  6.18 us
    ppermute x1, starting transfers between devices, sent_out(): return lax.ppermute(filters, CTX_Z, route)[None]  5.73 us
    all_to_all x1, waiting for transfers between devices, local(): x = lax.all_to_all(x, PLANE, split_axis=0, concat_axis=0, tiled=True)  5.38 us
    all_to_all x1, starting transfers between devices, local(): conv = lax.all_to_all(conv, PLANE, split_axis=0, concat_axis=0, tiled=True)  4.41 us
  transfers between devices with their start and end apart: 10, of which 7 were waited for; matrix products, arithmetic and copies ran while one was open for 1% of the time, Pallas kernels for 12%

profile of v4, /device:TPU:192, one launch (start us, length us, event | category | flops | bytes accessed | tf_op | source)
XLA Modules:
  0.0 86.9 jit_solution(5135818851200925332)
XLA Ops:
  0.6 5.7 %collective-permute-start = (f32[64,128]{1,0:T(8,128)}, f32[64,128]{1,0:T(8,128)S(1)}, u32[]{:S(2)}, u32[]{:S(2)}) collective-permute-start(f32[64,128]{1,0:T(8,128)} %param.13), channel_id=1, source_target_pairs={{0,16},{4,48},{8,64},{12,96},{16,136},{20,176},{24,216},{28,224},{... | collective-permute-start | bytes 98312 | tf_op jit(solution)/shard_map/ppermute | solution.py:370
  6.4 3.6 %pack.1 = bf16[32,2,128,128]{3,2,1,0:T(8,128)(2,1)} custom-call(bf16[128,4096]{1,0:T(8,128)(2,1)} %bitcast.22, bf16[128,4096]{1,0:T(8,128)(2,1)} %bitcast.14, bf16[128,4096]{1,0:T(8,128)(2,1)} %bitcast.16, bf16[128,4096]{1,0:T(8,128)(2,1)} %bitcast.18), custom_call_target="tpu_custom_call" | custom-call | flops 2097152 | bytes 6291456 | tf_op jit(solution)/shard_map/pack/pallas_call | solution.py:127
  10.0 0.0 collective-permute-done
  10.0 0.0 copy-start
  10.0 6.2 %all-to-all-start = ((bf16[32,2,128,128]{3,2,1,0:T(8,128)(2,1)}), bf16[32,2,128,128]{3,2,1,0:T(8,128)(2,1)S(1)}, u32[]{:S(2)}, u32[]{:S(2)}) async-start(bf16[32,2,128,128]{3,2,1,0:T(8,128)(2,1)} %pack.1), calls=%async_computation | async-start | bytes 4194304 | tf_op jit(solution)/shard_map/all_to_all | solution.py:406
  16.2 1.7 %collective-permute-start.1 = (f32[1,64,128]{2,1,0:T(8,128)S(1)}, f32[1,64,128]{2,1,0:T(8,128)S(1)}, u32[]{:S(2)}, u32[]{:S(2)}) collective-permute-start(f32[1,64,128]{2,1,0:T(8,128)S(1)} %bitcast.23), channel_id=1, source_target_pairs={{0,16},{4,20},{8,24},{12,28},{16,0},{20,4},{24,8},{28,12},{1,17},{... | collective-permute-start | bytes 98312 | tf_op jit(solution)/shard_map/ppermute | solution.py:364
  17.9 6.4 %collective-permute-done.1 = f32[1,64,128]{2,1,0:T(8,128)S(1)} collective-permute-done((f32[1,64,128]{2,1,0:T(8,128)S(1)}, f32[1,64,128]{2,1,0:T(8,128)S(1)}, u32[]{:S(2)}, u32[]{:S(2)}) %collective-permute-start.1) | collective-permute-done | bytes 32800 | tf_op jit(solution)/shard_map/ppermute | solution.py:364
  24.3 1.1 %collective-permute-start.2 = (f32[2,64,128]{2,1,0:T(8,128)S(1)}, f32[2,64,128]{2,1,0:T(8,128)S(1)}, u32[]{:S(2)}, u32[]{:S(2)}) collective-permute-start(f32[2,64,128]{2,1,0:T(8,128)S(1)} %pad_maximum_fusion), channel_id=1, source_target_pairs={{0,8},{4,12},{8,0},{12,4},{16,24},{20,28},{24,16},{28,20},{1,9},{5... | collective-permute-start | bytes 196616 | tf_op jit(solution)/shard_map/ppermute | solution.py:364
  25.4 4.1 %collective-permute-done.2 = f32[2,64,128]{2,1,0:T(8,128)S(1)} collective-permute-done((f32[2,64,128]{2,1,0:T(8,128)S(1)}, f32[2,64,128]{2,1,0:T(8,128)S(1)}, u32[]{:S(2)}, u32[]{:S(2)}) %collective-permute-start.2) | collective-permute-done | bytes 65568 | tf_op jit(solution)/shard_map/ppermute | solution.py:364
  29.5 0.7 collective-permute-start.3
  30.1 0.7 dynamic-slice_bitcast_fusion
  30.8 0.0 copy-done
  30.8 0.0 copy-start.3
  30.8 1.2 %copy-done.3 = bf16[1,128,4096]{2,1,0:T(8,128)(2,1)S(1)} copy-done((bf16[1,128,4096]{2,1,0:T(8,128)(2,1)S(1)}, bf16[1,128,4096]{2,1,0:T(8,128)(2,1)}, u32[]{:S(2)}) %copy-start.3) | copy-done | bytes 1048600
  32.1 1.1 %times.1 = bf16[128,4096]{1,0:T(8,128)(2,1)} custom-call(bf16[128,4096]{1,0:T(8,128)(2,1)S(1)} %bitcast.15, bf16[128,4096]{1,0:T(8,128)(2,1)S(1)} %bitcast.20), custom_call_target="tpu_custom_call" | custom-call | flops 1 | bytes 1 | tf_op jit(solution)/shard_map/times/pallas_call | solution.py:351
  33.1 0.1 pad_add_fusion.place_ref
  33.2 1.2 %collective-permute-done.3.far = f32[4,64,128]{2,1,0:T(8,128)S(1)} collective-permute-done((f32[4,64,128]{2,1,0:T(8,128)S(1)}, f32[4,64,128]{2,1,0:T(8,128)S(1)}, u32[]{:S(2)}, u32[]{:S(2)}) %collective-permute-start.3) | collective-permute-done | bytes 131104 | tf_op jit(solution)/shard_map/ppermute | solution.py:364
  34.4 0.0 copy-start.4
  34.4 1.0 %copy-done.4 = f32[4,32,1024]{2,1,0:T(8,128)S(1)} copy-done((f32[4,32,1024]{2,1,0:T(8,128)S(1)}, f32[4,32,1024]{2,1,0:T(8,128)}, u32[]{:S(2)}) %copy-start.4) | copy-done | bytes 524312
  35.5 3.1 %filter_spectrum.1 = (f32[2,1024,128]{2,1,0:T(8,128)}, f32[4,32,1024]{2,1,0:T(8,128)S(1)}) custom-call(s32[10]{0:T(128)S(1)} %pad_add_fusion.place_ref, f32[4,32,1024]{2,1,0:T(8,128)S(1)} %copy-done.4, f32[4,64,128]{2,1,0:T(8,128)S(1)} %constant_dynamic-update-slice_fusion.near, f32[4,64,128]{2,1,0:T(8,128)S(1)} %collective-permute-done.3.far), custom_call_target="tpu_custom_call" | custom-call | flops 1 | bytes 1 | tf_op jit(solution)/shard_map/filter_spectrum/pallas_call | solution.py:172
  38.5 5.4 %all-to-all-done.x = bf16[32,2,128,128]{3,2,1,0:T(8,128)(2,1)S(1)} async-done(((bf16[32,2,128,128]{3,2,1,0:T(8,128)(2,1)}), bf16[32,2,128,128]{3,2,1,0:T(8,128)(2,1)S(1)}, u32[]{:S(2)}, u32[]{:S(2)}) %all-to-all-start) | async-done | bytes 2097184 | tf_op jit(solution)/shard_map/all_to_all | solution.py:406
  43.9 7.7 %core.1 = (f32[4,64,128]{2,1,0:T(8,128)S(1)}, bf16[4,64,128]{2,1,0:T(8,128)(2,1)S(1)}, bf16[2,1024,512]{2,1,0:T(8,128)(2,1)S(1)}, bf16[1024,1024]{1,0:T(8,128)(2,1)S(1)}, bf16[1024,1024]{1,0:T(8,128)(2,1)S(1)}) custom-call(s32[10]{0:T(128)S(1)} %pad_add_fusion.place_ref, bf16[32,2,128,128]{3,2,1,0:T(8,128)(2,1)S(1)} %all-to-all-done.x, ...), custom_call_target="tpu_custom_call" | custom-call | flops 5242880000 | bytes 4194304 | tf_op jit(solution)/shard_map/core/pallas_call | solution.py:267
  51.6 1.4 %collective-permute-start.4 = (bf16[4,64,128]{2,1,0:T(8,128)(2,1)S(1)}, bf16[4,64,128]{2,1,0:T(8,128)(2,1)S(1)}, u32[]{:S(2)}, u32[]{:S(2)}) collective-permute-start(bf16[4,64,128]{2,1,0:T(8,128)(2,1)S(1)} %get-tuple-element.33), channel_id=1, source_target_pairs={{0,8},{4,12},{8,0},{12,4},{16,24},{20,28},{24,16},{28,20},{1,9},{5... | collective-permute-start | bytes 196616 | tf_op jit(solution)/shard_map/ppermute | solution.py:364
  53.0 3.1 %back.1 = bf16[32,128,128]{2,1,0:T(8,128)(2,1)} custom-call(bf16[2,1024,512]{2,1,0:T(8,128)(2,1)S(1)} %get-tuple-element.29.uv, bf16[1024,1024]{1,0:T(8,128)(2,1)S(1)} %get-tuple-element.30.cos, bf16[1024,1024]{1,0:T(8,128)(2,1)S(1)} %get-tuple-element.31.sin), custom_call_target="tpu_custom_call" | custom-call | flops 2202009600 | bytes 1048576 | tf_op jit(solution)/shard_map/back/pallas_call | solution.py:292
  56.1 0.0 copy-start.1
  56.1 0.0 copy-start.2
  56.1 1.5 %collective-permute-done.4 = bf16[4,64,128]{2,1,0:T(8,128)(2,1)S(1)} collective-permute-done((bf16[4,64,128]{2,1,0:T(8,128)(2,1)S(1)}, bf16[4,64,128]{2,1,0:T(8,128)(2,1)S(1)}, u32[]{:S(2)}, u32[]{:S(2)}) %collective-permute-start.4) | collective-permute-done | bytes 65568 | tf_op jit(solution)/shard_map/ppermute | solution.py:364
  57.6 2.2 %collective-permute-start.5 = (bf16[2,64,128]{2,1,0:T(8,128)(2,1)S(1)}, bf16[2,64,128]{2,1,0:T(8,128)(2,1)S(1)}, u32[]{:S(2)}, u32[]{:S(2)}) collective-permute-start(bf16[2,64,128]{2,1,0:T(8,128)(2,1)S(1)} %slice_select_fusion), channel_id=1, source_target_pairs={{0,4},{4,0},{8,12},{12,8},{16,20},{20,16},{24,28},{28,24},{1,5},{5... | collective-permute-start | bytes 98312 | tf_op jit(solution)/shard_map/ppermute | solution.py:364
  59.9 4.4 %all-to-all-start.1 = ((bf16[32,128,128]{2,1,0:T(8,128)(2,1)}), bf16[32,128,128]{2,1,0:T(8,128)(2,1)S(1)}, u32[]{:S(2)}, u32[]{:S(2)}) async-start(bf16[32,128,128]{2,1,0:T(8,128)(2,1)} %back.1), calls=%async_computation.1 | async-start | bytes 2097152 | tf_op jit(solution)/shard_map/all_to_all | solution.py:415
  64.3 0.0 collective-permute-done.5
  64.4 1.8 %collective-permute-start.6 = (bf16[1,64,128]{2,1,0:T(8,128)(2,1)S(1)}, bf16[1,64,128]{2,1,0:T(8,128)(2,1)S(1)}, u32[]{:S(2)}, u32[]{:S(2)}) collective-permute-start(bf16[1,64,128]{2,1,0:T(8,128)(2,1)S(1)} %slice_select_fusion.2), channel_id=1, source_target_pairs={{0,16},{4,20},{8,24},{12,28},{16,0},{20,4},{24,8},{28,12},{1,17},{... | collective-permute-start | bytes 49160 | tf_op jit(solution)/shard_map/ppermute | solution.py:364
  66.1 6.0 %collective-permute-done.6 = bf16[1,64,128]{2,1,0:T(8,128)(2,1)S(1)} collective-permute-done((bf16[1,64,128]{2,1,0:T(8,128)(2,1)S(1)}, bf16[1,64,128]{2,1,0:T(8,128)(2,1)S(1)}, u32[]{:S(2)}, u32[]{:S(2)}) %collective-permute-start.6) | collective-permute-done | bytes 16416 | tf_op jit(solution)/shard_map/ppermute | solution.py:364
  72.2 2.0 %collective-permute-start.7 = (f32[64,128]{1,0:T(8,128)S(1)}, f32[64,128]{1,0:T(8,128)S(1)}, u32[]{:S(2)}, u32[]{:S(2)}) collective-permute-start(f32[64,128]{1,0:T(8,128)S(1)} %bitcast.26), channel_id=1, source_target_pairs={{16,0},{48,4},{64,8},{96,12},{136,16},{176,20},{216,24},{224,28},{... | collective-permute-start | bytes 98312 | tf_op jit(solution)/shard_map/ppermute | solution.py:398
  74.2 11.0 %collective-permute-done.7.lags = f32[64,128]{1,0:T(8,128)S(1)} collective-permute-done((f32[64,128]{1,0:T(8,128)S(1)}, f32[64,128]{1,0:T(8,128)S(1)}, u32[]{:S(2)}, u32[]{:S(2)}) %collective-permute-start.7) | collective-permute-done | bytes 32800 | tf_op jit(solution)/shard_map/ppermute | solution.py:398
  85.2 0.0 all-to-all-done.1.conv
  85.2 0.0 copy-done.1
  85.2 0.0 copy-done.2
  85.2 1.6 %unpack.1 = (bf16[128,4096]{1,0:T(8,128)(2,1)}, bf16[128,4096]{1,0:T(8,128)(2,1)}, f32[64,128]{1,0:T(8,128)}) custom-call(bf16[32,128,128]{2,1,0:T(8,128)(2,1)S(1)} %all-to-all-done.1.conv, bf16[128,4096]{1,0:T(8,128)(2,1)S(1)} %bitcast.17, bf16[128,4096]{1,0:T(8,128)(2,1)S(1)} %bitcast.19, f32[64,128]{1,0:T(8,128)S(1)} %collective-permute-done.7.lags), custom_call_target="tpu_custom_call" | custom-call | flops 2097152 | bytes 5242880 | tf_op jit(solution)/shard_map/unpack/pallas_call | solution.py:333
  (17 shorter events, 0.1 us)
Async XLA Ops:
  0.6 9.4 %collective-permute-start = (f32[64,128]{1,0:T(8,128)}, f32[64,128]{1,0:T(8,128)S(1)}, u32[]{:S(2)}, u32[]{:S(2)}) collective-permute-start(f32[64,128]{1,0:T(8,128)} %param.13), channel_id=1, source_target_pairs={{0,16},{4,48},{8,64},{12,96},{16,136},{20,176},{24,216},{28,224},{... | collective-permute-start | bytes 98312 | tf_op jit(solution)/shard_map/ppermute | solution.py:370
  10.0 20.8 %copy-start = (bf16[1,128,4096]{2,1,0:T(8,128)(2,1)S(1)}, bf16[1,128,4096]{2,1,0:T(8,128)(2,1)}, u32[]{:S(2)}) copy-start(bf16[1,128,4096]{2,1,0:T(8,128)(2,1)} %param.12) | copy-start | bytes 3145732
  10.0 33.9 %all-to-all-start = ((bf16[32,2,128,128]{3,2,1,0:T(8,128)(2,1)}), bf16[32,2,128,128]{3,2,1,0:T(8,128)(2,1)S(1)}, u32[]{:S(2)}, u32[]{:S(2)}) async-start(bf16[32,2,128,128]{3,2,1,0:T(8,128)(2,1)} %pack.1), calls=%async_computation | async-start | bytes 4194304 | tf_op jit(solution)/shard_map/all_to_all | solution.py:406
  16.2 8.1 %collective-permute-start.1 = (f32[1,64,128]{2,1,0:T(8,128)S(1)}, f32[1,64,128]{2,1,0:T(8,128)S(1)}, u32[]{:S(2)}, u32[]{:S(2)}) collective-permute-start(f32[1,64,128]{2,1,0:T(8,128)S(1)} %bitcast.23), channel_id=1, source_target_pairs={{0,16},{4,20},{8,24},{12,28},{16,0},{20,4},{24,8},{28,12},{1,17},{... | collective-permute-start | bytes 98312 | tf_op jit(solution)/shard_map/ppermute | solution.py:364
  24.3 5.2 %collective-permute-start.2 = (f32[2,64,128]{2,1,0:T(8,128)S(1)}, f32[2,64,128]{2,1,0:T(8,128)S(1)}, u32[]{:S(2)}, u32[]{:S(2)}) collective-permute-start(f32[2,64,128]{2,1,0:T(8,128)S(1)} %pad_maximum_fusion), channel_id=1, source_target_pairs={{0,8},{4,12},{8,0},{12,4},{16,24},{20,28},{24,16},{28,20},{1,9},{5... | collective-permute-start | bytes 196616 | tf_op jit(solution)/shard_map/ppermute | solution.py:364
  29.5 5.0 %collective-permute-start.3 = (f32[4,64,128]{2,1,0:T(8,128)S(1)}, f32[4,64,128]{2,1,0:T(8,128)S(1)}, u32[]{:S(2)}, u32[]{:S(2)}) collective-permute-start(f32[4,64,128]{2,1,0:T(8,128)S(1)} %constant_dynamic-update-slice_fusion.near), channel_id=1, source_target_pairs={{0,4},{4,0},{8,12},{12,8},{16,20},{20,16},{24,28},{28,24},{1,5},{5... | collective-permute-start | bytes 393224 | tf_op jit(solution)/shard_map/ppermute | solution.py:364
  30.8 1.2 %copy-start.3 = (bf16[1,128,4096]{2,1,0:T(8,128)(2,1)S(1)}, bf16[1,128,4096]{2,1,0:T(8,128)(2,1)}, u32[]{:S(2)}) copy-start(bf16[1,128,4096]{2,1,0:T(8,128)(2,1)} %param.11) | copy-start | bytes 3145732
  34.4 1.0 %copy-start.4 = (f32[4,32,1024]{2,1,0:T(8,128)S(1)}, f32[4,32,1024]{2,1,0:T(8,128)}, u32[]{:S(2)}) copy-start(f32[4,32,1024]{2,1,0:T(8,128)} %constant.51.clone.seed) | copy-start | bytes 1572868
  51.6 6.0 %collective-permute-start.4 = (bf16[4,64,128]{2,1,0:T(8,128)(2,1)S(1)}, bf16[4,64,128]{2,1,0:T(8,128)(2,1)S(1)}, u32[]{:S(2)}, u32[]{:S(2)}) collective-permute-start(bf16[4,64,128]{2,1,0:T(8,128)(2,1)S(1)} %get-tuple-element.33), channel_id=1, source_target_pairs={{0,8},{4,12},{8,0},{12,4},{16,24},{20,28},{24,16},{28,20},{1,9},{5... | collective-permute-start | bytes 196616 | tf_op jit(solution)/shard_map/ppermute | solution.py:364
  56.1 29.1 %copy-start.1 = (bf16[1,128,4096]{2,1,0:T(8,128)(2,1)S(1)}, bf16[1,128,4096]{2,1,0:T(8,128)(2,1)}, u32[]{:S(2)}) copy-start(bf16[1,128,4096]{2,1,0:T(8,128)(2,1)} %param.9) | copy-start | bytes 3145732
  56.1 29.1 %copy-start.2 = (bf16[1,128,4096]{2,1,0:T(8,128)(2,1)S(1)}, bf16[1,128,4096]{2,1,0:T(8,128)(2,1)}, u32[]{:S(2)}) copy-start(bf16[1,128,4096]{2,1,0:T(8,128)(2,1)} %param.10) | copy-start | bytes 3145732
  57.6 6.6 %collective-permute-start.5 = (bf16[2,64,128]{2,1,0:T(8,128)(2,1)S(1)}, bf16[2,64,128]{2,1,0:T(8,128)(2,1)S(1)}, u32[]{:S(2)}, u32[]{:S(2)}) collective-permute-start(bf16[2,64,128]{2,1,0:T(8,128)(2,1)S(1)} %slice_select_fusion), channel_id=1, source_target_pairs={{0,4},{4,0},{8,12},{12,8},{16,20},{20,16},{24,28},{28,24},{1,5},{5... | collective-permute-start | bytes 98312 | tf_op jit(solution)/shard_map/ppermute | solution.py:364
  59.9 25.3 %all-to-all-start.1 = ((bf16[32,128,128]{2,1,0:T(8,128)(2,1)}), bf16[32,128,128]{2,1,0:T(8,128)(2,1)S(1)}, u32[]{:S(2)}, u32[]{:S(2)}) async-start(bf16[32,128,128]{2,1,0:T(8,128)(2,1)} %back.1), calls=%async_computation.1 | async-start | bytes 2097152 | tf_op jit(solution)/shard_map/all_to_all | solution.py:415
  64.4 7.7 %collective-permute-start.6 = (bf16[1,64,128]{2,1,0:T(8,128)(2,1)S(1)}, bf16[1,64,128]{2,1,0:T(8,128)(2,1)S(1)}, u32[]{:S(2)}, u32[]{:S(2)}) collective-permute-start(bf16[1,64,128]{2,1,0:T(8,128)(2,1)S(1)} %slice_select_fusion.2), channel_id=1, source_target_pairs={{0,16},{4,20},{8,24},{12,28},{16,0},{20,4},{24,8},{28,12},{1,17},{... | collective-permute-start | bytes 49160 | tf_op jit(solution)/shard_map/ppermute | solution.py:364
  72.2 13.0 %collective-permute-start.7 = (f32[64,128]{1,0:T(8,128)S(1)}, f32[64,128]{1,0:T(8,128)S(1)}, u32[]{:S(2)}, u32[]{:S(2)}) collective-permute-start(f32[64,128]{1,0:T(8,128)S(1)} %bitcast.26), channel_id=1, source_target_pairs={{16,0},{48,4},{64,8},{96,12},{136,16},{176,20},{216,24},{224,28},{... | collective-permute-start | bytes 98312 | tf_op jit(solution)/shard_map/ppermute | solution.py:398

commit v5 on v4

--- a/solution.py
+++ b/solution.py
@@ -237,7 +237,7 @@
     total = dot(fold, upper) + dot(fold, (lags - upper.astype(F32)).astype(BF16))
     for block in range(SEQ // BLOCK):
         home = place_ref[2 + block]
-        folded[((z ^ home) & 2) * 2 + (home & 1) * 2 + (home >> 2)] = total[:, lanes_of(block)]
+        folded[((z ^ home) & 1) * 4 + (home & 2) + (home >> 2)] = total[:, lanes_of(block)]
     keep[...] = folded[:4]
     give[...] = folded[4:].astype(BF16)
 
@@ -410,10 +410,10 @@
     filt, seed, query_grad = lax.optimization_barrier((filt, seed, times(g, conv_out[0])[None]))
 
     keep, give, uv, cos, sin = core(place, x, filt, seed)
-    kept, given = halves(keep + swap_z(give, 1).astype(F32), 0)
+    kept, given = halves(keep + swap_z(give, 0).astype(F32), 1)
     conv, kept, given = lax.optimization_barrier((back(uv, cos, sin), kept, given))
     conv = lax.all_to_all(conv, PLANE, split_axis=0, concat_axis=0, tiled=True)
-    kept, given = halves(joined(kept, given, 0), 2)
+    kept, given = halves(joined(kept, given, 1), 2)
     lags = joined(kept, given, 2)[0]
     key_grad, value_grad, filter_grad = unpack(conv, k, v, sent_home(lags))
     return query_grad, key_grad[None], value_grad[None], filter_grad

time: 87.4 us -> 86.1 us (0.985)
  waiting for transfers between devices: 35.5 us -> 33.9 us
    ppermute x6, starting transfers between devices: 8.74 us -> 6.51 us  [swap_z(): return lax.ppermute(block, 'z', [(i, i ^ 1 << bit) for i in range(8)])]
    ppermute x1, starting transfers between devices: 2.05 us -> 3.86 us  [sent_home(): return lax.ppermute(lags, CTX_Z, route)]
    ppermute x1, waiting for transfers between devices: 11 us -> 9.15 us  [sent_home(): return lax.ppermute(lags, CTX_Z, route)]
  transfers between devices with their start and end apart: 10 -> 10, of which waited for: 7 -> 7; matrix products, arithmetic and copies ran while one was open for 1% -> 1% of each run, Pallas kernels for 12% -> 13%
where the time goes in v5:
time: 86.1 us; the launch traced here: 85.3 us
  waiting for transfers between devices  33.9 us (39%)
  starting transfers between devices  27.2 us (32%)
  Pallas kernels  20.1 us (23%)
  local copies, waits for them, and re-layouts  2.99 us (3%)
  between operations  0.98 us (1%)
    ppermute x6, waiting for transfers between devices, swap_z(): return lax.ppermute(block, 'z', [(i, i ^ 1 << bit) for i in range(8)])  19.4 us
    ppermute x1, waiting for transfers between devices, sent_home(): return lax.ppermute(lags, CTX_Z, route)  9.15 us
    pallas_call x1, Pallas kernels, core(): pl.pallas_call(core_kernel, in_specs=[SMEM, VMEM, HBM, VMEM], out_specs=(...  7.7 us
    ppermute x6, starting transfers between devices, swap_z(): return lax.ppermute(block, 'z', [(i, i ^ 1 << bit) for i in range(8)])  6.51 us
    all_to_all x1, starting transfers between devices, local(): x = lax.all_to_all(x, PLANE, split_axis=0, concat_axis=0, tiled=True)  6.18 us
    ppermute x1, starting transfers between devices, sent_out(): return lax.ppermute(filters, CTX_Z, route)[None]  5.73 us
    all_to_all x1, waiting for transfers between devices, local(): x = lax.all_to_all(x, PLANE, split_axis=0, concat_axis=0, tiled=True)  5.38 us
    all_to_all x1, starting transfers between devices, local(): conv = lax.all_to_all(conv, PLANE, split_axis=0, concat_axis=0, tiled=True)  4.86 us
  transfers between devices with their start and end apart: 10, of which 7 were waited for; matrix products, arithmetic and copies ran while one was open for 1% of the time, Pallas kernels for 13%

profile of v5, /device:TPU:192, one launch (start us, length us, event | category | flops | bytes accessed | tf_op | source)
XLA Modules:
  0.0 85.3 jit_solution(11547597605671145925)
XLA Ops:
  0.6 5.7 %collective-permute-start = (f32[64,128]{1,0:T(8,128)}, f32[64,128]{1,0:T(8,128)S(1)}, u32[]{:S(2)}, u32[]{:S(2)}) collective-permute-start(f32[64,128]{1,0:T(8,128)} %param.13), channel_id=1, source_target_pairs={{0,16},{4,48},{8,64},{12,96},{16,136},{20,176},{24,216},{28,224},{... | collective-permute-start | bytes 98312 | tf_op jit(solution)/shard_map/ppermute | solution.py:370
  6.4 3.6 %pack.1 = bf16[32,2,128,128]{3,2,1,0:T(8,128)(2,1)} custom-call(bf16[128,4096]{1,0:T(8,128)(2,1)} %bitcast.22, bf16[128,4096]{1,0:T(8,128)(2,1)} %bitcast.14, bf16[128,4096]{1,0:T(8,128)(2,1)} %bitcast.16, bf16[128,4096]{1,0:T(8,128)(2,1)} %bitcast.18), custom_call_target="tpu_custom_call" | custom-call | flops 2097152 | bytes 6291456 | tf_op jit(solution)/shard_map/pack/pallas_call | solution.py:127
  10.0 0.0 collective-permute-done
  10.0 0.0 copy-start
  10.0 6.2 %all-to-all-start = ((bf16[32,2,128,128]{3,2,1,0:T(8,128)(2,1)}), bf16[32,2,128,128]{3,2,1,0:T(8,128)(2,1)S(1)}, u32[]{:S(2)}, u32[]{:S(2)}) async-start(bf16[32,2,128,128]{3,2,1,0:T(8,128)(2,1)} %pack.1), calls=%async_computation | async-start | bytes 4194304 | tf_op jit(solution)/shard_map/all_to_all | solution.py:406
  16.2 1.7 %collective-permute-start.1 = (f32[1,64,128]{2,1,0:T(8,128)S(1)}, f32[1,64,128]{2,1,0:T(8,128)S(1)}, u32[]{:S(2)}, u32[]{:S(2)}) collective-permute-start(f32[1,64,128]{2,1,0:T(8,128)S(1)} %bitcast.23), channel_id=1, source_target_pairs={{0,16},{4,20},{8,24},{12,28},{16,0},{20,4},{24,8},{28,12},{1,17},{... | collective-permute-start | bytes 98312 | tf_op jit(solution)/shard_map/ppermute | solution.py:364
  17.9 6.4 %collective-permute-done.1 = f32[1,64,128]{2,1,0:T(8,128)S(1)} collective-permute-done((f32[1,64,128]{2,1,0:T(8,128)S(1)}, f32[1,64,128]{2,1,0:T(8,128)S(1)}, u32[]{:S(2)}, u32[]{:S(2)}) %collective-permute-start.1) | collective-permute-done | bytes 32800 | tf_op jit(solution)/shard_map/ppermute | solution.py:364
  24.3 1.1 %collective-permute-start.2 = (f32[2,64,128]{2,1,0:T(8,128)S(1)}, f32[2,64,128]{2,1,0:T(8,128)S(1)}, u32[]{:S(2)}, u32[]{:S(2)}) collective-permute-start(f32[2,64,128]{2,1,0:T(8,128)S(1)} %pad_maximum_fusion), channel_id=1, source_target_pairs={{0,8},{4,12},{8,0},{12,4},{16,24},{20,28},{24,16},{28,20},{1,9},{5... | collective-permute-start | bytes 196616 | tf_op jit(solution)/shard_map/ppermute | solution.py:364
  25.4 4.1 %collective-permute-done.2 = f32[2,64,128]{2,1,0:T(8,128)S(1)} collective-permute-done((f32[2,64,128]{2,1,0:T(8,128)S(1)}, f32[2,64,128]{2,1,0:T(8,128)S(1)}, u32[]{:S(2)}, u32[]{:S(2)}) %collective-permute-start.2) | collective-permute-done | bytes 65568 | tf_op jit(solution)/shard_map/ppermute | solution.py:364
  29.5 0.7 collective-permute-start.3
  30.1 0.7 dynamic-slice_bitcast_fusion
  30.8 0.0 copy-done
  30.8 0.0 copy-start.3
  30.8 1.2 %copy-done.3 = bf16[1,128,4096]{2,1,0:T(8,128)(2,1)S(1)} copy-done((bf16[1,128,4096]{2,1,0:T(8,128)(2,1)S(1)}, bf16[1,128,4096]{2,1,0:T(8,128)(2,1)}, u32[]{:S(2)}) %copy-start.3) | copy-done | bytes 1048600
  32.1 1.1 %times.1 = bf16[128,4096]{1,0:T(8,128)(2,1)} custom-call(bf16[128,4096]{1,0:T(8,128)(2,1)S(1)} %bitcast.15, bf16[128,4096]{1,0:T(8,128)(2,1)S(1)} %bitcast.20), custom_call_target="tpu_custom_call" | custom-call | flops 1 | bytes 1 | tf_op jit(solution)/shard_map/times/pallas_call | solution.py:351
  33.1 0.1 pad_add_fusion.place_ref
  33.2 1.2 %collective-permute-done.3.far = f32[4,64,128]{2,1,0:T(8,128)S(1)} collective-permute-done((f32[4,64,128]{2,1,0:T(8,128)S(1)}, f32[4,64,128]{2,1,0:T(8,128)S(1)}, u32[]{:S(2)}, u32[]{:S(2)}) %collective-permute-start.3) | collective-permute-done | bytes 131104 | tf_op jit(solution)/shard_map/ppermute | solution.py:364
  34.4 0.0 copy-start.4
  34.4 1.0 %copy-done.4 = f32[4,32,1024]{2,1,0:T(8,128)S(1)} copy-done((f32[4,32,1024]{2,1,0:T(8,128)S(1)}, f32[4,32,1024]{2,1,0:T(8,128)}, u32[]{:S(2)}) %copy-start.4) | copy-done | bytes 524312
  35.5 3.1 %filter_spectrum.1 = (f32[2,1024,128]{2,1,0:T(8,128)}, f32[4,32,1024]{2,1,0:T(8,128)S(1)}) custom-call(s32[10]{0:T(128)S(1)} %pad_add_fusion.place_ref, f32[4,32,1024]{2,1,0:T(8,128)S(1)} %copy-done.4, f32[4,64,128]{2,1,0:T(8,128)S(1)} %constant_dynamic-update-slice_fusion.near, f32[4,64,128]{2,1,0:T(8,128)S(1)} %collective-permute-done.3.far), custom_call_target="tpu_custom_call" | custom-call | flops 1 | bytes 1 | tf_op jit(solution)/shard_map/filter_spectrum/pallas_call | solution.py:172
  38.5 5.4 %all-to-all-done.x = bf16[32,2,128,128]{3,2,1,0:T(8,128)(2,1)S(1)} async-done(((bf16[32,2,128,128]{3,2,1,0:T(8,128)(2,1)}), bf16[32,2,128,128]{3,2,1,0:T(8,128)(2,1)S(1)}, u32[]{:S(2)}, u32[]{:S(2)}) %all-to-all-start) | async-done | bytes 2097184 | tf_op jit(solution)/shard_map/all_to_all | solution.py:406
  43.9 7.7 %core.1 = (f32[4,64,128]{2,1,0:T(8,128)S(1)}, bf16[4,64,128]{2,1,0:T(8,128)(2,1)S(1)}, bf16[2,1024,512]{2,1,0:T(8,128)(2,1)S(1)}, bf16[1024,1024]{1,0:T(8,128)(2,1)S(1)}, bf16[1024,1024]{1,0:T(8,128)(2,1)S(1)}) custom-call(s32[10]{0:T(128)S(1)} %pad_add_fusion.place_ref, bf16[32,2,128,128]{3,2,1,0:T(8,128)(2,1)S(1)} %all-to-all-done.x, ...), custom_call_target="tpu_custom_call" | custom-call | flops 5242880000 | bytes 4194304 | tf_op jit(solution)/shard_map/core/pallas_call | solution.py:267
  51.6 1.1 %collective-permute-start.4 = (bf16[4,64,128]{2,1,0:T(8,128)(2,1)S(1)}, bf16[4,64,128]{2,1,0:T(8,128)(2,1)S(1)}, u32[]{:S(2)}, u32[]{:S(2)}) collective-permute-start(bf16[4,64,128]{2,1,0:T(8,128)(2,1)S(1)} %get-tuple-element.33), channel_id=1, source_target_pairs={{0,4},{4,0},{8,12},{12,8},{16,20},{20,16},{24,28},{28,24},{1,5},{5... | collective-permute-start | bytes 196616 | tf_op jit(solution)/shard_map/ppermute | solution.py:364
  52.7 3.1 %back.1 = bf16[32,128,128]{2,1,0:T(8,128)(2,1)} custom-call(bf16[2,1024,512]{2,1,0:T(8,128)(2,1)S(1)} %get-tuple-element.29.uv, bf16[1024,1024]{1,0:T(8,128)(2,1)S(1)} %get-tuple-element.30.cos, bf16[1024,1024]{1,0:T(8,128)(2,1)S(1)} %get-tuple-element.31.sin), custom_call_target="tpu_custom_call" | custom-call | flops 2202009600 | bytes 1048576 | tf_op jit(solution)/shard_map/back/pallas_call | solution.py:292
  55.8 0.0 copy-start.1
  55.8 0.0 copy-start.2
  55.8 0.8 collective-permute-done.4
  56.7 1.2 %collective-permute-start.5 = (bf16[2,64,128]{2,1,0:T(8,128)(2,1)S(1)}, bf16[2,64,128]{2,1,0:T(8,128)(2,1)S(1)}, u32[]{:S(2)}, u32[]{:S(2)}) collective-permute-start(bf16[2,64,128]{2,1,0:T(8,128)(2,1)S(1)} %slice_select_fusion), channel_id=1, source_target_pairs={{0,8},{4,12},{8,0},{12,4},{16,24},{20,28},{24,16},{28,20},{1,9},{5... | collective-permute-start | bytes 98312 | tf_op jit(solution)/shard_map/ppermute | solution.py:364
  57.8 4.9 %all-to-all-start.1 = ((bf16[32,128,128]{2,1,0:T(8,128)(2,1)}), bf16[32,128,128]{2,1,0:T(8,128)(2,1)S(1)}, u32[]{:S(2)}, u32[]{:S(2)}) async-start(bf16[32,128,128]{2,1,0:T(8,128)(2,1)} %back.1), calls=%async_computation.1 | async-start | bytes 2097152 | tf_op jit(solution)/shard_map/all_to_all | solution.py:415
  62.7 0.0 collective-permute-done.5
  62.8 0.8 collective-permute-start.6
  63.6 6.9 %collective-permute-done.6 = bf16[1,64,128]{2,1,0:T(8,128)(2,1)S(1)} collective-permute-done((bf16[1,64,128]{2,1,0:T(8,128)(2,1)S(1)}, bf16[1,64,128]{2,1,0:T(8,128)(2,1)S(1)}, u32[]{:S(2)}, u32[]{:S(2)}) %collective-permute-start.6) | collective-permute-done | bytes 16416 | tf_op jit(solution)/shard_map/ppermute | solution.py:364
  70.6 3.9 %collective-permute-start.7 = (f32[64,128]{1,0:T(8,128)S(1)}, f32[64,128]{1,0:T(8,128)S(1)}, u32[]{:S(2)}, u32[]{:S(2)}) collective-permute-start(f32[64,128]{1,0:T(8,128)S(1)} %bitcast.26), channel_id=1, source_target_pairs={{16,0},{48,4},{64,8},{96,12},{136,16},{176,20},{216,24},{224,28},{... | collective-permute-start | bytes 98312 | tf_op jit(solution)/shard_map/ppermute | solution.py:398
  74.4 9.2 %collective-permute-done.7.lags = f32[64,128]{1,0:T(8,128)S(1)} collective-permute-done((f32[64,128]{1,0:T(8,128)S(1)}, f32[64,128]{1,0:T(8,128)S(1)}, u32[]{:S(2)}, u32[]{:S(2)}) %collective-permute-start.7) | collective-permute-done | bytes 32800 | tf_op jit(solution)/shard_map/ppermute | solution.py:398
  83.6 0.0 all-to-all-done.1.conv
  83.6 0.0 copy-done.1
  83.6 0.0 copy-done.2
  83.6 1.6 %unpack.1 = (bf16[128,4096]{1,0:T(8,128)(2,1)}, bf16[128,4096]{1,0:T(8,128)(2,1)}, f32[64,128]{1,0:T(8,128)}) custom-call(bf16[32,128,128]{2,1,0:T(8,128)(2,1)S(1)} %all-to-all-done.1.conv, bf16[128,4096]{1,0:T(8,128)(2,1)S(1)} %bitcast.17, bf16[128,4096]{1,0:T(8,128)(2,1)S(1)} %bitcast.19, f32[64,128]{1,0:T(8,128)S(1)} %collective-permute-done.7.lags), custom_call_target="tpu_custom_call" | custom-call | flops 2097152 | bytes 5242880 | tf_op jit(solution)/shard_map/unpack/pallas_call | solution.py:333
  (17 shorter events, 0.1 us)
Async XLA Ops:
  0.6 9.4 %collective-permute-start = (f32[64,128]{1,0:T(8,128)}, f32[64,128]{1,0:T(8,128)S(1)}, u32[]{:S(2)}, u32[]{:S(2)}) collective-permute-start(f32[64,128]{1,0:T(8,128)} %param.13), channel_id=1, source_target_pairs={{0,16},{4,48},{8,64},{12,96},{16,136},{20,176},{24,216},{28,224},{... | collective-permute-start | bytes 98312 | tf_op jit(solution)/shard_map/ppermute | solution.py:370
  10.0 20.8 %copy-start = (bf16[1,128,4096]{2,1,0:T(8,128)(2,1)S(1)}, bf16[1,128,4096]{2,1,0:T(8,128)(2,1)}, u32[]{:S(2)}) copy-start(bf16[1,128,4096]{2,1,0:T(8,128)(2,1)} %param.12) | copy-start | bytes 3145732
  10.0 33.9 %all-to-all-start = ((bf16[32,2,128,128]{3,2,1,0:T(8,128)(2,1)}), bf16[32,2,128,128]{3,2,1,0:T(8,128)(2,1)S(1)}, u32[]{:S(2)}, u32[]{:S(2)}) async-start(bf16[32,2,128,128]{3,2,1,0:T(8,128)(2,1)} %pack.1), calls=%async_computation | async-start | bytes 4194304 | tf_op jit(solution)/shard_map/all_to_all | solution.py:406
  16.2 8.1 %collective-permute-start.1 = (f32[1,64,128]{2,1,0:T(8,128)S(1)}, f32[1,64,128]{2,1,0:T(8,128)S(1)}, u32[]{:S(2)}, u32[]{:S(2)}) collective-permute-start(f32[1,64,128]{2,1,0:T(8,128)S(1)} %bitcast.23), channel_id=1, source_target_pairs={{0,16},{4,20},{8,24},{12,28},{16,0},{20,4},{24,8},{28,12},{1,17},{... | collective-permute-start | bytes 98312 | tf_op jit(solution)/shard_map/ppermute | solution.py:364
  24.3 5.2 %collective-permute-start.2 = (f32[2,64,128]{2,1,0:T(8,128)S(1)}, f32[2,64,128]{2,1,0:T(8,128)S(1)}, u32[]{:S(2)}, u32[]{:S(2)}) collective-permute-start(f32[2,64,128]{2,1,0:T(8,128)S(1)} %pad_maximum_fusion), channel_id=1, source_target_pairs={{0,8},{4,12},{8,0},{12,4},{16,24},{20,28},{24,16},{28,20},{1,9},{5... | collective-permute-start | bytes 196616 | tf_op jit(solution)/shard_map/ppermute | solution.py:364
  29.5 5.0 %collective-permute-start.3 = (f32[4,64,128]{2,1,0:T(8,128)S(1)}, f32[4,64,128]{2,1,0:T(8,128)S(1)}, u32[]{:S(2)}, u32[]{:S(2)}) collective-permute-start(f32[4,64,128]{2,1,0:T(8,128)S(1)} %constant_dynamic-update-slice_fusion.near), channel_id=1, source_target_pairs={{0,4},{4,0},{8,12},{12,8},{16,20},{20,16},{24,28},{28,24},{1,5},{5... | collective-permute-start | bytes 393224 | tf_op jit(solution)/shard_map/ppermute | solution.py:364
  30.8 1.2 %copy-start.3 = (bf16[1,128,4096]{2,1,0:T(8,128)(2,1)S(1)}, bf16[1,128,4096]{2,1,0:T(8,128)(2,1)}, u32[]{:S(2)}) copy-start(bf16[1,128,4096]{2,1,0:T(8,128)(2,1)} %param.11) | copy-start | bytes 3145732
  34.4 1.0 %copy-start.4 = (f32[4,32,1024]{2,1,0:T(8,128)S(1)}, f32[4,32,1024]{2,1,0:T(8,128)}, u32[]{:S(2)}) copy-start(f32[4,32,1024]{2,1,0:T(8,128)} %constant.52.clone.seed) | copy-start | bytes 1572868
  51.6 5.0 %collective-permute-start.4 = (bf16[4,64,128]{2,1,0:T(8,128)(2,1)S(1)}, bf16[4,64,128]{2,1,0:T(8,128)(2,1)S(1)}, u32[]{:S(2)}, u32[]{:S(2)}) collective-permute-start(bf16[4,64,128]{2,1,0:T(8,128)(2,1)S(1)} %get-tuple-element.33), channel_id=1, source_target_pairs={{0,4},{4,0},{8,12},{12,8},{16,20},{20,16},{24,28},{28,24},{1,5},{5... | collective-permute-start | bytes 196616 | tf_op jit(solution)/shard_map/ppermute | solution.py:364
  55.8 27.8 %copy-start.1 = (bf16[1,128,4096]{2,1,0:T(8,128)(2,1)S(1)}, bf16[1,128,4096]{2,1,0:T(8,128)(2,1)}, u32[]{:S(2)}) copy-start(bf16[1,128,4096]{2,1,0:T(8,128)(2,1)} %param.9) | copy-start | bytes 3145732
  55.8 27.8 %copy-start.2 = (bf16[1,128,4096]{2,1,0:T(8,128)(2,1)S(1)}, bf16[1,128,4096]{2,1,0:T(8,128)(2,1)}, u32[]{:S(2)}) copy-start(bf16[1,128,4096]{2,1,0:T(8,128)(2,1)} %param.10) | copy-start | bytes 3145732
  56.7 6.0 %collective-permute-start.5 = (bf16[2,64,128]{2,1,0:T(8,128)(2,1)S(1)}, bf16[2,64,128]{2,1,0:T(8,128)(2,1)S(1)}, u32[]{:S(2)}, u32[]{:S(2)}) collective-permute-start(bf16[2,64,128]{2,1,0:T(8,128)(2,1)S(1)} %slice_select_fusion), channel_id=1, source_target_pairs={{0,8},{4,12},{8,0},{12,4},{16,24},{20,28},{24,16},{28,20},{1,9},{5... | collective-permute-start | bytes 98312 | tf_op jit(solution)/shard_map/ppermute | solution.py:364
  57.8 25.8 %all-to-all-start.1 = ((bf16[32,128,128]{2,1,0:T(8,128)(2,1)}), bf16[32,128,128]{2,1,0:T(8,128)(2,1)S(1)}, u32[]{:S(2)}, u32[]{:S(2)}) async-start(bf16[32,128,128]{2,1,0:T(8,128)(2,1)} %back.1), calls=%async_computation.1 | async-start | bytes 2097152 | tf_op jit(solution)/shard_map/all_to_all | solution.py:415
  62.8 7.7 %collective-permute-start.6 = (bf16[1,64,128]{2,1,0:T(8,128)(2,1)S(1)}, bf16[1,64,128]{2,1,0:T(8,128)(2,1)S(1)}, u32[]{:S(2)}, u32[]{:S(2)}) collective-permute-start(bf16[1,64,128]{2,1,0:T(8,128)(2,1)S(1)} %slice_select_fusion.2), channel_id=1, source_target_pairs={{0,16},{4,20},{8,24},{12,28},{16,0},{20,4},{24,8},{28,12},{1,17},{... | collective-permute-start | bytes 49160 | tf_op jit(solution)/shard_map/ppermute | solution.py:364
  70.6 13.0 %collective-permute-start.7 = (f32[64,128]{1,0:T(8,128)S(1)}, f32[64,128]{1,0:T(8,128)S(1)}, u32[]{:S(2)}, u32[]{:S(2)}) collective-permute-start(f32[64,128]{1,0:T(8,128)S(1)} %bitcast.26), channel_id=1, source_target_pairs={{16,0},{48,4},{64,8},{96,12},{136,16},{176,20},{216,24},{224,28},{... | collective-permute-start | bytes 98312 | tf_op jit(solution)/shard_map/ppermute | solution.py:398

commit v6 on v5

--- a/solution.py
+++ b/solution.py
@@ -8,7 +8,7 @@
 from jax.sharding import PartitionSpec as P
 
 CTX = ("xh", "y")
-PLANE = ("xh", "y", "xl", "core")
+PLANE = ("y", "core", "xh", "xl")
 CTX_Z = ("xh", "y", "z")
 SEQ = 1024
 BLOCK = 128
@@ -39,6 +39,10 @@
 def slot_of(z, home):
     n = z ^ home
     return (n & 1) * 4 + (n & 2) + (n >> 2)
+
+
+def chunk_at(n, r):
+    return 8 * (n % 4) + 4 * (r % 2) + 2 * (n // 4) + r // 2
 
 
 def dot(a, b):
@@ -100,17 +104,17 @@
             copy.wait()
         for t in range(j * tiles, (j + 1) * tiles):
             ahead, behind = lanes_of(t), lanes_of(GROUPS - 1 - t)
-            even, odd = 2 * t, 2 * t + 1
+            even, odd = (chunk_at(block // 4, block % 4) for block in (2 * t, 2 * t + 1))
             for kind in range(2):
                 a, b = 2 * kind, 2 * kind + 1
                 f = buf[a, :, ahead].astype(F32) * buf[b, :, ahead].astype(F32)
                 r = buf[a, :, behind].astype(F32) * buf[b, :, behind].astype(F32)
                 out[even, kind] = jnp.where(low, f, r).astype(BF16)
                 out[odd, kind] = jnp.where(low, r, f).astype(BF16)
-            pair = pl.ds(even, 2)
-            copy = pltpu.make_async_copy(out.at[pair], x_hbm.at[pair], sem_out.at[t])
-            copy.start()
-            leaving.append(copy)
+            for chunk in (even, odd):
+                copy = pltpu.make_async_copy(out.at[chunk], x_hbm.at[chunk], sem_out.at[chunk])
+                copy.start()
+                leaving.append(copy)
     for copy in leaving:
         copy.wait()
 
@@ -133,7 +137,7 @@
             pltpu.VMEM((4,) + q.shape, BF16),
             pltpu.VMEM((GROUPS, 2, BLOCK, LANES), BF16),
             pltpu.SemaphoreType.DMA((CUTS, 4, 2)),
-            pltpu.SemaphoreType.DMA((GROUPS // 2,)),
+            pltpu.SemaphoreType.DMA((GROUPS,)),
         ],
         compiler_params=LIMIT,
         cost_estimate=pl.CostEstimate(flops=2 * MIB, bytes_accessed=6 * MIB, transcendentals=0),
@@ -201,7 +205,7 @@
     filt_copy = pltpu.make_async_copy(filt_hbm, filt, sem_in.at[0])
     filt_copy.start()
     def columns(kind):
-        tiles = [[x[SPLIT * i + q, kind] for i in range(SEQ // BLOCK)] for q in range(SPLIT)]
+        tiles = [[x[chunk_at(i, q), kind] for i in range(SEQ // BLOCK)] for q in range(SPLIT)]
         return jnp.concatenate([jnp.concatenate(tile, axis=0) for tile in tiles], axis=1)
 
     def summed(value):
@@ -246,18 +250,17 @@
     step = 256
     steps = SEQ // step
     leaving = []
-    size = SPLIT * (step // BLOCK)
     for n in range(steps):
         at = pl.ds(n * step, step)
         value = dot(cos[at, :], uv[0]) + dot(sin[at, :], uv[1])
         value = (value * (1.0 / SEQ)).astype(BF16)
         for i in range(step // BLOCK):
             for q in range(SPLIT):
-                conv[n * size + SPLIT * i + q] = value[i * BLOCK:(i + 1) * BLOCK, lanes_of(q)]
-        part = pl.ds(n * size, size)
-        copy = pltpu.make_async_copy(conv.at[part], conv_hbm.at[part], sem_out.at[n])
-        copy.start()
-        leaving.append(copy)
+                chunk = chunk_at(n * (step // BLOCK) + i, q)
+                conv[chunk] = value[i * BLOCK:(i + 1) * BLOCK, lanes_of(q)]
+                copy = pltpu.make_async_copy(conv.at[chunk], conv_hbm.at[chunk], sem_out.at[chunk])
+                copy.start()
+                leaving.append(copy)
     for copy in leaving:
         copy.wait()
 
@@ -294,7 +297,7 @@
         in_specs=[VMEM] * 3,
         out_specs=HBM,
         out_shape=pltpu.HBM((GROUPS, BLOCK, LANES), BF16),
-        scratch_shapes=[pltpu.VMEM((GROUPS, BLOCK, LANES), BF16), pltpu.SemaphoreType.DMA((4,))],
+        scratch_shapes=[pltpu.VMEM((GROUPS, BLOCK, LANES), BF16), pltpu.SemaphoreType.DMA((GROUPS,))],
         compiler_params=SMALL,
         cost_estimate=pl.CostEstimate(flops=2100 * MIB, bytes_accessed=MIB, transcendentals=0),
         name="back",
@@ -310,8 +313,8 @@
     leaving = []
     for j in range(CUTS):
         for t in range(j * tiles, (j + 1) * tiles):
-            even = conv[2 * t].astype(F32)
-            odd = conv[2 * t + 1].astype(F32)
+            even = conv[chunk_at(t // 2, 2 * t % 4)].astype(F32)
+            odd = conv[chunk_at(t // 2, 2 * t % 4 + 1)].astype(F32)
             ahead, behind = jnp.where(low, even, odd), jnp.where(low, odd, even)
             for cols, grad in ((lanes_of(t), ahead), (lanes_of(GROUPS - 1 - t), behind)):
                 key[:, cols] = (grad * v_in[:, cols].astype(F32)).astype(BF16)

time: 86.1 us -> 85.5 us (level)
  waiting for transfers between devices: 33.9 us -> 32.7 us
where the time goes in v6:
time: 85.5 us; the launch traced here: 84.6 us
  waiting for transfers between devices  32.7 us (38%)
  starting transfers between devices  27.3 us (32%)
  Pallas kernels  20.4 us (24%)
  local copies, waits for them, and re-layouts  2.99 us (3%)
  between operations  0.98 us (1%)
    ppermute x6, waiting for transfers between devices, swap_z(): return lax.ppermute(block, 'z', [(i, i ^ 1 << bit) for i in range(8)])  18.6 us
    ppermute x1, waiting for transfers between devices, sent_home(): return lax.ppermute(lags, CTX_Z, route)  9.02 us
    pallas_call x1, Pallas kernels, core(): pl.pallas_call(core_kernel, in_specs=[SMEM, VMEM, HBM, VMEM], out_specs=(...  7.7 us
    ppermute x6, starting transfers between devices, swap_z(): return lax.ppermute(block, 'z', [(i, i ^ 1 << bit) for i in range(8)])  6.68 us
    all_to_all x1, starting transfers between devices, local(): x = lax.all_to_all(x, PLANE, split_axis=0, concat_axis=0, tiled=True)  6.07 us
    ppermute x1, starting transfers between devices, sent_out(): return lax.ppermute(filters, CTX_Z, route)[None]  5.73 us
    all_to_all x1, waiting for transfers between devices, local(): x = lax.all_to_all(x, PLANE, split_axis=0, concat_axis=0, tiled=True)  5.12 us
    all_to_all x1, starting transfers between devices, local(): conv = lax.all_to_all(conv, PLANE, split_axis=0, concat_axis=0, tiled=True)  4.89 us
  transfers between devices with their start and end apart: 10, of which 7 were waited for; matrix products, arithmetic and copies ran while one was open for 1% of the time, Pallas kernels for 13%

profile of v6, /device:TPU:192, one launch (start us, length us, event | category | flops | bytes accessed | tf_op | source)
XLA Modules:
  0.0 84.6 jit_solution(11371415789079467151)
XLA Ops:
  0.6 5.7 %collective-permute-start = (f32[64,128]{1,0:T(8,128)}, f32[64,128]{1,0:T(8,128)S(1)}, u32[]{:S(2)}, u32[]{:S(2)}) collective-permute-start(f32[64,128]{1,0:T(8,128)} %param.13), channel_id=1, source_target_pairs={{0,16},{4,48},{8,64},{12,96},{16,136},{20,176},{24,216},{28,224},{... | collective-permute-start | bytes 98312 | tf_op jit(solution)/shard_map/ppermute | solution.py:373
  6.4 3.7 %pack.1 = bf16[32,2,128,128]{3,2,1,0:T(8,128)(2,1)} custom-call(bf16[128,4096]{1,0:T(8,128)(2,1)} %bitcast.22, bf16[128,4096]{1,0:T(8,128)(2,1)} %bitcast.14, bf16[128,4096]{1,0:T(8,128)(2,1)} %bitcast.16, bf16[128,4096]{1,0:T(8,128)(2,1)} %bitcast.18), custom_call_target="tpu_custom_call" | custom-call | flops 2097152 | bytes 6291456 | tf_op jit(solution)/shard_map/pack/pallas_call | solution.py:131
  10.1 0.0 collective-permute-done
  10.1 0.0 copy-start
  10.1 6.1 %all-to-all-start = ((bf16[32,2,128,128]{3,2,1,0:T(8,128)(2,1)}), bf16[32,2,128,128]{3,2,1,0:T(8,128)(2,1)S(1)}, u32[]{:S(2)}, u32[]{:S(2)}) async-start(bf16[32,2,128,128]{3,2,1,0:T(8,128)(2,1)} %pack.1), calls=%async_computation | async-start | bytes 4194304 | tf_op jit(solution)/shard_map/all_to_all | solution.py:409
  16.2 1.7 %collective-permute-start.1 = (f32[1,64,128]{2,1,0:T(8,128)S(1)}, f32[1,64,128]{2,1,0:T(8,128)S(1)}, u32[]{:S(2)}, u32[]{:S(2)}) collective-permute-start(f32[1,64,128]{2,1,0:T(8,128)S(1)} %bitcast.23), channel_id=1, source_target_pairs={{0,16},{4,20},{8,24},{12,28},{16,0},{20,4},{24,8},{28,12},{1,17},{... | collective-permute-start | bytes 98312 | tf_op jit(solution)/shard_map/ppermute | solution.py:367
  17.9 6.4 %collective-permute-done.1 = f32[1,64,128]{2,1,0:T(8,128)S(1)} collective-permute-done((f32[1,64,128]{2,1,0:T(8,128)S(1)}, f32[1,64,128]{2,1,0:T(8,128)S(1)}, u32[]{:S(2)}, u32[]{:S(2)}) %collective-permute-start.1) | collective-permute-done | bytes 32800 | tf_op jit(solution)/shard_map/ppermute | solution.py:367
  24.3 1.1 %collective-permute-start.2 = (f32[2,64,128]{2,1,0:T(8,128)S(1)}, f32[2,64,128]{2,1,0:T(8,128)S(1)}, u32[]{:S(2)}, u32[]{:S(2)}) collective-permute-start(f32[2,64,128]{2,1,0:T(8,128)S(1)} %pad_maximum_fusion), channel_id=1, source_target_pairs={{0,8},{4,12},{8,0},{12,4},{16,24},{20,28},{24,16},{28,20},{1,9},{5... | collective-permute-start | bytes 196616 | tf_op jit(solution)/shard_map/ppermute | solution.py:367
  25.4 4.1 %collective-permute-done.2 = f32[2,64,128]{2,1,0:T(8,128)S(1)} collective-permute-done((f32[2,64,128]{2,1,0:T(8,128)S(1)}, f32[2,64,128]{2,1,0:T(8,128)S(1)}, u32[]{:S(2)}, u32[]{:S(2)}) %collective-permute-start.2) | collective-permute-done | bytes 65568 | tf_op jit(solution)/shard_map/ppermute | solution.py:367
  29.5 0.7 collective-permute-start.3
  30.1 0.7 dynamic-slice_bitcast_fusion
  30.8 0.0 copy-done
  30.8 0.0 copy-start.3
  30.8 1.2 %copy-done.3 = bf16[1,128,4096]{2,1,0:T(8,128)(2,1)S(1)} copy-done((bf16[1,128,4096]{2,1,0:T(8,128)(2,1)S(1)}, bf16[1,128,4096]{2,1,0:T(8,128)(2,1)}, u32[]{:S(2)}) %copy-start.3) | copy-done | bytes 1048600
  32.1 1.1 %times.1 = bf16[128,4096]{1,0:T(8,128)(2,1)} custom-call(bf16[128,4096]{1,0:T(8,128)(2,1)S(1)} %bitcast.15, bf16[128,4096]{1,0:T(8,128)(2,1)S(1)} %bitcast.20), custom_call_target="tpu_custom_call" | custom-call | flops 1 | bytes 1 | tf_op jit(solution)/shard_map/times/pallas_call | solution.py:354
  33.1 0.1 pad_add_fusion.place_ref
  33.2 1.2 %collective-permute-done.3.far = f32[4,64,128]{2,1,0:T(8,128)S(1)} collective-permute-done((f32[4,64,128]{2,1,0:T(8,128)S(1)}, f32[4,64,128]{2,1,0:T(8,128)S(1)}, u32[]{:S(2)}, u32[]{:S(2)}) %collective-permute-start.3) | collective-permute-done | bytes 131104 | tf_op jit(solution)/shard_map/ppermute | solution.py:367
  34.4 0.0 copy-start.4
  34.4 1.0 %copy-done.4 = f32[4,32,1024]{2,1,0:T(8,128)S(1)} copy-done((f32[4,32,1024]{2,1,0:T(8,128)S(1)}, f32[4,32,1024]{2,1,0:T(8,128)}, u32[]{:S(2)}) %copy-start.4) | copy-done | bytes 524312
  35.5 3.0 %filter_spectrum.1 = (f32[2,1024,128]{2,1,0:T(8,128)}, f32[4,32,1024]{2,1,0:T(8,128)S(1)}) custom-call(s32[10]{0:T(128)S(1)} %pad_add_fusion.place_ref, f32[4,32,1024]{2,1,0:T(8,128)S(1)} %copy-done.4, f32[4,64,128]{2,1,0:T(8,128)S(1)} %constant_dynamic-update-slice_fusion.near, f32[4,64,128]{2,1,0:T(8,128)S(1)} %collective-permute-done.3.far), custom_call_target="tpu_custom_call" | custom-call | flops 1 | bytes 1 | tf_op jit(solution)/shard_map/filter_spectrum/pallas_call | solution.py:176
  38.5 5.1 %all-to-all-done.x = bf16[32,2,128,128]{3,2,1,0:T(8,128)(2,1)S(1)} async-done(((bf16[32,2,128,128]{3,2,1,0:T(8,128)(2,1)}), bf16[32,2,128,128]{3,2,1,0:T(8,128)(2,1)S(1)}, u32[]{:S(2)}, u32[]{:S(2)}) %all-to-all-start) | async-done | bytes 2097184 | tf_op jit(solution)/shard_map/all_to_all | solution.py:409
  43.7 7.7 %core.1 = (f32[4,64,128]{2,1,0:T(8,128)S(1)}, bf16[4,64,128]{2,1,0:T(8,128)(2,1)S(1)}, bf16[2,1024,512]{2,1,0:T(8,128)(2,1)S(1)}, bf16[1024,1024]{1,0:T(8,128)(2,1)S(1)}, bf16[1024,1024]{1,0:T(8,128)(2,1)S(1)}) custom-call(s32[10]{0:T(128)S(1)} %pad_add_fusion.place_ref, bf16[32,2,128,128]{3,2,1,0:T(8,128)(2,1)S(1)} %all-to-all-done.x, ...), custom_call_target="tpu_custom_call" | custom-call | flops 5242880000 | bytes 4194304 | tf_op jit(solution)/shard_map/core/pallas_call | solution.py:270
  51.4 1.1 %collective-permute-start.4 = (bf16[4,64,128]{2,1,0:T(8,128)(2,1)S(1)}, bf16[4,64,128]{2,1,0:T(8,128)(2,1)S(1)}, u32[]{:S(2)}, u32[]{:S(2)}) collective-permute-start(bf16[4,64,128]{2,1,0:T(8,128)(2,1)S(1)} %get-tuple-element.33), channel_id=1, source_target_pairs={{0,4},{4,0},{8,12},{12,8},{16,20},{20,16},{24,28},{28,24},{1,5},{5... | collective-permute-start | bytes 196616 | tf_op jit(solution)/shard_map/ppermute | solution.py:367
  52.5 3.3 %back.1 = bf16[32,128,128]{2,1,0:T(8,128)(2,1)} custom-call(bf16[2,1024,512]{2,1,0:T(8,128)(2,1)S(1)} %get-tuple-element.29.uv, bf16[1024,1024]{1,0:T(8,128)(2,1)S(1)} %get-tuple-element.30.cos, bf16[1024,1024]{1,0:T(8,128)(2,1)S(1)} %get-tuple-element.31.sin), custom_call_target="tpu_custom_call" | custom-call | flops 2202009600 | bytes 1048576 | tf_op jit(solution)/shard_map/back/pallas_call | solution.py:295
  55.8 0.0 copy-start.1
  55.8 0.0 copy-start.2
  55.8 0.1 collective-permute-done.4
  56.0 1.2 %collective-permute-start.5 = (bf16[2,64,128]{2,1,0:T(8,128)(2,1)S(1)}, bf16[2,64,128]{2,1,0:T(8,128)(2,1)S(1)}, u32[]{:S(2)}, u32[]{:S(2)}) collective-permute-start(bf16[2,64,128]{2,1,0:T(8,128)(2,1)S(1)} %slice_select_fusion), channel_id=1, source_target_pairs={{0,8},{4,12},{8,0},{12,4},{16,24},{20,28},{24,16},{28,20},{1,9},{5... | collective-permute-start | bytes 98312 | tf_op jit(solution)/shard_map/ppermute | solution.py:367
  57.1 4.9 %all-to-all-start.1 = ((bf16[32,128,128]{2,1,0:T(8,128)(2,1)}), bf16[32,128,128]{2,1,0:T(8,128)(2,1)S(1)}, u32[]{:S(2)}, u32[]{:S(2)}) async-start(bf16[32,128,128]{2,1,0:T(8,128)(2,1)} %back.1), calls=%async_computation.1 | async-start | bytes 2097152 | tf_op jit(solution)/shard_map/all_to_all | solution.py:418
  62.0 0.0 collective-permute-done.5
  62.1 1.0 %collective-permute-start.6 = (bf16[1,64,128]{2,1,0:T(8,128)(2,1)S(1)}, bf16[1,64,128]{2,1,0:T(8,128)(2,1)S(1)}, u32[]{:S(2)}, u32[]{:S(2)}) collective-permute-start(bf16[1,64,128]{2,1,0:T(8,128)(2,1)S(1)} %slice_select_fusion.2), channel_id=1, source_target_pairs={{0,16},{4,20},{8,24},{12,28},{16,0},{20,4},{24,8},{28,12},{1,17},{... | collective-permute-start | bytes 49160 | tf_op jit(solution)/shard_map/ppermute | solution.py:367
  63.1 6.7 %collective-permute-done.6 = bf16[1,64,128]{2,1,0:T(8,128)(2,1)S(1)} collective-permute-done((bf16[1,64,128]{2,1,0:T(8,128)(2,1)S(1)}, bf16[1,64,128]{2,1,0:T(8,128)(2,1)S(1)}, u32[]{:S(2)}, u32[]{:S(2)}) %collective-permute-start.6) | collective-permute-done | bytes 16416 | tf_op jit(solution)/shard_map/ppermute | solution.py:367
  69.9 4.0 %collective-permute-start.7 = (f32[64,128]{1,0:T(8,128)S(1)}, f32[64,128]{1,0:T(8,128)S(1)}, u32[]{:S(2)}, u32[]{:S(2)}) collective-permute-start(f32[64,128]{1,0:T(8,128)S(1)} %bitcast.26), channel_id=1, source_target_pairs={{16,0},{48,4},{64,8},{96,12},{136,16},{176,20},{216,24},{224,28},{... | collective-permute-start | bytes 98312 | tf_op jit(solution)/shard_map/ppermute | solution.py:401
  73.9 9.0 %collective-permute-done.7.lags = f32[64,128]{1,0:T(8,128)S(1)} collective-permute-done((f32[64,128]{1,0:T(8,128)S(1)}, f32[64,128]{1,0:T(8,128)S(1)}, u32[]{:S(2)}, u32[]{:S(2)}) %collective-permute-start.7) | collective-permute-done | bytes 32800 | tf_op jit(solution)/shard_map/ppermute | solution.py:401
  82.9 0.0 all-to-all-done.1.conv
  82.9 0.0 copy-done.1
  82.9 0.0 copy-done.2
  82.9 1.6 %unpack.1 = (bf16[128,4096]{1,0:T(8,128)(2,1)}, bf16[128,4096]{1,0:T(8,128)(2,1)}, f32[64,128]{1,0:T(8,128)}) custom-call(bf16[32,128,128]{2,1,0:T(8,128)(2,1)S(1)} %all-to-all-done.1.conv, bf16[128,4096]{1,0:T(8,128)(2,1)S(1)} %bitcast.17, bf16[128,4096]{1,0:T(8,128)(2,1)S(1)} %bitcast.19, f32[64,128]{1,0:T(8,128)S(1)} %collective-permute-done.7.lags), custom_call_target="tpu_custom_call" | custom-call | flops 2097152 | bytes 5242880 | tf_op jit(solution)/shard_map/unpack/pallas_call | solution.py:336
  (17 shorter events, 0.1 us)
Async XLA Ops:
  0.6 9.5 %collective-permute-start = (f32[64,128]{1,0:T(8,128)}, f32[64,128]{1,0:T(8,128)S(1)}, u32[]{:S(2)}, u32[]{:S(2)}) collective-permute-start(f32[64,128]{1,0:T(8,128)} %param.13), channel_id=1, source_target_pairs={{0,16},{4,48},{8,64},{12,96},{16,136},{20,176},{24,216},{28,224},{... | collective-permute-start | bytes 98312 | tf_op jit(solution)/shard_map/ppermute | solution.py:373
  10.1 20.7 %copy-start = (bf16[1,128,4096]{2,1,0:T(8,128)(2,1)S(1)}, bf16[1,128,4096]{2,1,0:T(8,128)(2,1)}, u32[]{:S(2)}) copy-start(bf16[1,128,4096]{2,1,0:T(8,128)(2,1)} %param.12) | copy-start | bytes 3145732
  10.1 33.5 %all-to-all-start = ((bf16[32,2,128,128]{3,2,1,0:T(8,128)(2,1)}), bf16[32,2,128,128]{3,2,1,0:T(8,128)(2,1)S(1)}, u32[]{:S(2)}, u32[]{:S(2)}) async-start(bf16[32,2,128,128]{3,2,1,0:T(8,128)(2,1)} %pack.1), calls=%async_computation | async-start | bytes 4194304 | tf_op jit(solution)/shard_map/all_to_all | solution.py:409
  16.2 8.1 %collective-permute-start.1 = (f32[1,64,128]{2,1,0:T(8,128)S(1)}, f32[1,64,128]{2,1,0:T(8,128)S(1)}, u32[]{:S(2)}, u32[]{:S(2)}) collective-permute-start(f32[1,64,128]{2,1,0:T(8,128)S(1)} %bitcast.23), channel_id=1, source_target_pairs={{0,16},{4,20},{8,24},{12,28},{16,0},{20,4},{24,8},{28,12},{1,17},{... | collective-permute-start | bytes 98312 | tf_op jit(solution)/shard_map/ppermute | solution.py:367
  24.3 5.2 %collective-permute-start.2 = (f32[2,64,128]{2,1,0:T(8,128)S(1)}, f32[2,64,128]{2,1,0:T(8,128)S(1)}, u32[]{:S(2)}, u32[]{:S(2)}) collective-permute-start(f32[2,64,128]{2,1,0:T(8,128)S(1)} %pad_maximum_fusion), channel_id=1, source_target_pairs={{0,8},{4,12},{8,0},{12,4},{16,24},{20,28},{24,16},{28,20},{1,9},{5... | collective-permute-start | bytes 196616 | tf_op jit(solution)/shard_map/ppermute | solution.py:367
  29.5 5.0 %collective-permute-start.3 = (f32[4,64,128]{2,1,0:T(8,128)S(1)}, f32[4,64,128]{2,1,0:T(8,128)S(1)}, u32[]{:S(2)}, u32[]{:S(2)}) collective-permute-start(f32[4,64,128]{2,1,0:T(8,128)S(1)} %constant_dynamic-update-slice_fusion.near), channel_id=1, source_target_pairs={{0,4},{4,0},{8,12},{12,8},{16,20},{20,16},{24,28},{28,24},{1,5},{5... | collective-permute-start | bytes 393224 | tf_op jit(solution)/shard_map/ppermute | solution.py:367
  30.8 1.2 %copy-start.3 = (bf16[1,128,4096]{2,1,0:T(8,128)(2,1)S(1)}, bf16[1,128,4096]{2,1,0:T(8,128)(2,1)}, u32[]{:S(2)}) copy-start(bf16[1,128,4096]{2,1,0:T(8,128)(2,1)} %param.11) | copy-start | bytes 3145732
  34.4 1.0 %copy-start.4 = (f32[4,32,1024]{2,1,0:T(8,128)S(1)}, f32[4,32,1024]{2,1,0:T(8,128)}, u32[]{:S(2)}) copy-start(f32[4,32,1024]{2,1,0:T(8,128)} %constant.52.clone.seed) | copy-start | bytes 1572868
  51.4 4.5 %collective-permute-start.4 = (bf16[4,64,128]{2,1,0:T(8,128)(2,1)S(1)}, bf16[4,64,128]{2,1,0:T(8,128)(2,1)S(1)}, u32[]{:S(2)}, u32[]{:S(2)}) collective-permute-start(bf16[4,64,128]{2,1,0:T(8,128)(2,1)S(1)} %get-tuple-element.33), channel_id=1, source_target_pairs={{0,4},{4,0},{8,12},{12,8},{16,20},{20,16},{24,28},{28,24},{1,5},{5... | collective-permute-start | bytes 196616 | tf_op jit(solution)/shard_map/ppermute | solution.py:367
  55.8 27.1 %copy-start.1 = (bf16[1,128,4096]{2,1,0:T(8,128)(2,1)S(1)}, bf16[1,128,4096]{2,1,0:T(8,128)(2,1)}, u32[]{:S(2)}) copy-start(bf16[1,128,4096]{2,1,0:T(8,128)(2,1)} %param.9) | copy-start | bytes 3145732
  55.8 27.1 %copy-start.2 = (bf16[1,128,4096]{2,1,0:T(8,128)(2,1)S(1)}, bf16[1,128,4096]{2,1,0:T(8,128)(2,1)}, u32[]{:S(2)}) copy-start(bf16[1,128,4096]{2,1,0:T(8,128)(2,1)} %param.10) | copy-start | bytes 3145732
  56.0 6.1 %collective-permute-start.5 = (bf16[2,64,128]{2,1,0:T(8,128)(2,1)S(1)}, bf16[2,64,128]{2,1,0:T(8,128)(2,1)S(1)}, u32[]{:S(2)}, u32[]{:S(2)}) collective-permute-start(bf16[2,64,128]{2,1,0:T(8,128)(2,1)S(1)} %slice_select_fusion), channel_id=1, source_target_pairs={{0,8},{4,12},{8,0},{12,4},{16,24},{20,28},{24,16},{28,20},{1,9},{5... | collective-permute-start | bytes 98312 | tf_op jit(solution)/shard_map/ppermute | solution.py:367
  57.1 25.7 %all-to-all-start.1 = ((bf16[32,128,128]{2,1,0:T(8,128)(2,1)}), bf16[32,128,128]{2,1,0:T(8,128)(2,1)S(1)}, u32[]{:S(2)}, u32[]{:S(2)}) async-start(bf16[32,128,128]{2,1,0:T(8,128)(2,1)} %back.1), calls=%async_computation.1 | async-start | bytes 2097152 | tf_op jit(solution)/shard_map/all_to_all | solution.py:418
  62.1 7.7 %collective-permute-start.6 = (bf16[1,64,128]{2,1,0:T(8,128)(2,1)S(1)}, bf16[1,64,128]{2,1,0:T(8,128)(2,1)S(1)}, u32[]{:S(2)}, u32[]{:S(2)}) collective-permute-start(bf16[1,64,128]{2,1,0:T(8,128)(2,1)S(1)} %slice_select_fusion.2), channel_id=1, source_target_pairs={{0,16},{4,20},{8,24},{12,28},{16,0},{20,4},{24,8},{28,12},{1,17},{... | collective-permute-start | bytes 49160 | tf_op jit(solution)/shard_map/ppermute | solution.py:367
  69.9 13.0 %collective-permute-start.7 = (f32[64,128]{1,0:T(8,128)S(1)}, f32[64,128]{1,0:T(8,128)S(1)}, u32[]{:S(2)}, u32[]{:S(2)}) collective-permute-start(f32[64,128]{1,0:T(8,128)S(1)} %bitcast.26), channel_id=1, source_target_pairs={{16,0},{48,4},{64,8},{96,12},{136,16},{176,20},{216,24},{224,28},{... | collective-permute-start | bytes 98312 | tf_op jit(solution)/shard_map/ppermute | solution.py:401
